TPU v7x, 128 devices: a whole 4x4x4 slice. The times are simulated.
128 devices in a mesh: ha: 16 (over z, y_lo, core), wa: 8 (over x, y_hi).
Axes of the slice: x: 4, y: 4 (y_hi: 2, y_lo: 2; y = y_hi * 2 + y_lo), z: 4, core: 2. Of those that a mesh axis runs over, the one named last changes fastest.
Arguments:
- frames: bfloat16 [64, 256, 2048], P(None, 'ha', 'wa'), may hold values from -6 to 6
- w_in: bfloat16 [128, 64], replicated, may hold values from -0.75 to 0.75
- grid_mix: bfloat16 [256, 256], replicated, may hold values from -0.375 to 0.375
- block_mix: bfloat16 [256, 256], replicated, may hold values from -0.375 to 0.375
- w_out: bfloat16 [64, 64], replicated, may hold values from -0.75 to 0.75
- conv_w: bfloat16 [3, 3, 64, 64], replicated, may hold values from -0.25 to 0.25
- cotangent: bfloat16 [64, 256, 2048], P(None, 'ha', 'wa'), may hold values from -6 to 6
Outputs:
- restored: bfloat16 [64, 256, 2048], P(None, 'ha', 'wa')
- grad_frames: bfloat16 [64, 256, 2048], P(None, 'ha', 'wa')
- grad_w_in: float32 [128, 64], replicated
- grad_grid: float32 [256, 256], replicated
- grad_block: float32 [256, 256], replicated
- grad_w_out: float32 [64, 64], replicated
- grad_conv: float32 [3, 3, 64, 64], replicated
All inputs are finite; a program needn't handle non-finite values.
Results may differ from a plain program's by a relative error of at most 0.0079.
Values may be sent and summed in bfloat16 or wider, within the bound.
A program may use at most 64 MiB of HBM per device.

v0:
```python
import jax
import jax.numpy as jnp
from jax import lax
from jax.experimental import pallas as pl
from jax.experimental.pallas import tpu as pltpu
from jax.sharding import PartitionSpec as P

BF = jnp.bfloat16
F32 = jnp.float32
EPS = 1e-06
MESH = pl.DeviceIdType.MESH

CH = 64
HC = 32
ROWS = 16
COLS = 256
LANES = 128
NA = 16
NW = 8

(G_ROW0, G_PACK0, G_ROW1, G_PACK1, G_VA, G_GA, G_B, G_B2, G_A2, G_E1, G_E2, G_E3, G_E4, G_T1, G_T2, G_T3) = range(16)
GROUPS = 16


def dot(a, b):
    return lax.dot_general(a, b, (((1,), (0,)), ((), ())), preferred_element_type=F32)


def dot_nt(a, b):
    return lax.dot_general(a, b, (((1,), (1,)), ((), ())), preferred_element_type=F32)


def dot_tn(a, b):
    return lax.dot_general(a, b, (((0,), (0,)), ((), ())), preferred_element_type=F32)


def swap_granules(load, store, depth):
    lane = lax.broadcasted_iota(jnp.int32, (depth, LANES), 1)
    for row_half in range(2):
        for col_half in range(2):
            held = [load(row_half * 8 + k, col_half) for k in range(8)]
            for s in range(3):
                width = 16 << s
                low = (lane & width) == 0
                for k in range(8):
                    if not k & (1 << s):
                        a, b = held[k], held[k | (1 << s)]
                        held[k] = jnp.where(low, a, pltpu.roll(b, width, 1))
                        held[k | (1 << s)] = jnp.where(low, pltpu.roll(a, LANES - width, 1), b)
            for k in range(8):
                store(col_half * 8 + k, row_half, held[k])


def half(t):
    return slice(t * LANES, (t + 1) * LANES)


def kernel(
    frames, w_in, grid_mix, block_mix, w_out, conv_w, cot,
    rest_out, gframe_out, early_out, tail_out,
    turn, xb, nb, unit, inv, dgelu, gates, bval, u3, v3, gj, gg, bback, xt, bt, bm, gbv,
    sa, ra, x32, sb, rb, sb2, rb2, sa2, ra2, gated, gbef, jp,
    row_in, pack_out, pack_in, edge_l, edge_r,
    se, re1, e1, re2, e2, re3, e4, re4, st, rt1, t1, rt2, t2, rt3,
    ssem, rsem,
):
    ia = lax.axis_index("ha")
    iw = lax.axis_index("wa")
    up, down = lax.rem(ia + NA - 1, NA), lax.rem(ia + 1, NA)
    left, right = lax.rem(iw + NW - 1, NW), lax.rem(iw + 1, NW)
    lane = lax.broadcasted_iota(jnp.int32, (CH, LANES), 1)

    def push(src, dst, g, where):
        pltpu.make_async_remote_copy(
            src_ref=src, dst_ref=dst, send_sem=ssem.at[g], recv_sem=rsem.at[g], device_id=where, device_id_type=MESH
        ).start()

    def over_w(src_of, dst, g):
        for k in range(1, NW):
            peer = lax.rem(iw + k, NW)
            push(src_of(peer), dst, g, (ia, peer))

    def over_a(src_of, dst, g):
        for k in range(1, NA):
            peer = lax.rem(ia + k, NA)
            push(src_of(peer), dst, g, (peer, iw))

    def arrived(ref, g):
        pltpu.make_async_copy(ref, ref, rsem.at[g]).wait()

    def gone(ref, g):
        pltpu.make_async_copy(ref, ref, ssem.at[g]).wait()

    barrier = pltpu.get_barrier_semaphore()
    peers = [(ia, lax.rem(iw + k, NW)) for k in range(1, NW)]
    peers += [(lax.rem(ia + k, NA), iw) for k in range(1, NA)]
    peers += [(a, b) for a in (up, down) for b in (left, right)]
    for peer in peers:
        pl.semaphore_signal(barrier, inc=1, device_id=peer, device_id_type=MESH)

    def turn_in(src):
        for t in range(2):
            turn[t] = src[:, :, half(t)].astype(F32).reshape(CH * ROWS, LANES)

    def turned(r, t):
        return turn[t, pl.ds(r, CH, stride=ROWS), :]

    def edges(pack, t0, t1, r):
        pack = jnp.where(lane == r, pltpu.roll(t0, r, 1), pack)
        return jnp.where(lane == ROWS + r, pltpu.roll(t1, r + 17, 1), pack)

    def send_halo(field, pack, which, g_row, g_pack):
        pack_out[which] = pack.astype(BF)
        push(field.at[1, CH : 2 * CH], row_in.at[which, 1], g_row, (up, iw))
        push(field.at[ROWS, CH : 2 * CH], row_in.at[which, 0], g_row, (down, iw))
        for slot, where in enumerate(
            [(ia, right), (ia, left), (down, right), (down, left), (up, right), (up, left)]
        ):
            push(pack_out.at[which], pack_in.at[which, slot], g_pack, where)

    def take_halo(field, which, g_row, g_pack):
        arrived(row_in.at[which], g_row)
        arrived(pack_in.at[which], g_pack)
        top = row_in[which, 0].astype(F32) * jnp.where(ia > 0, 1.0, 0.0)
        field[0, CH : 2 * CH] = top.astype(BF)
        bottom = row_in[which, 1].astype(F32) * jnp.where(ia < NA - 1, 1.0, 0.0)
        field[ROWS + 1, CH : 2 * CH] = bottom.astype(BF)
        first = jnp.where(ia > 0, 0, 1)
        last = jnp.where(ia < NA - 1, ROWS + 2, ROWS + 1)
        got = [pack_in[which, k].astype(F32) for k in range(6)]

        def assemble(middle, above, below, has):
            joined = jnp.where(lane == 0, above, jnp.where(lane == ROWS + 1, below, middle))
            return jnp.where((lane >= first) & (lane < jnp.where(has, last, 0)), joined, 0.0)

        edge_l[...] = assemble(
            pltpu.roll(got[0], 113, 1), pltpu.roll(got[2], 97, 1), pltpu.roll(got[4], 1, 1), iw > 0
        )
        edge_r[...] = assemble(
            pltpu.roll(got[1], 1, 1), pltpu.roll(got[3], 113, 1), pltpu.roll(got[5], 17, 1), iw < NW - 1
        )

        def shifts(p, carry):
            t0 = field[p, CH : 2 * CH, half(0)].astype(F32)
            t1 = field[p, CH : 2 * CH, half(1)].astype(F32)
            a0, a1 = pltpu.roll(t0, 1, 1), pltpu.roll(t1, 1, 1)
            b0, b1 = pltpu.roll(t0, LANES - 1, 1), pltpu.roll(t1, LANES - 1, 1)
            lh = pltpu.roll(edge_l[...], lax.rem(LANES - p, LANES), 1)
            rh = pltpu.roll(edge_r[...], LANES - 1 - p, 1)
            field[p, 0:CH, half(0)] = jnp.where(lane == 0, lh, a0).astype(BF)
            field[p, 0:CH, half(1)] = jnp.where(lane == 0, a0, a1).astype(BF)
            field[p, 2 * CH :, half(0)] = jnp.where(lane == LANES - 1, b1, b0).astype(BF)
            field[p, 2 * CH :, half(1)] = jnp.where(lane == LANES - 1, rh, b1).astype(BF)
            return carry

        lax.fori_loop(0, ROWS + 2, shifts, 0)

    turn_in(cot)

    def cot_row(r, pack):
        t0, t1 = turned(r, 0), turned(r, 1)
        u3[r + 1, CH : 2 * CH, half(0)] = t0.astype(BF)
        u3[r + 1, CH : 2 * CH, half(1)] = t1.astype(BF)
        return edges(pack, t0, t1, r)

    pack = lax.fori_loop(0, ROWS, cot_row, jnp.zeros((CH, LANES), F32))
    pl.semaphore_wait(barrier, len(peers))
    send_halo(u3, pack, 0, G_ROW0, G_PACK0)

    turn_in(frames)

    def first_row(r, carry):
        for t in range(2):
            x = turned(r, t)
            xb[r, :, half(t)] = x.astype(BF)
            off = x - jnp.mean(x, axis=0, keepdims=True)
            rstd = lax.rsqrt(jnp.mean(off * off, axis=0, keepdims=True) + EPS)
            u = off * rstd
            unit[r, :, half(t)] = u
            inv[r, :, half(t)] = jnp.broadcast_to(rstd, (8, LANES))
            nb[r, :, half(t)] = u.astype(BF)
        before = dot(w_in[...], nb[r])
        root = 0.7978845608028654
        square = before * before
        t = jnp.tanh(root * (before + 0.044715 * (before * square)))
        cdf = 0.5 * (1.0 + t)
        hidden = before * cdf
        dgelu[r] = cdf + before * ((0.5 * root) * (1.0 - t * t) * (1.0 + (3 * 0.044715) * square))
        hb = hidden.astype(BF)
        gates[r, 0:HC] = hb[0:HC]
        gates[r, HC:CH] = hb[CH : CH + HC]
        bval[r] = hb[CH + HC :]
        sa[0, r // 2, 0, lax.rem(r, 2)] = hb[HC:CH, half(0)]
        sa[0, r // 2, 1, lax.rem(r, 2)] = hb[HC:CH, half(1)]
        return carry

    lax.fori_loop(0, ROWS, first_row, 0)
    over_w(lambda peer: sa.at[0, peer], ra.at[0, iw], G_VA)
    ra[0, iw] = sa[0, iw]

    take_halo(u3, 0, G_ROW0, G_PACK0)
    back_w = jnp.concatenate(
        [conv_w[2 - a, 2 - b] for a in range(3) for b in range(3)], axis=0
    ).astype(F32).T.astype(BF)
    w_out_t = w_out[...].astype(F32).T.astype(BF)

    def back_row(r, carry):
        total = dot(back_w, u3[pl.ds(r, 3)].reshape(9 * CH, COLS))
        g = (total + u3[r + 1, CH : 2 * CH].astype(F32)).astype(BF)
        gj[r] = g
        up_gated = dot(w_out_t, g)
        gg[r] = up_gated
        mixed = (up_gated * gates[r].astype(F32)).astype(BF)
        sa[1, r // 2, 0, lax.rem(r, 2)] = mixed[0:HC, half(0)]
        sa[1, r // 2, 1, lax.rem(r, 2)] = mixed[0:HC, half(1)]
        bback[r] = mixed[HC:]
        return carry

    lax.fori_loop(0, ROWS, back_row, 0)
    over_w(lambda peer: sa.at[1, peer], ra.at[1, iw], G_GA)
    ra[1, iw] = sa[1, iw]

    def put(ref):
        def store(k, t, value):
            ref[k, :, half(t)] = value.astype(ref.dtype)

        return store

    swap_granules(lambda k, t: bval[k, :, half(t)].astype(F32), put(xt), HC)
    swap_granules(lambda k, t: bback[k, :, half(t)].astype(F32), put(bt), HC)
    values = xt[...].reshape(ROWS * HC, COLS)
    backs = bt[...].reshape(ROWS * HC, COLS)
    mixed = dot_nt(values, block_mix[...])
    swap_granules(lambda k, t: mixed[k * HC : (k + 1) * HC, half(t)], put(bm), HC)
    unmixed = dot(backs, block_mix[...])
    swap_granules(lambda k, t: unmixed[k * HC : (k + 1) * HC, half(t)], put(gbv), HC)
    part_block = dot_tn(backs, values).astype(BF)
    se[2 * COLS : 3 * COLS] = part_block[:, half(0)]
    se[3 * COLS :] = part_block[:, half(1)]

    arrived(ra.at[0, pl.ds(0, NW - 1)], G_VA)
    arrived(ra.at[1, pl.ds(0, NW - 1)], G_GA)

    def widen(j, carry):
        for a in range(2):
            for t in range(2):
                for r in range(2):
                    x32[pl.ds(((a * 2 + r) * 16 + j * 2 + t) * HC, HC), :] = ra[a, j, t, r].astype(F32)
        return carry

    lax.fori_loop(0, NW, widen, 0)

    def pick(q, carry):
        for a in range(2):
            for r in range(2):
                for c in range(4):
                    start = (a * 2 + r) * 16 * HC + q * 4 + c
                    sb[r * 8 + q, a, :, half(c)] = x32[pl.ds(start, 16, stride=HC), :].astype(BF)
        return carry

    lax.fori_loop(0, 8, pick, 0)
    over_a(lambda peer: sb.at[peer], rb.at[ia], G_B)
    rb[ia] = sb[ia]
    arrived(rb.at[pl.ds(0, NA - 1)], G_B)

    table = rb[:, 0].reshape(256, 512)
    back = rb[:, 1].reshape(256, 512)
    mix = grid_mix[...]
    sb2[:, 0] = dot(mix, table).astype(BF).reshape(NA, 16, 512)
    sb2[:, 1] = dot_tn(mix, back).astype(BF).reshape(NA, 16, 512)
    over_a(lambda peer: sb2.at[peer], rb2.at[ia], G_B2)
    rb2[ia] = sb2[ia]
    part_grid = dot_nt(back, table).astype(BF)
    se[0:COLS] = part_grid[:, half(0)]
    se[COLS : 2 * COLS] = part_grid[:, half(1)]
    over_w(lambda peer: se.at[pl.ds(pl.multiple_of(peer * 128, 128), 128)], re1.at[iw], G_E1)
    re1[iw] = se[pl.ds(pl.multiple_of(iw * 128, 128), 128)]

    arrived(rb2.at[pl.ds(0, NA - 1)], G_B2)

    def unpick(q, carry):
        for a in range(2):
            for r in range(2):
                for c in range(4):
                    start = ((a * 2 + r) * HC + q * 4 + c) * 16
                    x32[pl.ds(start, 16), :] = rb2[r * 8 + q, a, :, half(c)].astype(F32)
        return carry

    lax.fori_loop(0, 8, unpick, 0)

    def narrow(j, carry):
        for a in range(2):
            for t in range(2):
                for r in range(2):
                    start = (a * 2 + r) * HC * 16 + j * 2 + t
                    sa2[j, a, t, r] = x32[pl.ds(start, HC, stride=16), :].astype(BF)
        return carry

    lax.fori_loop(0, NW, narrow, 0)
    over_w(lambda peer: sa2.at[peer], ra2.at[iw], G_A2)
    ra2[iw] = sa2[iw]

    arrived(re1.at[pl.ds(0, NW - 1)], G_E1)
    total = re1[0].astype(F32)
    for k in range(1, NW):
        total = total + re1[k].astype(F32)
    e1[...] = total
    over_a(lambda peer: e1.at[pl.ds(pl.multiple_of(peer * 8, 8), 8)], re2.at[ia], G_E2)
    re2[ia] = e1[pl.ds(pl.multiple_of(ia * 8, 8), 8)]

    arrived(ra2.at[pl.ds(0, NW - 1)], G_A2)

    jp[0] = jnp.zeros((CH, COLS), BF)
    jp[1] = jnp.zeros((CH, COLS), BF)
    jp[ROWS + 2] = jnp.zeros((CH, COLS), BF)
    jp[ROWS + 3] = jnp.zeros((CH, COLS), BF)

    def returned(a, r):
        return [ra2[r // 2, a, t, lax.rem(r, 2)].astype(F32) for t in range(2)]

    def joined_row(r, pack):
        grid_mixed = returned(0, r)
        for t in range(2):
            gates_t = gates[r, :, half(t)].astype(F32)
            gated[r, 0:HC, half(t)] = (gates_t[0:HC] * (grid_mixed[t] + 1.0)).astype(BF)
            gated[r, HC:, half(t)] = (gates_t[HC:] * (bm[r, :, half(t)] + 1.0)).astype(BF)
        j = (xb[r].astype(F32) + dot(w_out[...], gated[r])).astype(BF)
        jp[r + 2] = j
        v3[r + 1, CH : 2 * CH] = j
        jf = j.astype(F32)
        return edges(pack, jf[:, half(0)], jf[:, half(1)], r)

    pack = lax.fori_loop(0, ROWS, joined_row, jnp.zeros((CH, LANES), F32))
    send_halo(v3, pack, 1, G_ROW1, G_PACK1)

    def before_row(r, carry):
        p_in, p_out = carry
        grid_mixed = returned(0, r)
        grid_back = returned(1, r)
        for t in range(2):
            g = gg[r, :, half(t)]
            d = dgelu[r, :, half(t)]
            gbef[r, 0:HC, half(t)] = (d[0:HC] * (g[0:HC] * (grid_mixed[t] + 1.0))).astype(BF)
            gbef[r, HC:CH, half(t)] = (d[HC:CH] * grid_back[t]).astype(BF)
            gbef[r, CH : CH + HC, half(t)] = (d[CH : CH + HC] * (g[HC:] * (bm[r, :, half(t)] + 1.0))).astype(BF)
            gbef[r, CH + HC :, half(t)] = (d[CH + HC :] * gbv[r, :, half(t)]).astype(BF)
        return p_in + dot_nt(gbef[r], nb[r]), p_out + dot_nt(gj[r], gated[r])

    p_in, p_out = lax.fori_loop(
        0, ROWS, before_row, (jnp.zeros((2 * CH, CH), F32), jnp.zeros((CH, CH), F32))
    )

    def conv_row(p, total):
        return total + dot_nt(u3[p], jp[pl.ds(p, 3)].reshape(3 * CH, COLS))

    p_conv = lax.fori_loop(0, ROWS + 2, conv_row, jnp.zeros((3 * CH, 3 * CH), F32))
    st[0 : 3 * CH] = p_conv[:, half(0)].astype(BF)
    st[3 * CH :] = jnp.concatenate(
        [p_conv[:, 2 * CH :], jnp.concatenate([p_in, p_out], axis=0)], axis=1
    ).astype(BF)
    over_w(lambda peer: st.at[pl.ds(pl.multiple_of(peer * 48, 16), 48)], rt1.at[iw], G_T1)
    rt1[iw] = st[pl.ds(pl.multiple_of(iw * 48, 16), 48)]

    arrived(re2.at[pl.ds(0, NA - 1)], G_E2)
    total = re2[0]
    for k in range(1, NA):
        total = total + re2[k]
    e2[...] = total
    over_a(lambda peer: e2, re3.at[ia], G_E3)
    re3[ia] = e2[...]

    w_in_t = w_in[...].astype(F32).T.astype(BF)

    def frame_row(r, carry):
        normed = dot(w_in_t, gbef[r])
        u = unit[r]
        mean_grad = jnp.mean(normed, axis=0, keepdims=True)
        mean_proj = jnp.mean(normed * u, axis=0, keepdims=True)
        source = inv[r, 0:1] * (normed - mean_grad - u * mean_proj)
        gframe_out[r] = (gj[r].astype(F32) + source).astype(BF)
        return carry

    lax.fori_loop(0, ROWS, frame_row, 0)

    arrived(rt1.at[pl.ds(0, NW - 1)], G_T1)
    total = rt1[0].astype(F32)
    for k in range(1, NW):
        total = total + rt1[k].astype(F32)
    t1[...] = total.astype(BF)
    over_a(lambda peer: t1, rt2.at[ia], G_T2)
    rt2[ia] = t1[...]

    arrived(re3.at[pl.ds(0, NA - 1)], G_E3)
    e4[...] = re3[...].reshape(128, LANES).astype(BF)
    over_w(lambda peer: e4, re4.at[iw], G_E4)
    re4[iw] = e4[...]

    take_halo(v3, 1, G_ROW1, G_PACK1)
    arrived(rt2.at[pl.ds(0, NA - 1)], G_T2)
    total = rt2[0].astype(F32)
    for k in range(1, NA):
        total = total + rt2[k].astype(F32)
    t2[...] = total.astype(BF)
    over_w(lambda peer: t2, rt3.at[iw], G_T3)
    rt3[iw] = t2[...]

    conv_k = jnp.concatenate(
        [conv_w[a, b].astype(F32).T for a in range(3) for b in range(3)], axis=0
    ).T.astype(BF)

    def out_row(r, carry):
        total = dot(conv_k, v3[pl.ds(r, 3)].reshape(9 * CH, COLS))
        rest_out[r] = (total + v3[r + 1, CH : 2 * CH].astype(F32)).astype(BF)
        return carry

    lax.fori_loop(0, ROWS, out_row, 0)

    arrived(re4.at[pl.ds(0, NW - 1)], G_E4)
    early_out[...] = re4[...]
    arrived(rt3.at[pl.ds(0, NW - 1)], G_T3)
    tail_out[...] = rt3[...]

    gone(row_in.at[0], G_ROW0)
    gone(pack_in.at[0], G_PACK0)
    gone(row_in.at[1], G_ROW1)
    gone(pack_in.at[1], G_PACK1)
    gone(sa.at[0, pl.ds(0, NW - 1)], G_VA)
    gone(sa.at[1, pl.ds(0, NW - 1)], G_GA)
    gone(sb.at[pl.ds(0, NA - 1)], G_B)
    gone(sb2.at[pl.ds(0, NA - 1)], G_B2)
    gone(sa2.at[pl.ds(0, NW - 1)], G_A2)
    gone(re1.at[pl.ds(0, NW - 1)], G_E1)
    gone(re2.at[pl.ds(0, NA - 1)], G_E2)
    gone(re3.at[pl.ds(0, NA - 1)], G_E3)
    gone(re4.at[pl.ds(0, NW - 1)], G_E4)
    gone(rt1.at[pl.ds(0, NW - 1)], G_T1)
    gone(rt2.at[pl.ds(0, NA - 1)], G_T2)
    gone(rt3.at[pl.ds(0, NW - 1)], G_T3)


def vm(*shape, dtype=BF):
    return pltpu.VMEM(shape, dtype)


SCRATCH = [
    vm(2, CH * ROWS, LANES, dtype=F32),
    vm(ROWS, CH, COLS),
    vm(ROWS, CH, COLS),
    vm(ROWS, CH, COLS, dtype=F32),
    vm(ROWS, 8, COLS, dtype=F32),
    vm(ROWS, 2 * CH, COLS, dtype=F32),
    vm(ROWS, CH, COLS),
    vm(ROWS, HC, COLS),
    vm(ROWS + 2, 3 * CH, COLS),
    vm(ROWS + 2, 3 * CH, COLS),
    vm(ROWS, CH, COLS),
    vm(ROWS, CH, COLS, dtype=F32),
    vm(ROWS, HC, COLS),
    vm(ROWS, HC, COLS),
    vm(ROWS, HC, COLS),
    vm(ROWS, HC, COLS, dtype=F32),
    vm(ROWS, HC, COLS, dtype=F32),
    vm(2, NW, 2, 2, HC, LANES),
    vm(2, NW, 2, 2, HC, LANES),
    vm(2 * 2 * 16 * HC, LANES, dtype=F32),
    vm(NA, 2, 16, 512),
    vm(NA, 2, 16, 512),
    vm(NA, 2, 16, 512),
    vm(NA, 2, 16, 512),
    vm(NW, 2, 2, 2, HC, LANES),
    vm(NW, 2, 2, 2, HC, LANES),
    vm(ROWS, CH, COLS),
    vm(ROWS, 2 * CH, COLS),
    vm(ROWS + 4, CH, COLS),
    vm(2, 2, CH, COLS),
    vm(2, CH, LANES),
    vm(2, 6, CH, LANES),
    vm(CH, LANES, dtype=F32),
    vm(CH, LANES, dtype=F32),
    vm(4 * COLS, LANES),
    vm(NW, 128, LANES),
    vm(128, LANES, dtype=F32),
    vm(NA, 8, LANES, dtype=F32),
    vm(8, LANES, dtype=F32),
    vm(NA, 8, LANES, dtype=F32),
    vm(128, LANES),
    vm(NW, 128, LANES),
    vm(6 * CH, LANES),
    vm(NW, 48, LANES),
    vm(48, LANES),
    vm(NA, 48, LANES),
    vm(48, LANES),
    vm(NW, 48, LANES),
    pltpu.SemaphoreType.DMA((GROUPS,)),
    pltpu.SemaphoreType.DMA((GROUPS,)),
]


def body(frames, w_in, grid_mix, block_mix, w_out, conv_w, cotangent):
    scale = float(ROWS * NA * COLS * NW) ** (-0.5)
    vmem = pl.BlockSpec(memory_space=pltpu.VMEM)
    rest, gframe, early, tail = pl.pallas_call(
        kernel,
        out_shape=(
            jax.ShapeDtypeStruct((ROWS, CH, COLS), BF),
            jax.ShapeDtypeStruct((ROWS, CH, COLS), BF),
            jax.ShapeDtypeStruct((NW, 128, LANES), BF),
            jax.ShapeDtypeStruct((NW, 48, LANES), BF),
        ),
        in_specs=[vmem] * 7,
        out_specs=(vmem,) * 4,
        scratch_shapes=SCRATCH,
        compiler_params=pltpu.CompilerParams(
            collective_id=0, has_side_effects=True, vmem_limit_bytes=56 * 1024 * 1024
        ),
    )(frames, w_in, grid_mix, block_mix, w_out, conv_w, cotangent)
    early = early.reshape(4, COLS, LANES).astype(F32) * scale
    tail = tail.reshape(2, 3 * CH, LANES).astype(F32) * scale
    grad_grid = jnp.concatenate([early[0], early[1]], axis=1)
    grad_block = jnp.concatenate([early[2], early[3]], axis=1)
    table = jnp.concatenate([tail[0], tail[1, :, :CH]], axis=1)
    grad_conv = table.reshape(3, CH, 3, CH)[::-1].transpose(2, 0, 1, 3)
    grad_w_in = tail[1, : 2 * CH, CH:]
    grad_w_out = tail[1, 2 * CH :, CH:]
    return (
        rest.transpose(1, 0, 2),
        gframe.transpose(1, 0, 2),
        grad_w_in,
        grad_grid,
        grad_block,
        grad_w_out,
        grad_conv,
    )


def solution(mesh):
    placed = (P(None, "ha", "wa"), P(), P(), P(), P(), P(), P(None, "ha", "wa"))
    return jax.shard_map(
        body,
        mesh=mesh,
        in_specs=placed,
        out_specs=(P(None, "ha", "wa"), P(None, "ha", "wa"), P(), P(), P(), P(), P()),
        check_vma=False,
    )
```

profile of v0, /device:TPU:1, one launch (start us, length us, event | category | flops | bytes accessed | tf_op | source)
XLA Modules:
  0.0 92.5 jit_solution(17228571578011340442)
XLA Ops:
  0.6 1.4 %copy.17.w_in = bf16[128,64]{1,0:T(8,128)(2,1)} copy(bf16[128,64]{0,1:T(8,128)(2,1)} %param.8) | data formatting | bytes 32768 | tf_op args[1]
  2.1 83.5 %shard_map.126 = (bf16[16,64,256]{2,1,0:T(8,128)(2,1)}, bf16[16,64,256]{2,1,0:T(8,128)(2,1)}, bf16[8,128,128]{2,1,0:T(8,128)(2,1)}, bf16[8,48,128]{2,1,0:T(8,128)(2,1)}) custom-call(bf16[64,16,256]{2,1,0:T(8,128)(2,1)} %frames.1, bf16[128,64]{1,0:T(8,128)(2,1)} %copy.17.w_in, bf16[256,256]{1,0:T(8,128)(2,1)} %grid_mix.1, bf16[256,256]{1,0:T(8,128)(2,1)} %block_mix.1, ...), custom_call_target="tpu_custom_call" | custom-call | tf_op jit(solution)/shard_map/pallas_call | solution.py:502
  85.6 0.0 copy-start
  85.6 2.2 %copy.19 = bf16[64,16,256]{2,1,0:T(8,128)(2,1)} copy(bf16[64,16,256]{2,0,1:T(8,128)(2,1)} %bitcast.19) | data formatting | bytes 1048576
  87.8 0.0 copy-done
  87.8 0.0 copy-start.2
  87.8 1.1 %copy.20 = bf16[64,16,256]{2,1,0:T(8,128)(2,1)} copy(bf16[64,16,256]{2,0,1:T(8,128)(2,1)S(1)} %bitcast.18) | data formatting | bytes 1048576
  88.9 0.0 copy-done.2
  88.9 0.0 copy-start.1
  88.9 0.1 slice.37
  89.0 0.7 copy.22
  89.7 0.1 copy-done.1
  89.9 0.8 pad_maximum_fusion
  90.8 0.7 slice_bitcast_fusion.1
  91.5 0.2 reshape.35
  91.7 0.1 reverse_bitcast_fusion
  91.7 0.7 copy.21
  (6 shorter events, 0.1 us)
Async XLA Ops:
  85.6 2.2 %copy-start = (bf16[16,64,256]{2,1,0:T(8,128)(2,1)S(1)}, bf16[16,64,256]{2,1,0:T(8,128)(2,1)}, u32[]{:S(2)}) copy-start(bf16[16,64,256]{2,1,0:T(8,128)(2,1)} %get-tuple-element.12) | copy-start | bytes 1572868
  87.8 1.1 %copy-start.2 = (bf16[8,48,128]{2,1,0:T(8,128)(2,1)S(1)}, bf16[8,48,128]{2,1,0:T(8,128)(2,1)}, u32[]{:S(2)}) copy-start(bf16[8,48,128]{2,1,0:T(8,128)(2,1)} %get-tuple-element.13) | copy-start | bytes 294916
  88.9 1.0 %copy-start.1 = (bf16[8,128,128]{2,1,0:T(8,128)(2,1)S(1)}, bf16[8,128,128]{2,1,0:T(8,128)(2,1)}, u32[]{:S(2)}) copy-start(bf16[8,128,128]{2,1,0:T(8,128)(2,1)} %get-tuple-element.14) | copy-start | bytes 786436
where the time goes:
time: 92.7 us; the launch traced here: 92.5 us
  Pallas kernels  83.5 us (90%)
  local copies, waits for them, and re-layouts  7.35 us (8%)
    pallas_call x1, Pallas kernels, body(): pl.pallas_call(kernel, out_shape=(jax.ShapeDtypeStruct((ROWS, CH, COLS),...  83.5 us
    unnamed x11, local copies, waits for them, and re-layouts  6.3 us

commit v1 on v0

v1 whole, which is shorter than its diff:
```python
import jax
import jax.numpy as jnp
from jax import lax
from jax.experimental import pallas as pl
from jax.experimental.pallas import tpu as pltpu
from jax.sharding import PartitionSpec as P

BF = jnp.bfloat16
F32 = jnp.float32
EPS = 1e-06
MESH = pl.DeviceIdType.MESH

CH = 64
HC = 32
ROWS = 16
COLS = 256
LANES = 128
NA = 16
NW = 8

(G_ROW0, G_PACK0, G_ROW1, G_PACK1, G_VA, G_VB, G_VC, G_VD, G_GA, G_GB, G_GC, G_GD) = range(12)
(G_E1, G_E2, G_E3, G_E4, G_T1, G_T2, G_T3) = range(12, 19)
GROUPS = 19


def dot(a, b):
    return lax.dot_general(a, b, (((1,), (0,)), ((), ())), preferred_element_type=F32)


def dot_nt(a, b):
    return lax.dot_general(a, b, (((1,), (1,)), ((), ())), preferred_element_type=F32)


def dot_tn(a, b):
    return lax.dot_general(a, b, (((0,), (0,)), ((), ())), preferred_element_type=F32)


def swap_granules(load, store, depth):
    lane = lax.broadcasted_iota(jnp.int32, (depth, LANES), 1)
    for row_half in range(2):
        for col_half in range(2):
            held = [load(row_half * 8 + k, col_half) for k in range(8)]
            for s in range(3):
                width = 16 << s
                low = (lane & width) == 0
                for k in range(8):
                    if not k & (1 << s):
                        a, b = held[k], held[k | (1 << s)]
                        held[k] = jnp.where(low, a, pltpu.roll(b, width, 1))
                        held[k | (1 << s)] = jnp.where(low, pltpu.roll(a, LANES - width, 1), b)
            for k in range(8):
                store(col_half * 8 + k, row_half, held[k])


def half(t):
    return slice(t * LANES, (t + 1) * LANES)


def loop(count, step, carry=0, unroll=1):
    return lax.fori_loop(0, count, step, carry, unroll=unroll)


def gelu_parts(x):
    root = 0.7978845608028654
    square = x * x
    t = jnp.tanh(root * (x + 0.044715 * (x * square)))
    cdf = 0.5 * (1.0 + t)
    return x * cdf, cdf + x * ((0.5 * root) * (1.0 - t * t) * (1.0 + (3 * 0.044715) * square))


def kernel(
    frames_hbm, w_in_t_hbm, grid_mix_hbm, block_mix_hbm, w_out_hbm, conv_w_hbm, cot_hbm,
    rest_out, gframe_out, early_out, tail_out,
    frames, w_in_t, grid_mix, block_mix, w_out, conv_w, cot, w_in,
    turn, xb, nb, unit, inv, dgelu, gates, bval, u3, v3, gj, gg, bback, xt, bt, bm, gbv,
    va, va_in, vx, vb, vb_in, vc, vc_in, vd, vd_in,
    ga, ga_in, gx, gb, gb_in, gc, gc_in, gd, gd_in,
    gated, gbef, jp, row_in, pack_out, pack_in, edge_l, edge_r,
    se, re1, e1, re2, e2, re3, e4, re4, st, rt1, t1, rt2, t2, rt3,
    ssem, rsem, isem,
):
    ia = lax.axis_index("ha")
    iw = lax.axis_index("wa")
    up, down = lax.rem(ia + NA - 1, NA), lax.rem(ia + 1, NA)
    left, right = lax.rem(iw + NW - 1, NW), lax.rem(iw + 1, NW)
    lane = lax.broadcasted_iota(jnp.int32, (CH, LANES), 1)

    loads = [
        pltpu.make_async_copy(src, dst, isem.at[k])
        for k, (src, dst) in enumerate(
            [
                (frames_hbm, frames),
                (w_in_t_hbm, w_in_t),
                (cot_hbm, cot),
                (conv_w_hbm, conv_w),
                (w_out_hbm, w_out),
                (block_mix_hbm, block_mix),
                (grid_mix_hbm, grid_mix),
            ]
        )
    ]
    for load in loads:
        load.start()

    def push(src, dst, g, where):
        pltpu.make_async_remote_copy(
            src_ref=src, dst_ref=dst, send_sem=ssem.at[g], recv_sem=rsem.at[g], device_id=where, device_id_type=MESH
        ).start()

    def over_w(src_of, dst, g):
        for k in range(1, NW):
            peer = lax.rem(iw + k, NW)
            push(src_of(peer), dst, g, (ia, peer))

    def over_a(src_of, dst, g):
        for k in range(1, NA):
            peer = lax.rem(ia + k, NA)
            push(src_of(peer), dst, g, (peer, iw))

    def arrived(ref, g):
        pltpu.make_async_copy(ref, ref, rsem.at[g]).wait()

    def gone(ref, g):
        pltpu.make_async_copy(ref, ref, ssem.at[g]).wait()

    def from_w(ref, g):
        arrived(ref.at[pl.ds(0, NW - 1)], g)

    def from_a(ref, g):
        arrived(ref.at[pl.ds(0, NA - 1)], g)

    barrier = pltpu.get_barrier_semaphore()
    peers = [(ia, lax.rem(iw + k, NW)) for k in range(1, NW)]
    peers += [(lax.rem(ia + k, NA), iw) for k in range(1, NA)]
    peers += [(a, b) for a in (up, down) for b in (left, right)]
    for peer in peers:
        pl.semaphore_signal(barrier, inc=1, device_id=peer, device_id_type=MESH)

    def turn_in(src):
        for t in range(2):
            turn[t] = src[:, :, half(t)].astype(F32).reshape(CH * ROWS, LANES)

    def turned(r, t):
        return turn[t, pl.ds(r, CH, stride=ROWS), :]

    def edges(pack, t0, t1, r):
        pack = jnp.where(lane == r, pltpu.roll(t0, r, 1), pack)
        return jnp.where(lane == ROWS + r, pltpu.roll(t1, r + 17, 1), pack)

    def send_halo(field, pack, which, g_row, g_pack):
        pack_out[which] = pack.astype(BF)
        push(field.at[1, CH : 2 * CH], row_in.at[which, 1], g_row, (up, iw))
        push(field.at[ROWS, CH : 2 * CH], row_in.at[which, 0], g_row, (down, iw))
        for slot, where in enumerate(
            [(ia, right), (ia, left), (down, right), (down, left), (up, right), (up, left)]
        ):
            push(pack_out.at[which], pack_in.at[which, slot], g_pack, where)

    def take_halo(field, which, g_row, g_pack):
        arrived(row_in.at[which], g_row)
        arrived(pack_in.at[which], g_pack)
        top = row_in[which, 0].astype(F32) * jnp.where(ia > 0, 1.0, 0.0)
        field[0, CH : 2 * CH] = top.astype(BF)
        bottom = row_in[which, 1].astype(F32) * jnp.where(ia < NA - 1, 1.0, 0.0)
        field[ROWS + 1, CH : 2 * CH] = bottom.astype(BF)
        first = jnp.where(ia > 0, 0, 1)
        last = jnp.where(ia < NA - 1, ROWS + 2, ROWS + 1)
        got = [pack_in[which, k].astype(F32) for k in range(6)]

        def assemble(middle, above, below, has):
            joined = jnp.where(lane == 0, above, jnp.where(lane == ROWS + 1, below, middle))
            return jnp.where((lane >= first) & (lane < jnp.where(has, last, 0)), joined, 0.0)

        edge_l[...] = assemble(
            pltpu.roll(got[0], 113, 1), pltpu.roll(got[2], 97, 1), pltpu.roll(got[4], 1, 1), iw > 0
        )
        edge_r[...] = assemble(
            pltpu.roll(got[1], 1, 1), pltpu.roll(got[3], 113, 1), pltpu.roll(got[5], 17, 1), iw < NW - 1
        )

        def shifts(p, carry):
            t0 = field[p, CH : 2 * CH, half(0)].astype(F32)
            t1 = field[p, CH : 2 * CH, half(1)].astype(F32)
            a0, a1 = pltpu.roll(t0, 1, 1), pltpu.roll(t1, 1, 1)
            b0, b1 = pltpu.roll(t0, LANES - 1, 1), pltpu.roll(t1, LANES - 1, 1)
            lh = pltpu.roll(edge_l[...], lax.rem(LANES - p, LANES), 1)
            rh = pltpu.roll(edge_r[...], LANES - 1 - p, 1)
            field[p, 0:CH, half(0)] = jnp.where(lane == 0, lh, a0).astype(BF)
            field[p, 0:CH, half(1)] = jnp.where(lane == 0, a0, a1).astype(BF)
            field[p, 2 * CH :, half(0)] = jnp.where(lane == LANES - 1, b1, b0).astype(BF)
            field[p, 2 * CH :, half(1)] = jnp.where(lane == LANES - 1, rh, b1).astype(BF)
            return carry

        loop(ROWS + 2, shifts, unroll=3)

    def step_a(a, a_in, g):
        over_w(lambda peer: a.at[peer], a_in.at[iw], g)
        a_in[iw] = a[iw]

    def step_b(a_in, x, b, b_in, g_a, g_b):
        from_w(a_in, g_a)

        def widen(j, carry):
            for t in range(2):
                for r in range(2):
                    x[pl.ds((r * 16 + j * 2 + t) * HC, HC), :] = a_in[j, t, r].astype(F32)
            return carry

        loop(NW, widen, unroll=4)

        def pick(q, carry):
            for r in range(2):
                for c in range(4):
                    b[r * 8 + q, :, half(c)] = x[pl.ds(r * 16 * HC + q * 4 + c, 16, stride=HC), :].astype(BF)
            return carry

        loop(8, pick, unroll=4)
        over_a(lambda peer: b.at[peer], b_in.at[ia], g_b)
        b_in[ia] = b[ia]

    def step_c(mixed, c, c_in, g):
        c[...] = mixed.astype(BF).reshape(NA, 16, 512)
        over_a(lambda peer: c.at[peer], c_in.at[ia], g)
        c_in[ia] = c[ia]

    def step_d(c_in, x, d, d_in, g_c, g_d):
        from_a(c_in, g_c)

        def unpick(q, carry):
            for r in range(2):
                for c in range(4):
                    x[pl.ds((r * HC + q * 4 + c) * 16, 16), :] = c_in[r * 8 + q, :, half(c)].astype(F32)
            return carry

        loop(8, unpick, unroll=4)

        def narrow(j, carry):
            for t in range(2):
                for r in range(2):
                    d[j, t, r] = x[pl.ds(r * HC * 16 + j * 2 + t, HC, stride=16), :].astype(BF)
            return carry

        loop(NW, narrow, unroll=4)
        over_w(lambda peer: d.at[peer], d_in.at[iw], g_d)
        d_in[iw] = d[iw]

    loads[0].wait()
    loads[1].wait()
    turn_in(frames)
    w_in[...] = w_in_t[...].astype(F32).T.astype(BF)

    def value_row(r, carry):
        for t in range(2):
            x = turned(r, t)
            xb[r, :, half(t)] = x.astype(BF)
            off = x - jnp.mean(x, axis=0, keepdims=True)
            rstd = lax.rsqrt(jnp.mean(off * off, axis=0, keepdims=True) + EPS)
            u = off * rstd
            unit[r, :, half(t)] = u
            inv[r, :, half(t)] = jnp.broadcast_to(rstd, (8, LANES))
            nb[r, :, half(t)] = u.astype(BF)
        value, slope = gelu_parts(dot(w_in[HC:CH], nb[r]))
        dgelu[r, HC:CH] = slope
        value = value.astype(BF)
        va[r // 2, 0, lax.rem(r, 2)] = value[:, half(0)]
        va[r // 2, 1, lax.rem(r, 2)] = value[:, half(1)]
        return carry

    loop(ROWS, value_row, unroll=4)
    pl.semaphore_wait(barrier, len(peers))
    step_a(va, va_in, G_VA)

    loads[2].wait()
    turn_in(cot)

    def cot_row(r, pack):
        t0, t1 = turned(r, 0), turned(r, 1)
        u3[r + 1, CH : 2 * CH, half(0)] = t0.astype(BF)
        u3[r + 1, CH : 2 * CH, half(1)] = t1.astype(BF)
        return edges(pack, t0, t1, r)

    pack = loop(ROWS, cot_row, jnp.zeros((CH, LANES), F32), unroll=4)
    send_halo(u3, pack, 0, G_ROW0, G_PACK0)

    def gate_row(r, carry):
        before = dot(w_in[...], nb[r])
        value, slope = gelu_parts(before[0:HC])
        gates[r, 0:HC] = value.astype(BF)
        dgelu[r, 0:HC] = slope
        value, slope = gelu_parts(before[CH:])
        dgelu[r, CH:] = slope
        value = value.astype(BF)
        gates[r, HC:CH] = value[0:HC]
        bval[r] = value[HC:]
        return carry

    loop(ROWS, gate_row, unroll=2)
    step_b(va_in, vx, vb, vb_in, G_VA, G_VB)

    take_halo(u3, 0, G_ROW0, G_PACK0)
    for load in loads[3:]:
        load.wait()
    back_w = jnp.concatenate(
        [conv_w[2 - a, 2 - b] for a in range(3) for b in range(3)], axis=0
    ).astype(F32).T.astype(BF)
    w_out_t = w_out[...].astype(F32).T.astype(BF)

    def back_row(r, carry):
        total = dot(back_w, u3[pl.ds(r, 3)].reshape(9 * CH, COLS))
        g = (total + u3[r + 1, CH : 2 * CH].astype(F32)).astype(BF)
        gj[r] = g
        up_gated = dot(w_out_t, g)
        gg[r] = up_gated
        mixed = (up_gated * gates[r].astype(F32)).astype(BF)
        ga[r // 2, 0, lax.rem(r, 2)] = mixed[0:HC, half(0)]
        ga[r // 2, 1, lax.rem(r, 2)] = mixed[0:HC, half(1)]
        bback[r] = mixed[HC:]
        return carry

    loop(ROWS, back_row, unroll=4)
    step_a(ga, ga_in, G_GA)

    mix = grid_mix[...]
    from_a(vb_in, G_VB)
    step_c(dot(mix, vb_in[...].reshape(256, 512)), vc, vc_in, G_VC)

    def put(ref):
        def store(k, t, value):
            ref[k, :, half(t)] = value.astype(ref.dtype)

        return store

    swap_granules(lambda k, t: bval[k, :, half(t)].astype(F32), put(xt), HC)
    values = xt[...].reshape(ROWS * HC, COLS)
    mixed = dot_nt(values, block_mix[...])
    swap_granules(lambda k, t: mixed[k * HC : (k + 1) * HC, half(t)], put(bm), HC)

    step_b(ga_in, gx, gb, gb_in, G_GA, G_GB)
    step_d(vc_in, vx, vd, vd_in, G_VC, G_VD)

    swap_granules(lambda k, t: bback[k, :, half(t)].astype(F32), put(bt), HC)
    backs = bt[...].reshape(ROWS * HC, COLS)
    unmixed = dot(backs, block_mix[...])
    swap_granules(lambda k, t: unmixed[k * HC : (k + 1) * HC, half(t)], put(gbv), HC)
    part_block = dot_tn(backs, values).astype(BF)
    se[2 * COLS : 3 * COLS] = part_block[:, half(0)]
    se[3 * COLS :] = part_block[:, half(1)]

    from_a(gb_in, G_GB)
    back = gb_in[...].reshape(256, 512)
    step_c(dot_tn(mix, back), gc, gc_in, G_GC)
    part_grid = dot_nt(back, vb_in[...].reshape(256, 512)).astype(BF)
    se[0:COLS] = part_grid[:, half(0)]
    se[COLS : 2 * COLS] = part_grid[:, half(1)]
    over_w(lambda peer: se.at[pl.ds(pl.multiple_of(peer * 128, 128), 128)], re1.at[iw], G_E1)
    re1[iw] = se[pl.ds(pl.multiple_of(iw * 128, 128), 128)]

    for k in (0, 1, ROWS + 2, ROWS + 3):
        jp[k] = jnp.zeros((CH, COLS), BF)
    from_w(vd_in, G_VD)

    def returned(ref, r):
        return [ref[r // 2, t, lax.rem(r, 2)].astype(F32) for t in range(2)]

    def joined_row(r, pack):
        grid_mixed = returned(vd_in, r)
        for t in range(2):
            gates_t = gates[r, :, half(t)].astype(F32)
            gated[r, 0:HC, half(t)] = (gates_t[0:HC] * (grid_mixed[t] + 1.0)).astype(BF)
            gated[r, HC:, half(t)] = (gates_t[HC:] * (bm[r, :, half(t)] + 1.0)).astype(BF)
        j = (xb[r].astype(F32) + dot(w_out[...], gated[r])).astype(BF)
        jp[r + 2] = j
        v3[r + 1, CH : 2 * CH] = j
        jf = j.astype(F32)
        return edges(pack, jf[:, half(0)], jf[:, half(1)], r)

    pack = loop(ROWS, joined_row, jnp.zeros((CH, LANES), F32), unroll=4)
    send_halo(v3, pack, 1, G_ROW1, G_PACK1)

    step_d(gc_in, gx, gd, gd_in, G_GC, G_GD)

    def conv_row(p, total):
        return total + dot_nt(u3[p], jp[pl.ds(p, 3)].reshape(3 * CH, COLS))

    p_conv = loop(ROWS + 2, conv_row, jnp.zeros((3 * CH, 3 * CH), F32), unroll=3)

    from_w(re1, G_E1)
    total = re1[0].astype(F32)
    for k in range(1, NW):
        total = total + re1[k].astype(F32)
    e1[...] = total
    over_a(lambda peer: e1.at[pl.ds(pl.multiple_of(peer * 8, 8), 8)], re2.at[ia], G_E2)
    re2[ia] = e1[pl.ds(pl.multiple_of(ia * 8, 8), 8)]

    from_w(gd_in, G_GD)

    def before_row(r, carry):
        p_in, p_out = carry
        grid_mixed = returned(vd_in, r)
        grid_back = returned(gd_in, r)
        for t in range(2):
            g = gg[r, :, half(t)]
            d = dgelu[r, :, half(t)]
            gbef[r, 0:HC, half(t)] = (d[0:HC] * (g[0:HC] * (grid_mixed[t] + 1.0))).astype(BF)
            gbef[r, HC:CH, half(t)] = (d[HC:CH] * grid_back[t]).astype(BF)
            gbef[r, CH : CH + HC, half(t)] = (d[CH : CH + HC] * (g[HC:] * (bm[r, :, half(t)] + 1.0))).astype(BF)
            gbef[r, CH + HC :, half(t)] = (d[CH + HC :] * gbv[r, :, half(t)]).astype(BF)
        return p_in + dot_nt(nb[r], gbef[r]), p_out + dot_nt(gj[r], gated[r])

    p_in, p_out = loop(
        ROWS, before_row, (jnp.zeros((CH, 2 * CH), F32), jnp.zeros((CH, CH), F32)), unroll=4
    )
    st[0 : 3 * CH] = p_conv[:, half(0)].astype(BF)
    st[3 * CH : 4 * CH] = p_in.astype(BF)
    third = p_conv[:, 2 * CH :]
    st[4 * CH :] = jnp.concatenate(
        [third[: 2 * CH], jnp.concatenate([third[2 * CH :], p_out], axis=0)], axis=1
    ).astype(BF)
    over_w(lambda peer: st.at[pl.ds(pl.multiple_of(peer * 48, 16), 48)], rt1.at[iw], G_T1)
    rt1[iw] = st[pl.ds(pl.multiple_of(iw * 48, 16), 48)]

    from_a(re2, G_E2)
    total = re2[0]
    for k in range(1, NA):
        total = total + re2[k]
    e2[...] = total
    over_a(lambda peer: e2, re3.at[ia], G_E3)
    re3[ia] = e2[...]

    def frame_row(r, carry):
        normed = dot(w_in_t[...], gbef[r])
        u = unit[r]
        mean_grad = jnp.mean(normed, axis=0, keepdims=True)
        mean_proj = jnp.mean(normed * u, axis=0, keepdims=True)
        source = gj[r].astype(F32) + inv[r, 0:1] * (normed - mean_grad - u * mean_proj)
        for t in range(2):
            gframe_out[t, pl.ds(r * CH, CH), :] = source[:, half(t)]
        return carry

    loop(ROWS, frame_row, unroll=4)

    from_w(rt1, G_T1)
    total = rt1[0].astype(F32)
    for k in range(1, NW):
        total = total + rt1[k].astype(F32)
    t1[...] = total.astype(BF)
    over_a(lambda peer: t1, rt2.at[ia], G_T2)
    rt2[ia] = t1[...]

    from_a(re3, G_E3)
    e4[...] = re3[...].reshape(128, LANES).astype(BF)
    over_w(lambda peer: e4, re4.at[iw], G_E4)
    re4[iw] = e4[...]

    take_halo(v3, 1, G_ROW1, G_PACK1)
    from_a(rt2, G_T2)
    total = rt2[0].astype(F32)
    for k in range(1, NA):
        total = total + rt2[k].astype(F32)
    t2[...] = total.astype(BF)
    over_w(lambda peer: t2, rt3.at[iw], G_T3)
    rt3[iw] = t2[...]

    conv_k = jnp.concatenate(
        [conv_w[a, b].astype(F32).T for a in range(3) for b in range(3)], axis=0
    ).T.astype(BF)

    def out_row(r, carry):
        total = dot(conv_k, v3[pl.ds(r, 3)].reshape(9 * CH, COLS))
        total = total + v3[r + 1, CH : 2 * CH].astype(F32)
        for t in range(2):
            rest_out[t, pl.ds(r * CH, CH), :] = total[:, half(t)]
        return carry

    loop(ROWS, out_row, unroll=4)

    from_w(re4, G_E4)
    early_out[...] = re4[...]
    from_w(rt3, G_T3)
    tail_out[...] = rt3[...]

    for which, g_row, g_pack in ((0, G_ROW0, G_PACK0), (1, G_ROW1, G_PACK1)):
        gone(row_in.at[which], g_row)
        gone(pack_in.at[which], g_pack)
    for ref, g in (
        (va_in, G_VA), (vd_in, G_VD), (ga_in, G_GA), (gd_in, G_GD),
        (re1, G_E1), (re4, G_E4), (rt1, G_T1), (rt3, G_T3),
    ):
        gone(ref.at[pl.ds(0, NW - 1)], g)
    for ref, g in (
        (vb_in, G_VB), (vc_in, G_VC), (gb_in, G_GB), (gc_in, G_GC), (re2, G_E2), (re3, G_E3), (rt2, G_T2),
    ):
        gone(ref.at[pl.ds(0, NA - 1)], g)


def finish(rest, gframe, early, tail, restored, grad_frames, grad_w_in_t, grad_grid, grad_block, grad_w_out, grad_conv):
    scale = float(ROWS * NA * COLS * NW) ** (-0.5)

    def channel(c, carry):
        for src, dst in ((rest, restored), (gframe, grad_frames)):
            for t in range(2):
                dst[c, :, half(t)] = src[t, pl.ds(c, ROWS, stride=CH), :].astype(BF)
        return carry

    loop(CH, channel, unroll=8)

    for k in range(2):
        grad_grid[:, half(k)] = early[k * COLS : (k + 1) * COLS].astype(F32) * scale
        grad_block[:, half(k)] = early[(2 + k) * COLS : (3 + k) * COLS].astype(F32) * scale
    grad_w_in_t[...] = tail[3 * CH : 4 * CH].astype(F32) * scale
    last = tail[4 * CH :].astype(F32) * scale
    grad_w_out[...] = last[CH:, CH:]
    for b in range(3):
        rows = slice((2 - b) * CH, (3 - b) * CH)
        pair = tail[rows].astype(F32) * scale
        grad_conv[0, b] = pair[:, :CH]
        grad_conv[1, b] = pair[:, CH:]
    grad_conv[2, 2] = last[:CH, :CH]
    grad_conv[2, 1] = last[CH:, :CH]
    grad_conv[2, 0] = last[:CH, CH:]


def vm(*shape, dtype=BF):
    return pltpu.VMEM(shape, dtype)


def exchange():
    message_w = vm(NW, 2, 2, HC, LANES)
    message_a = vm(NA, 16, 512)
    return [message_w, message_w, vm(2 * 16 * HC, LANES, dtype=F32)] + [message_a] * 4 + [message_w] * 2


SCRATCH = [
    vm(CH, ROWS, COLS),
    vm(CH, 2 * CH),
    vm(COLS, COLS),
    vm(COLS, COLS),
    vm(CH, CH),
    vm(3, 3, CH, CH),
    vm(CH, ROWS, COLS),
    vm(2 * CH, CH),
    vm(2, CH * ROWS, LANES, dtype=F32),
    vm(ROWS, CH, COLS),
    vm(ROWS, CH, COLS),
    vm(ROWS, CH, COLS, dtype=F32),
    vm(ROWS, 8, COLS, dtype=F32),
    vm(ROWS, 2 * CH, COLS, dtype=F32),
    vm(ROWS, CH, COLS),
    vm(ROWS, HC, COLS),
    vm(ROWS + 2, 3 * CH, COLS),
    vm(ROWS + 2, 3 * CH, COLS),
    vm(ROWS, CH, COLS),
    vm(ROWS, CH, COLS, dtype=F32),
    vm(ROWS, HC, COLS),
    vm(ROWS, HC, COLS),
    vm(ROWS, HC, COLS),
    vm(ROWS, HC, COLS, dtype=F32),
    vm(ROWS, HC, COLS, dtype=F32),
    *exchange(),
    *exchange(),
    vm(ROWS, CH, COLS),
    vm(ROWS, 2 * CH, COLS),
    vm(ROWS + 4, CH, COLS),
    vm(2, 2, CH, COLS),
    vm(2, CH, LANES),
    vm(2, 6, CH, LANES),
    vm(CH, LANES, dtype=F32),
    vm(CH, LANES, dtype=F32),
    vm(4 * COLS, LANES),
    vm(NW, 128, LANES),
    vm(128, LANES, dtype=F32),
    vm(NA, 8, LANES, dtype=F32),
    vm(8, LANES, dtype=F32),
    vm(NA, 8, LANES, dtype=F32),
    vm(128, LANES),
    vm(NW, 128, LANES),
    vm(6 * CH, LANES),
    vm(NW, 48, LANES),
    vm(48, LANES),
    vm(NA, 48, LANES),
    vm(48, LANES),
    vm(NW, 48, LANES),
    pltpu.SemaphoreType.DMA((GROUPS,)),
    pltpu.SemaphoreType.DMA((GROUPS,)),
    pltpu.SemaphoreType.DMA((7,)),
]


def body(frames, w_in, grid_mix, block_mix, w_out, conv_w, cotangent):
    vmem = pl.BlockSpec(memory_space=pltpu.VMEM)
    shape = jax.ShapeDtypeStruct
    rest, gframe, early, tail = pl.pallas_call(
        kernel,
        out_shape=(
            shape((2, ROWS * CH, LANES), F32),
            shape((2, ROWS * CH, LANES), F32),
            shape((NW, 128, LANES), BF),
            shape((NW, 48, LANES), BF),
        ),
        in_specs=[pl.BlockSpec(memory_space=pltpu.HBM)] * 7,
        out_specs=(vmem,) * 4,
        scratch_shapes=SCRATCH,
        compiler_params=pltpu.CompilerParams(
            collective_id=0, has_side_effects=True, vmem_limit_bytes=32 * 1024 * 1024
        ),
    )(frames, w_in.T, grid_mix, block_mix, w_out, conv_w, cotangent)
    restored, grad_frames, grad_w_in_t, grad_grid, grad_block, grad_w_out, grad_conv = pl.pallas_call(
        finish,
        out_shape=(
            shape((CH, ROWS, COLS), BF),
            shape((CH, ROWS, COLS), BF),
            shape((CH, 2 * CH), F32),
            shape((COLS, COLS), F32),
            shape((COLS, COLS), F32),
            shape((CH, CH), F32),
            shape((3, 3, CH, CH), F32),
        ),
        in_specs=[vmem] * 4,
        out_specs=(vmem,) * 7,
        compiler_params=pltpu.CompilerParams(vmem_limit_bytes=16 * 1024 * 1024),
    )(rest, gframe, early.reshape(4 * COLS, LANES), tail.reshape(6 * CH, LANES))
    return restored, grad_frames, grad_w_in_t.T, grad_grid, grad_block, grad_w_out, grad_conv


def solution(mesh):
    placed = (P(None, "ha", "wa"), P(), P(), P(), P(), P(), P(None, "ha", "wa"))
    return jax.shard_map(
        body,
        mesh=mesh,
        in_specs=placed,
        out_specs=(P(None, "ha", "wa"), P(None, "ha", "wa"), P(), P(), P(), P(), P()),
        check_vma=False,
    )
```

time: 92.7 us -> 79 us (0.85)
  the two profiles are of different devices: /device:TPU:1 before, /device:TPU:24 now
where the time goes in v1:
time: 79 us; the launch traced here: 78.6 us
  Pallas kernels  71.8 us (91%)
  local copies, waits for them, and re-layouts  6.23 us (8%)
    pallas_call x1, Pallas kernels, body(): pl.pallas_call(kernel, out_shape=(shape((2, ROWS * CH, LANES), F32), shap...  69.1 us
    unnamed x14, local copies, waits for them, and re-layouts  6.23 us
    pallas_call x1, Pallas kernels, body(): pl.pallas_call(finish, out_shape=(shape((CH, ROWS, COLS), BF), shape((CH,...  2.63 us

profile of v1, /device:TPU:24, one launch (start us, length us, event | category | flops | bytes accessed | tf_op | source)
XLA Modules:
  0.0 78.6 jit_solution(6360115667745546887)
XLA Ops:
  0.6 0.0 copy-start
  0.6 1.0 %copy-done = bf16[64,16,256]{2,1,0:T(8,128)(2,1)S(1)} copy-done((bf16[64,16,256]{2,1,0:T(8,128)(2,1)S(1)}, bf16[64,16,256]{2,1,0:T(8,128)(2,1)}, u32[]{:S(2)}) %copy-start) | copy-done | bytes 524312
  1.7 0.0 copy-start.1
  1.7 1.0 %copy-done.1 = bf16[64,16,256]{2,1,0:T(8,128)(2,1)S(1)} copy-done((bf16[64,16,256]{2,1,0:T(8,128)(2,1)S(1)}, bf16[64,16,256]{2,1,0:T(8,128)(2,1)}, u32[]{:S(2)}) %copy-start.1) | copy-done | bytes 524312
  2.7 0.0 copy-start.2
  2.7 0.9 %copy-done.2 = bf16[3,3,64,64]{3,2,1,0:T(8,128)(2,1)S(1)} copy-done((bf16[3,3,64,64]{3,2,1,0:T(8,128)(2,1)S(1)}, bf16[3,3,64,64]{3,2,1,0:T(8,128)(2,1)}, u32[]{:S(2)}) %copy-start.2) | copy-done | bytes 73752
  3.6 0.0 copy-start.3
  3.6 0.9 %copy-done.3 = bf16[256,256]{1,0:T(8,128)(2,1)S(1)} copy-done((bf16[256,256]{1,0:T(8,128)(2,1)S(1)}, bf16[256,256]{1,0:T(8,128)(2,1)}, u32[]{:S(2)}) %copy-start.3) | copy-done | bytes 131096
  4.5 0.0 copy-start.4
  4.5 0.9 %copy-done.4 = bf16[256,256]{1,0:T(8,128)(2,1)S(1)} copy-done((bf16[256,256]{1,0:T(8,128)(2,1)S(1)}, bf16[256,256]{1,0:T(8,128)(2,1)}, u32[]{:S(2)}) %copy-start.4) | copy-done | bytes 131096
  5.4 0.0 copy-start.5
  5.4 0.7 copy-done.5
  6.2 0.0 copy-start.6
  6.2 0.7 copy-done.6
  6.9 69.1 %shard_map.126 = (f32[2,1024,128]{2,1,0:T(8,128)S(1)}, f32[2,1024,128]{2,1,0:T(8,128)S(1)}, bf16[8,128,128]{2,1,0:T(8,128)(2,1)S(1)}, bf16[8,48,128]{2,1,0:T(8,128)(2,1)S(1)}) custom-call(bf16[64,16,256]{2,1,0:T(8,128)(2,1)S(1)} %copy-done, bf16[64,128]{1,0:T(8,128)(2,1)S(1)} %bitcast.6, bf16[256,256]{1,0:T(8,128)(2,1)S(1)} %copy-done.3, ...), custom_call_target="tpu_custom_call" | custom-call | tf_op jit(solution)/shard_map/pallas_call | solution.py:592
  76.0 2.6 %shard_map.127 = (bf16[64,16,256]{2,1,0:T(8,128)(2,1)}, bf16[64,16,256]{2,1,0:T(8,128)(2,1)}, f32[64,128]{1,0:T(8,128)}, f32[256,256]{1,0:T(8,128)}, f32[256,256...) custom-call(f32[2,1024,128]{2,1,0:T(8,128)S(1)} %get-tuple-element.18.rest, ...), custom_call_target="tpu_custom_call" | custom-call | tf_op jit(solution)/shard_map/pallas_call | solution.py:607
Async XLA Ops:
  0.6 1.0 %copy-start = (bf16[64,16,256]{2,1,0:T(8,128)(2,1)S(1)}, bf16[64,16,256]{2,1,0:T(8,128)(2,1)}, u32[]{:S(2)}) copy-start(bf16[64,16,256]{2,1,0:T(8,128)(2,1)} %frames_hbm.1) | copy-start | bytes 1572868
  1.7 1.0 %copy-start.1 = (bf16[64,16,256]{2,1,0:T(8,128)(2,1)S(1)}, bf16[64,16,256]{2,1,0:T(8,128)(2,1)}, u32[]{:S(2)}) copy-start(bf16[64,16,256]{2,1,0:T(8,128)(2,1)} %cot_hbm.1) | copy-start | bytes 1572868
  2.7 0.9 %copy-start.2 = (bf16[3,3,64,64]{3,2,1,0:T(8,128)(2,1)S(1)}, bf16[3,3,64,64]{3,2,1,0:T(8,128)(2,1)}, u32[]{:S(2)}) copy-start(bf16[3,3,64,64]{3,2,1,0:T(8,128)(2,1)} %conv_w_hbm.1) | copy-start | bytes 221188
  3.6 0.9 %copy-start.3 = (bf16[256,256]{1,0:T(8,128)(2,1)S(1)}, bf16[256,256]{1,0:T(8,128)(2,1)}, u32[]{:S(2)}) copy-start(bf16[256,256]{1,0:T(8,128)(2,1)} %grid_mix_hbm.1) | copy-start | bytes 393220
  4.5 0.9 %copy-start.4 = (bf16[256,256]{1,0:T(8,128)(2,1)S(1)}, bf16[256,256]{1,0:T(8,128)(2,1)}, u32[]{:S(2)}) copy-start(bf16[256,256]{1,0:T(8,128)(2,1)} %block_mix_hbm.1) | copy-start | bytes 393220
  5.4 0.7 copy-start.5
  6.2 0.7 copy-start.6

commit v2 on v1

--- a/solution.py
+++ b/solution.py
@@ -62,10 +62,11 @@
 
 def gelu_parts(x):
     root = 0.7978845608028654
+    cube = root * 0.044715
     square = x * x
-    t = jnp.tanh(root * (x + 0.044715 * (x * square)))
-    cdf = 0.5 * (1.0 + t)
-    return x * cdf, cdf + x * ((0.5 * root) * (1.0 - t * t) * (1.0 + (3 * 0.044715) * square))
+    h = 0.5 * jnp.tanh(x * (cube * square + root)) + 0.5
+    value = x * h
+    return value, h + value * (1.0 - h) * ((6.0 * cube) * square + 2.0 * root)
 
 
 def kernel(
@@ -193,6 +194,16 @@
 
         loop(ROWS + 2, shifts, unroll=3)
 
+    def conv_start(w, field):
+        y = dot(w, field[0])
+        z = dot(w, field[1])
+        return z[0:CH], y[0:CH] + z[CH : 2 * CH]
+
+    def conv_step(w, field, r, carry):
+        later, now = carry
+        y = dot(w, field[r + 2])
+        return now + y[2 * CH :], (y[0:CH], later + y[CH : 2 * CH])
+
     def step_a(a, a_in, g):
         over_w(lambda peer: a.at[peer], a_in.at[iw], g)
         a_in[iw] = a[iw]
@@ -294,19 +305,19 @@
         bval[r] = value[HC:]
         return carry
 
-    loop(ROWS, gate_row, unroll=2)
+    loop(ROWS, gate_row, unroll=4)
     step_b(va_in, vx, vb, vb_in, G_VA, G_VB)
 
     take_halo(u3, 0, G_ROW0, G_PACK0)
     for load in loads[3:]:
         load.wait()
     back_w = jnp.concatenate(
-        [conv_w[2 - a, 2 - b] for a in range(3) for b in range(3)], axis=0
+        [jnp.concatenate([conv_w[2 - a, 2 - b] for a in range(3)], axis=1) for b in range(3)], axis=0
     ).astype(F32).T.astype(BF)
     w_out_t = w_out[...].astype(F32).T.astype(BF)
 
     def back_row(r, carry):
-        total = dot(back_w, u3[pl.ds(r, 3)].reshape(9 * CH, COLS))
+        total, carry = conv_step(back_w, u3, r, carry)
         g = (total + u3[r + 1, CH : 2 * CH].astype(F32)).astype(BF)
         gj[r] = g
         up_gated = dot(w_out_t, g)
@@ -317,7 +328,7 @@
         bback[r] = mixed[HC:]
         return carry
 
-    loop(ROWS, back_row, unroll=4)
+    loop(ROWS, back_row, conv_start(back_w, u3), unroll=4)
     step_a(ga, ga_in, G_GA)
 
     mix = grid_mix[...]
@@ -379,11 +390,6 @@
 
     step_d(gc_in, gx, gd, gd_in, G_GC, G_GD)
 
-    def conv_row(p, total):
-        return total + dot_nt(u3[p], jp[pl.ds(p, 3)].reshape(3 * CH, COLS))
-
-    p_conv = loop(ROWS + 2, conv_row, jnp.zeros((3 * CH, 3 * CH), F32), unroll=3)
-
     from_w(re1, G_E1)
     total = re1[0].astype(F32)
     for k in range(1, NW):
@@ -391,6 +397,19 @@
     e1[...] = total
     over_a(lambda peer: e1.at[pl.ds(pl.multiple_of(peer * 8, 8), 8)], re2.at[ia], G_E2)
     re2[ia] = e1[pl.ds(pl.multiple_of(ia * 8, 8), 8)]
+
+    def conv_row(p, total):
+        return total + dot_nt(u3[p], jp[pl.ds(p, 3)].reshape(3 * CH, COLS))
+
+    p_conv = loop(ROWS + 2, conv_row, jnp.zeros((3 * CH, 3 * CH), F32), unroll=6)
+
+    from_a(re2, G_E2)
+    total = re2[0]
+    for k in range(1, NA):
+        total = total + re2[k]
+    e2[...] = total
+    over_a(lambda peer: e2, re3.at[ia], G_E3)
+    re3[ia] = e2[...]
 
     from_w(gd_in, G_GD)
 
@@ -419,13 +438,10 @@
     over_w(lambda peer: st.at[pl.ds(pl.multiple_of(peer * 48, 16), 48)], rt1.at[iw], G_T1)
     rt1[iw] = st[pl.ds(pl.multiple_of(iw * 48, 16), 48)]
 
-    from_a(re2, G_E2)
-    total = re2[0]
-    for k in range(1, NA):
-        total = total + re2[k]
-    e2[...] = total
-    over_a(lambda peer: e2, re3.at[ia], G_E3)
-    re3[ia] = e2[...]
+    from_a(re3, G_E3)
+    e4[...] = re3[...].reshape(128, LANES).astype(BF)
+    over_w(lambda peer: e4, re4.at[iw], G_E4)
+    re4[iw] = e4[...]
 
     def frame_row(r, carry):
         normed = dot(w_in_t[...], gbef[r])
@@ -447,11 +463,6 @@
     over_a(lambda peer: t1, rt2.at[ia], G_T2)
     rt2[ia] = t1[...]
 
-    from_a(re3, G_E3)
-    e4[...] = re3[...].reshape(128, LANES).astype(BF)
-    over_w(lambda peer: e4, re4.at[iw], G_E4)
-    re4[iw] = e4[...]
-
     take_halo(v3, 1, G_ROW1, G_PACK1)
     from_a(rt2, G_T2)
     total = rt2[0].astype(F32)
@@ -462,17 +473,17 @@
     rt3[iw] = t2[...]
 
     conv_k = jnp.concatenate(
-        [conv_w[a, b].astype(F32).T for a in range(3) for b in range(3)], axis=0
-    ).T.astype(BF)
+        [jnp.concatenate([conv_w[a, b] for b in range(3)], axis=1) for a in range(3)], axis=0
+    )
 
     def out_row(r, carry):
-        total = dot(conv_k, v3[pl.ds(r, 3)].reshape(9 * CH, COLS))
+        total, carry = conv_step(conv_k, v3, r, carry)
         total = total + v3[r + 1, CH : 2 * CH].astype(F32)
         for t in range(2):
             rest_out[t, pl.ds(r * CH, CH), :] = total[:, half(t)]
         return carry
 
-    loop(ROWS, out_row, unroll=4)
+    loop(ROWS, out_row, conv_start(conv_k, v3), unroll=4)
 
     from_w(re4, G_E4)
     early_out[...] = re4[...]
@@ -587,6 +598,7 @@
 
 
 def body(frames, w_in, grid_mix, block_mix, w_out, conv_w, cotangent):
+    operands = (frames, w_in.T, grid_mix, block_mix, w_out, conv_w, cotangent)
     vmem = pl.BlockSpec(memory_space=pltpu.VMEM)
     shape = jax.ShapeDtypeStruct
     rest, gframe, early, tail = pl.pallas_call(
@@ -603,7 +615,7 @@
         compiler_params=pltpu.CompilerParams(
             collective_id=0, has_side_effects=True, vmem_limit_bytes=32 * 1024 * 1024
         ),
-    )(frames, w_in.T, grid_mix, block_mix, w_out, conv_w, cotangent)
+    )(*[pltpu.with_memory_space_constraint(x, pltpu.HBM) for x in operands])
     restored, grad_frames, grad_w_in_t, grad_grid, grad_block, grad_w_out, grad_conv = pl.pallas_call(
         finish,
         out_shape=(

time: 79 us -> 69.1 us (0.87)
  the two profiles are of different devices: /device:TPU:24 before, /device:TPU:1 now
where the time goes in v2:
time: 69.1 us; the launch traced here: 69 us
  Pallas kernels  68.3 us (99%)
    pallas_call x1, Pallas kernels, body(): pl.pallas_call(kernel, out_shape=(shape((2, ROWS * CH, LANES), F32), shap...  65.7 us
    pallas_call x1, Pallas kernels, body(): pl.pallas_call(finish, out_shape=(shape((CH, ROWS, COLS), BF), shape((CH,...  2.63 us

profile of v2, /device:TPU:1, one launch (start us, length us, event | category | flops | bytes accessed | tf_op | source)
XLA Modules:
  0.0 69.0 jit_solution(9650003316849763806)
XLA Ops:
  0.6 65.7 %shard_map.126 = (f32[2,1024,128]{2,1,0:T(8,128)S(1)}, f32[2,1024,128]{2,1,0:T(8,128)S(1)}, bf16[8,128,128]{2,1,0:T(8,128)(2,1)S(1)}, bf16[8,48,128]{2,1,0:T(8,128)(2,1)S(1)}) custom-call(bf16[64,16,256]{2,1,0:T(8,128)(2,1)} %frames_hbm.1, bf16[64,128]{1,0:T(8,128)(2,1)} %bitcast.6, bf16[256,256]{1,0:T(8,128)(2,1)} %grid_mix_hbm.1, ...), custom_call_target="tpu_custom_call" | custom-call | tf_op jit(solution)/shard_map/pallas_call | solution.py:604
  66.3 2.6 %shard_map.127 = (bf16[64,16,256]{2,1,0:T(8,128)(2,1)}, bf16[64,16,256]{2,1,0:T(8,128)(2,1)}, f32[64,128]{1,0:T(8,128)}, f32[256,256]{1,0:T(8,128)}, f32[256,256...) custom-call(f32[2,1024,128]{2,1,0:T(8,128)S(1)} %get-tuple-element.18.rest, ...), custom_call_target="tpu_custom_call" | custom-call | tf_op jit(solution)/shard_map/pallas_call | solution.py:619

commit v3 on v2

--- a/solution.py
+++ b/solution.py
@@ -192,7 +192,7 @@
             field[p, 2 * CH :, half(1)] = jnp.where(lane == LANES - 1, rh, b1).astype(BF)
             return carry
 
-        loop(ROWS + 2, shifts, unroll=3)
+        loop(ROWS + 2, shifts, unroll=9)
 
     def conv_start(w, field):
         y = dot(w, field[0])
@@ -217,7 +217,7 @@
                     x[pl.ds((r * 16 + j * 2 + t) * HC, HC), :] = a_in[j, t, r].astype(F32)
             return carry
 
-        loop(NW, widen, unroll=4)
+        loop(NW, widen, unroll=8)
 
         def pick(q, carry):
             for r in range(2):
@@ -225,7 +225,7 @@
                     b[r * 8 + q, :, half(c)] = x[pl.ds(r * 16 * HC + q * 4 + c, 16, stride=HC), :].astype(BF)
             return carry
 
-        loop(8, pick, unroll=4)
+        loop(8, pick, unroll=8)
         over_a(lambda peer: b.at[peer], b_in.at[ia], g_b)
         b_in[ia] = b[ia]
 
@@ -243,7 +243,7 @@
                     x[pl.ds((r * HC + q * 4 + c) * 16, 16), :] = c_in[r * 8 + q, :, half(c)].astype(F32)
             return carry
 
-        loop(8, unpick, unroll=4)
+        loop(8, unpick, unroll=8)
 
         def narrow(j, carry):
             for t in range(2):
@@ -251,7 +251,7 @@
                     d[j, t, r] = x[pl.ds(r * HC * 16 + j * 2 + t, HC, stride=16), :].astype(BF)
             return carry
 
-        loop(NW, narrow, unroll=4)
+        loop(NW, narrow, unroll=8)
         over_w(lambda peer: d.at[peer], d_in.at[iw], g_d)
         d_in[iw] = d[iw]
 
@@ -277,7 +277,7 @@
         va[r // 2, 1, lax.rem(r, 2)] = value[:, half(1)]
         return carry
 
-    loop(ROWS, value_row, unroll=4)
+    loop(ROWS, value_row, unroll=8)
     pl.semaphore_wait(barrier, len(peers))
     step_a(va, va_in, G_VA)
 
@@ -290,7 +290,7 @@
         u3[r + 1, CH : 2 * CH, half(1)] = t1.astype(BF)
         return edges(pack, t0, t1, r)
 
-    pack = loop(ROWS, cot_row, jnp.zeros((CH, LANES), F32), unroll=4)
+    pack = loop(ROWS, cot_row, jnp.zeros((CH, LANES), F32), unroll=8)
     send_halo(u3, pack, 0, G_ROW0, G_PACK0)
 
     def gate_row(r, carry):
@@ -305,7 +305,7 @@
         bval[r] = value[HC:]
         return carry
 
-    loop(ROWS, gate_row, unroll=4)
+    loop(ROWS, gate_row, unroll=8)
     step_b(va_in, vx, vb, vb_in, G_VA, G_VB)
 
     take_halo(u3, 0, G_ROW0, G_PACK0)
@@ -328,7 +328,7 @@
         bback[r] = mixed[HC:]
         return carry
 
-    loop(ROWS, back_row, conv_start(back_w, u3), unroll=4)
+    loop(ROWS, back_row, conv_start(back_w, u3), unroll=8)
     step_a(ga, ga_in, G_GA)
 
     mix = grid_mix[...]
@@ -385,7 +385,7 @@
         jf = j.astype(F32)
         return edges(pack, jf[:, half(0)], jf[:, half(1)], r)
 
-    pack = loop(ROWS, joined_row, jnp.zeros((CH, LANES), F32), unroll=4)
+    pack = loop(ROWS, joined_row, jnp.zeros((CH, LANES), F32), unroll=8)
     send_halo(v3, pack, 1, G_ROW1, G_PACK1)
 
     step_d(gc_in, gx, gd, gd_in, G_GC, G_GD)
@@ -401,7 +401,7 @@
     def conv_row(p, total):
         return total + dot_nt(u3[p], jp[pl.ds(p, 3)].reshape(3 * CH, COLS))
 
-    p_conv = loop(ROWS + 2, conv_row, jnp.zeros((3 * CH, 3 * CH), F32), unroll=6)
+    p_conv = loop(ROWS + 2, conv_row, jnp.zeros((3 * CH, 3 * CH), F32), unroll=9)
 
     from_a(re2, G_E2)
     total = re2[0]
@@ -453,7 +453,7 @@
             gframe_out[t, pl.ds(r * CH, CH), :] = source[:, half(t)]
         return carry
 
-    loop(ROWS, frame_row, unroll=4)
+    loop(ROWS, frame_row, unroll=8)
 
     from_w(rt1, G_T1)
     total = rt1[0].astype(F32)
@@ -483,7 +483,7 @@
             rest_out[t, pl.ds(r * CH, CH), :] = total[:, half(t)]
         return carry
 
-    loop(ROWS, out_row, conv_start(conv_k, v3), unroll=4)
+    loop(ROWS, out_row, conv_start(conv_k, v3), unroll=8)
 
     from_w(re4, G_E4)
     early_out[...] = re4[...]

time: 69.1 us -> 67.8 us (0.981)
  Pallas kernels: 68.3 us -> 67 us
    pallas_call x1, Pallas kernels: 65.7 us -> 64.4 us  [body(): pl.pallas_call(kernel, out_shape=(shape((2, ROWS * CH, LANES), F32), shap...]
where the time goes in v3:
time: 67.8 us; the launch traced here: 67.6 us
  Pallas kernels  67 us (99%)
    pallas_call x1, Pallas kernels, body(): pl.pallas_call(kernel, out_shape=(shape((2, ROWS * CH, LANES), F32), shap...  64.4 us
    pallas_call x1, Pallas kernels, body(): pl.pallas_call(finish, out_shape=(shape((CH, ROWS, COLS), BF), shape((CH,...  2.63 us

profile of v3, /device:TPU:1, one launch (start us, length us, event | category | flops | bytes accessed | tf_op | source)
XLA Modules:
  0.0 67.6 jit_solution(12309203459646433942)
XLA Ops:
  0.6 64.4 %shard_map.126 = (f32[2,1024,128]{2,1,0:T(8,128)S(1)}, f32[2,1024,128]{2,1,0:T(8,128)S(1)}, bf16[8,128,128]{2,1,0:T(8,128)(2,1)S(1)}, bf16[8,48,128]{2,1,0:T(8,128)(2,1)S(1)}) custom-call(bf16[64,16,256]{2,1,0:T(8,128)(2,1)} %frames_hbm.1, bf16[64,128]{1,0:T(8,128)(2,1)} %bitcast.6, bf16[256,256]{1,0:T(8,128)(2,1)} %grid_mix_hbm.1, ...), custom_call_target="tpu_custom_call" | custom-call | tf_op jit(solution)/shard_map/pallas_call | solution.py:604
  65.0 2.6 %shard_map.127 = (bf16[64,16,256]{2,1,0:T(8,128)(2,1)}, bf16[64,16,256]{2,1,0:T(8,128)(2,1)}, f32[64,128]{1,0:T(8,128)}, f32[256,256]{1,0:T(8,128)}, f32[256,256...) custom-call(f32[2,1024,128]{2,1,0:T(8,128)S(1)} %get-tuple-element.18.rest, ...), custom_call_target="tpu_custom_call" | custom-call | tf_op jit(solution)/shard_map/pallas_call | solution.py:619

commit v4 on v3

--- a/solution.py
+++ b/solution.py
@@ -17,10 +17,12 @@
 LANES = 128
 NA = 16
 NW = 8
+NEAR = 8
+FAR = 16
 
 (G_ROW0, G_PACK0, G_ROW1, G_PACK1, G_VA, G_VB, G_VC, G_VD, G_GA, G_GB, G_GC, G_GD) = range(12)
-(G_E1, G_E2, G_E3, G_E4, G_T1, G_T2, G_T3) = range(12, 19)
-GROUPS = 19
+(G_E0, G_E1, G_E2, G_E3, G_E4, G_E5, G_T1, G_T2, G_T3) = range(12, 21)
+GROUPS = 21
 
 
 def dot(a, b):
@@ -77,7 +79,7 @@
     va, va_in, vx, vb, vb_in, vc, vc_in, vd, vd_in,
     ga, ga_in, gx, gb, gb_in, gc, gc_in, gd, gd_in,
     gated, gbef, jp, row_in, pack_out, pack_in, edge_l, edge_r,
-    se, re1, e1, re2, e2, re3, e4, re4, st, rt1, t1, rt2, t2, rt3,
+    mixp, se, re0, e0, re1, e1, re2, e2, re3, e4, re4, e5, st, rt1, t1, rt2, t2, rt3,
     ssem, rsem, isem,
 ):
     ia = lax.axis_index("ha")
@@ -108,15 +110,31 @@
             src_ref=src, dst_ref=dst, send_sem=ssem.at[g], recv_sem=rsem.at[g], device_id=where, device_id_type=MESH
         ).start()
 
-    def over_w(src_of, dst, g):
-        for k in range(1, NW):
-            peer = lax.rem(iw + k, NW)
-            push(src_of(peer), dst, g, (ia, peer))
-
-    def over_a(src_of, dst, g):
-        for k in range(1, NA):
-            peer = lax.rem(ia + k, NA)
-            push(src_of(peer), dst, g, (peer, iw))
+    near = lax.rem(iw, 2) * 4 + lax.rem(ia, 4)
+    far = ia // 4 * 4 + iw // 2
+
+    def near_device(peer):
+        return ia // 4 * 4 + lax.rem(peer, 4), iw // 2 * 2 + peer // 4
+
+    def far_device(peer):
+        return peer // 4 * 4 + lax.rem(ia, 4), lax.rem(peer, 4) * 2 + lax.rem(iw, 2)
+
+    near_peers = [lax.rem(near + k, NEAR) for k in range(1, NEAR)]
+    far_peers = [lax.rem(far + k, FAR) for k in range(1, FAR)]
+    twin = near + 1 - 2 * lax.rem(near, 2)
+
+    def over_near(src_of, dst, g):
+        for peer in near_peers:
+            push(src_of(peer), dst, g, near_device(peer))
+
+    def over_far(src_of, dst, g):
+        for peer in far_peers:
+            push(src_of(peer), dst, g, far_device(peer))
+
+    def over_y(src_of, dst, g):
+        for k in range(1, 4):
+            peer = lax.rem(near + 2 * k, NEAR)
+            push(src_of(peer // 2), dst, g, near_device(peer))
 
     def arrived(ref, g):
         pltpu.make_async_copy(ref, ref, rsem.at[g]).wait()
@@ -124,16 +142,19 @@
     def gone(ref, g):
         pltpu.make_async_copy(ref, ref, ssem.at[g]).wait()
 
-    def from_w(ref, g):
-        arrived(ref.at[pl.ds(0, NW - 1)], g)
-
-    def from_a(ref, g):
-        arrived(ref.at[pl.ds(0, NA - 1)], g)
+    def from_near(ref, g):
+        arrived(ref.at[pl.ds(0, NEAR - 1)], g)
+
+    def from_far(ref, g):
+        arrived(ref.at[pl.ds(0, FAR - 1)], g)
+
+    mine = lax.rem(near, 2) * 512
+    level = near // 2
 
     barrier = pltpu.get_barrier_semaphore()
-    peers = [(ia, lax.rem(iw + k, NW)) for k in range(1, NW)]
-    peers += [(lax.rem(ia + k, NA), iw) for k in range(1, NA)]
-    peers += [(a, b) for a in (up, down) for b in (left, right)]
+    peers = [near_device(peer) for peer in near_peers]
+    peers += [far_device(peer) for peer in far_peers]
+    peers += [(a, b) for a in (up, ia, down) for b in (left, right)] + [(up, iw), (down, iw)]
     for peer in peers:
         pl.semaphore_signal(barrier, inc=1, device_id=peer, device_id_type=MESH)
 
@@ -205,11 +226,11 @@
         return now + y[2 * CH :], (y[0:CH], later + y[CH : 2 * CH])
 
     def step_a(a, a_in, g):
-        over_w(lambda peer: a.at[peer], a_in.at[iw], g)
-        a_in[iw] = a[iw]
+        over_near(lambda peer: a.at[peer], a_in.at[near], g)
+        a_in[near] = a[near]
 
     def step_b(a_in, x, b, b_in, g_a, g_b):
-        from_w(a_in, g_a)
+        from_near(a_in, g_a)
 
         def widen(j, carry):
             for t in range(2):
@@ -217,7 +238,7 @@
                     x[pl.ds((r * 16 + j * 2 + t) * HC, HC), :] = a_in[j, t, r].astype(F32)
             return carry
 
-        loop(NW, widen, unroll=8)
+        loop(NEAR, widen, unroll=8)
 
         def pick(q, carry):
             for r in range(2):
@@ -226,16 +247,16 @@
             return carry
 
         loop(8, pick, unroll=8)
-        over_a(lambda peer: b.at[peer], b_in.at[ia], g_b)
-        b_in[ia] = b[ia]
+        over_far(lambda peer: b.at[peer], b_in.at[far], g_b)
+        b_in[far] = b[far]
 
     def step_c(mixed, c, c_in, g):
-        c[...] = mixed.astype(BF).reshape(NA, 16, 512)
-        over_a(lambda peer: c.at[peer], c_in.at[ia], g)
-        c_in[ia] = c[ia]
+        c[...] = mixed.astype(BF).reshape(FAR, 16, 512)
+        over_far(lambda peer: c.at[peer], c_in.at[far], g)
+        c_in[far] = c[far]
 
     def step_d(c_in, x, d, d_in, g_c, g_d):
-        from_a(c_in, g_c)
+        from_far(c_in, g_c)
 
         def unpick(q, carry):
             for r in range(2):
@@ -251,9 +272,9 @@
                     d[j, t, r] = x[pl.ds(r * HC * 16 + j * 2 + t, HC, stride=16), :].astype(BF)
             return carry
 
-        loop(NW, narrow, unroll=8)
-        over_w(lambda peer: d.at[peer], d_in.at[iw], g_d)
-        d_in[iw] = d[iw]
+        loop(NEAR, narrow, unroll=8)
+        over_near(lambda peer: d.at[peer], d_in.at[near], g_d)
+        d_in[near] = d[near]
 
     loads[0].wait()
     loads[1].wait()
@@ -281,6 +302,17 @@
     pl.semaphore_wait(barrier, len(peers))
     step_a(va, va_in, G_VA)
 
+    def order():
+        row = lax.broadcasted_iota(jnp.int32, (COLS, COLS), 0)
+        cell = lax.broadcasted_iota(jnp.int32, (COLS, COLS), 1)
+        found = (row & 0xC1) | ((row & 6) << 3) | ((row & 48) >> 2) | ((row & 8) >> 2)
+        return jnp.where(cell == found, 1.0, 0.0).astype(BF)
+
+    def mix_in_order():
+        swap = order()
+        return dot_nt(dot(swap, grid_mix[...]).astype(BF), swap).astype(BF)
+
+
     loads[2].wait()
     turn_in(cot)
 
@@ -306,11 +338,12 @@
         return carry
 
     loop(ROWS, gate_row, unroll=8)
-    step_b(va_in, vx, vb, vb_in, G_VA, G_VB)
-
-    take_halo(u3, 0, G_ROW0, G_PACK0)
     for load in loads[3:]:
         load.wait()
+    mixp[...] = mix_in_order()
+    step_b(va_in, vx, vb, vb_in, G_VA, G_VB)
+
+    take_halo(u3, 0, G_ROW0, G_PACK0)
     back_w = jnp.concatenate(
         [jnp.concatenate([conv_w[2 - a, 2 - b] for a in range(3)], axis=1) for b in range(3)], axis=0
     ).astype(F32).T.astype(BF)
@@ -331,9 +364,8 @@
     loop(ROWS, back_row, conv_start(back_w, u3), unroll=8)
     step_a(ga, ga_in, G_GA)
 
-    mix = grid_mix[...]
-    from_a(vb_in, G_VB)
-    step_c(dot(mix, vb_in[...].reshape(256, 512)), vc, vc_in, G_VC)
+    from_far(vb_in, G_VB)
+    step_c(dot(mixp[...], vb_in[...].reshape(256, 512)), vc, vc_in, G_VC)
 
     def put(ref):
         def store(k, t, value):
@@ -357,18 +389,18 @@
     se[2 * COLS : 3 * COLS] = part_block[:, half(0)]
     se[3 * COLS :] = part_block[:, half(1)]
 
-    from_a(gb_in, G_GB)
+    from_far(gb_in, G_GB)
     back = gb_in[...].reshape(256, 512)
-    step_c(dot_tn(mix, back), gc, gc_in, G_GC)
+    step_c(dot_tn(mixp[...], back), gc, gc_in, G_GC)
     part_grid = dot_nt(back, vb_in[...].reshape(256, 512)).astype(BF)
+    part_grid = dot(dot_tn(order(), part_grid).astype(BF), order()).astype(BF)
     se[0:COLS] = part_grid[:, half(0)]
     se[COLS : 2 * COLS] = part_grid[:, half(1)]
-    over_w(lambda peer: se.at[pl.ds(pl.multiple_of(peer * 128, 128), 128)], re1.at[iw], G_E1)
-    re1[iw] = se[pl.ds(pl.multiple_of(iw * 128, 128), 128)]
+    push(se.at[pl.ds(pl.multiple_of(512 - mine, 512), 512)], re0, G_E0, near_device(twin))
 
     for k in (0, 1, ROWS + 2, ROWS + 3):
         jp[k] = jnp.zeros((CH, COLS), BF)
-    from_w(vd_in, G_VD)
+    from_near(vd_in, G_VD)
 
     def returned(ref, r):
         return [ref[r // 2, t, lax.rem(r, 2)].astype(F32) for t in range(2)]
@@ -388,30 +420,35 @@
     pack = loop(ROWS, joined_row, jnp.zeros((CH, LANES), F32), unroll=8)
     send_halo(v3, pack, 1, G_ROW1, G_PACK1)
 
+    arrived(re0, G_E0)
+    e0[...] = (se[pl.ds(pl.multiple_of(mine, 512), 512)].astype(F32) + re0[...].astype(F32)).astype(BF)
+    over_y(lambda peer: e0.at[pl.ds(pl.multiple_of(peer * 128, 128), 128)], re1.at[level], G_E1)
+    re1[level] = e0[pl.ds(pl.multiple_of(level * 128, 128), 128)]
+
     step_d(gc_in, gx, gd, gd_in, G_GC, G_GD)
 
-    from_w(re1, G_E1)
+    arrived(re1.at[pl.ds(0, 3)], G_E1)
     total = re1[0].astype(F32)
-    for k in range(1, NW):
+    for k in range(1, 4):
         total = total + re1[k].astype(F32)
     e1[...] = total
-    over_a(lambda peer: e1.at[pl.ds(pl.multiple_of(peer * 8, 8), 8)], re2.at[ia], G_E2)
-    re2[ia] = e1[pl.ds(pl.multiple_of(ia * 8, 8), 8)]
+    over_far(lambda peer: e1.at[pl.ds(pl.multiple_of(peer * 8, 8), 8)], re2.at[far], G_E2)
+    re2[far] = e1[pl.ds(pl.multiple_of(far * 8, 8), 8)]
 
     def conv_row(p, total):
         return total + dot_nt(u3[p], jp[pl.ds(p, 3)].reshape(3 * CH, COLS))
 
     p_conv = loop(ROWS + 2, conv_row, jnp.zeros((3 * CH, 3 * CH), F32), unroll=9)
 
-    from_a(re2, G_E2)
+    from_far(re2, G_E2)
     total = re2[0]
     for k in range(1, NA):
         total = total + re2[k]
     e2[...] = total
-    over_a(lambda peer: e2, re3.at[ia], G_E3)
-    re3[ia] = e2[...]
-
-    from_w(gd_in, G_GD)
+    over_far(lambda peer: e2, re3.at[far], G_E3)
+    re3[far] = e2[...]
+
+    from_near(gd_in, G_GD)
 
     def before_row(r, carry):
         p_in, p_out = carry
@@ -435,13 +472,13 @@
     st[4 * CH :] = jnp.concatenate(
         [third[: 2 * CH], jnp.concatenate([third[2 * CH :], p_out], axis=0)], axis=1
     ).astype(BF)
-    over_w(lambda peer: st.at[pl.ds(pl.multiple_of(peer * 48, 16), 48)], rt1.at[iw], G_T1)
-    rt1[iw] = st[pl.ds(pl.multiple_of(iw * 48, 16), 48)]
-
-    from_a(re3, G_E3)
+    over_near(lambda peer: st.at[pl.ds(pl.multiple_of(peer * 48, 16), 48)], rt1.at[near], G_T1)
+    rt1[near] = st[pl.ds(pl.multiple_of(near * 48, 16), 48)]
+
+    from_far(re3, G_E3)
     e4[...] = re3[...].reshape(128, LANES).astype(BF)
-    over_w(lambda peer: e4, re4.at[iw], G_E4)
-    re4[iw] = e4[...]
+    over_y(lambda peer: e4, re4.at[level], G_E4)
+    re4[level] = e4[...]
 
     def frame_row(r, carry):
         normed = dot(w_in_t[...], gbef[r])
@@ -455,22 +492,26 @@
 
     loop(ROWS, frame_row, unroll=8)
 
-    from_w(rt1, G_T1)
+    from_near(rt1, G_T1)
     total = rt1[0].astype(F32)
     for k in range(1, NW):
         total = total + rt1[k].astype(F32)
     t1[...] = total.astype(BF)
-    over_a(lambda peer: t1, rt2.at[ia], G_T2)
-    rt2[ia] = t1[...]
+    over_far(lambda peer: t1, rt2.at[far], G_T2)
+    rt2[far] = t1[...]
+
+    arrived(re4.at[pl.ds(0, 3)], G_E4)
+    push(re4, e5, G_E5, near_device(twin))
+    early_out[pl.ds(pl.multiple_of(mine, 512), 512)] = re4[...].reshape(512, LANES)
 
     take_halo(v3, 1, G_ROW1, G_PACK1)
-    from_a(rt2, G_T2)
+    from_far(rt2, G_T2)
     total = rt2[0].astype(F32)
     for k in range(1, NA):
         total = total + rt2[k].astype(F32)
     t2[...] = total.astype(BF)
-    over_w(lambda peer: t2, rt3.at[iw], G_T3)
-    rt3[iw] = t2[...]
+    over_near(lambda peer: t2, rt3.at[near], G_T3)
+    rt3[near] = t2[...]
 
     conv_k = jnp.concatenate(
         [jnp.concatenate([conv_w[a, b] for b in range(3)], axis=1) for a in range(3)], axis=0
@@ -485,9 +526,9 @@
 
     loop(ROWS, out_row, conv_start(conv_k, v3), unroll=8)
 
-    from_w(re4, G_E4)
-    early_out[...] = re4[...]
-    from_w(rt3, G_T3)
+    arrived(e5, G_E5)
+    early_out[pl.ds(pl.multiple_of(512 - mine, 512), 512)] = e5[...].reshape(512, LANES)
+    from_near(rt3, G_T3)
     tail_out[...] = rt3[...]
 
     for which, g_row, g_pack in ((0, G_ROW0, G_PACK0), (1, G_ROW1, G_PACK1)):
@@ -495,13 +536,17 @@
         gone(pack_in.at[which], g_pack)
     for ref, g in (
         (va_in, G_VA), (vd_in, G_VD), (ga_in, G_GA), (gd_in, G_GD),
-        (re1, G_E1), (re4, G_E4), (rt1, G_T1), (rt3, G_T3),
+        (rt1, G_T1), (rt3, G_T3),
     ):
-        gone(ref.at[pl.ds(0, NW - 1)], g)
+        gone(ref.at[pl.ds(0, NEAR - 1)], g)
     for ref, g in (
         (vb_in, G_VB), (vc_in, G_VC), (gb_in, G_GB), (gc_in, G_GC), (re2, G_E2), (re3, G_E3), (rt2, G_T2),
     ):
-        gone(ref.at[pl.ds(0, NA - 1)], g)
+        gone(ref.at[pl.ds(0, FAR - 1)], g)
+    gone(re0, G_E0)
+    gone(re1.at[pl.ds(0, 3)], G_E1)
+    gone(re4.at[pl.ds(0, 3)], G_E4)
+    gone(e5, G_E5)
 
 
 def finish(rest, gframe, early, tail, restored, grad_frames, grad_w_in_t, grad_grid, grad_block, grad_w_out, grad_conv):
@@ -577,14 +622,18 @@
     vm(2, 6, CH, LANES),
     vm(CH, LANES, dtype=F32),
     vm(CH, LANES, dtype=F32),
+    vm(COLS, COLS),
     vm(4 * COLS, LANES),
-    vm(NW, 128, LANES),
+    vm(512, LANES),
+    vm(512, LANES),
+    vm(4, 128, LANES),
     vm(128, LANES, dtype=F32),
     vm(NA, 8, LANES, dtype=F32),
     vm(8, LANES, dtype=F32),
     vm(NA, 8, LANES, dtype=F32),
     vm(128, LANES),
-    vm(NW, 128, LANES),
+    vm(4, 128, LANES),
+    vm(4, 128, LANES),
     vm(6 * CH, LANES),
     vm(NW, 48, LANES),
     vm(48, LANES),
@@ -606,7 +655,7 @@
         out_shape=(
             shape((2, ROWS * CH, LANES), F32),
             shape((2, ROWS * CH, LANES), F32),
-            shape((NW, 128, LANES), BF),
+            shape((4 * COLS, LANES), BF),
             shape((NW, 48, LANES), BF),
         ),
         in_specs=[pl.BlockSpec(memory_space=pltpu.HBM)] * 7,
@@ -630,7 +679,7 @@
         in_specs=[vmem] * 4,
         out_specs=(vmem,) * 7,
         compiler_params=pltpu.CompilerParams(vmem_limit_bytes=16 * 1024 * 1024),
-    )(rest, gframe, early.reshape(4 * COLS, LANES), tail.reshape(6 * CH, LANES))
+    )(rest, gframe, early, tail.reshape(6 * CH, LANES))
     return restored, grad_frames, grad_w_in_t.T, grad_grid, grad_block, grad_w_out, grad_conv
 
 

time: 67.8 us -> 63.7 us (0.940)
  Pallas kernels: 67 us -> 62.9 us
    pallas_call x1, Pallas kernels: 64.4 us -> 60.3 us  [body(): pl.pallas_call(kernel, out_shape=(shape((2, ROWS * CH, LANES), F32), shap...]
where the time goes in v4:
time: 63.7 us; the launch traced here: 63.6 us
  Pallas kernels  62.9 us (99%)
  between operations  0.64 us (1%)
    pallas_call x1, Pallas kernels, body(): pl.pallas_call(kernel, out_shape=(shape((2, ROWS * CH, LANES), F32), shap...  60.3 us
    pallas_call x1, Pallas kernels, body(): pl.pallas_call(finish, out_shape=(shape((CH, ROWS, COLS), BF), shape((CH,...  2.63 us

profile of v4, /device:TPU:1, one launch (start us, length us, event | category | flops | bytes accessed | tf_op | source)
XLA Modules:
  0.0 63.6 jit_solution(16777794541622233765)
XLA Ops:
  0.6 60.3 %shard_map.126 = (f32[2,1024,128]{2,1,0:T(8,128)S(1)}, f32[2,1024,128]{2,1,0:T(8,128)S(1)}, bf16[1024,128]{1,0:T(8,128)(2,1)S(1)}, bf16[8,48,128]{2,1,0:T(8,128)(2,1)S(1)}) custom-call(bf16[64,16,256]{2,1,0:T(8,128)(2,1)} %frames_hbm.1, bf16[64,128]{1,0:T(8,128)(2,1)} %bitcast.4, bf16[256,256]{1,0:T(8,128)(2,1)} %grid_mix_hbm.1, ...), custom_call_target="tpu_custom_call" | custom-call | tf_op jit(solution)/shard_map/pallas_call | solution.py:653
  60.9 2.6 %shard_map.127 = (bf16[64,16,256]{2,1,0:T(8,128)(2,1)}, bf16[64,16,256]{2,1,0:T(8,128)(2,1)}, f32[64,128]{1,0:T(8,128)}, f32[256,256]{1,0:T(8,128)}, f32[256,256...) custom-call(f32[2,1024,128]{2,1,0:T(8,128)S(1)} %get-tuple-element.18.rest, ...), custom_call_target="tpu_custom_call" | custom-call | tf_op jit(solution)/shard_map/pallas_call | solution.py:668

commit v5 on v4

--- a/solution.py
+++ b/solution.py
@@ -21,8 +21,8 @@
 FAR = 16
 
 (G_ROW0, G_PACK0, G_ROW1, G_PACK1, G_VA, G_VB, G_VC, G_VD, G_GA, G_GB, G_GC, G_GD) = range(12)
-(G_E0, G_E1, G_E2, G_E3, G_E4, G_E5, G_T1, G_T2, G_T3) = range(12, 21)
-GROUPS = 21
+(G_E0, G_E1, G_E2, G_E3, G_E4, G_E5, G_E6, G_T1, G_T2, G_T3) = range(12, 22)
+GROUPS = 22
 
 
 def dot(a, b):
@@ -38,7 +38,7 @@
 
 
 def swap_granules(load, store, depth):
-    lane = lax.broadcasted_iota(jnp.int32, (depth, LANES), 1)
+    lane = lax.broadcasted_iota(jnp.int16, (depth, LANES), 1)
     for row_half in range(2):
         for col_half in range(2):
             held = [load(row_half * 8 + k, col_half) for k in range(8)]
@@ -79,14 +79,15 @@
     va, va_in, vx, vb, vb_in, vc, vc_in, vd, vd_in,
     ga, ga_in, gx, gb, gb_in, gc, gc_in, gd, gd_in,
     gated, gbef, jp, row_in, pack_out, pack_in, edge_l, edge_r,
-    mixp, se, re0, e0, re1, e1, re2, e2, re3, e4, re4, e5, st, rt1, t1, rt2, t2, rt3,
+    mixp, se, re0, e0, re1, e1, re2, e2, re3, e3, re4, re5, re6, st, rt1, t1, rt2, t2, rt3,
     ssem, rsem, isem,
 ):
     ia = lax.axis_index("ha")
     iw = lax.axis_index("wa")
     up, down = lax.rem(ia + NA - 1, NA), lax.rem(ia + 1, NA)
     left, right = lax.rem(iw + NW - 1, NW), lax.rem(iw + 1, NW)
-    lane = lax.broadcasted_iota(jnp.int32, (CH, LANES), 1)
+    lane = lax.broadcasted_iota(jnp.int16, (CH, LANES), 1)
+    lane_wide = lax.broadcasted_iota(jnp.int32, (CH, LANES), 1)
 
     loads = [
         pltpu.make_async_copy(src, dst, isem.at[k])
@@ -131,6 +132,16 @@
         for peer in far_peers:
             push(src_of(peer), dst, g, far_device(peer))
 
+    def over_x(src_of, dst, g):
+        for k in range(1, 4):
+            peer = lax.rem(iw // 2 + k, 4)
+            push(src_of(peer), dst, g, (ia, peer * 2 + lax.rem(iw, 2)))
+
+    def over_z(src_of, dst, g):
+        for k in range(1, 4):
+            peer = lax.rem(ia // 4 + k, 4)
+            push(src_of(peer), dst, g, (peer * 4 + lax.rem(ia, 4), iw))
+
     def over_y(src_of, dst, g):
         for k in range(1, 4):
             peer = lax.rem(near + 2 * k, NEAR)
@@ -149,7 +160,7 @@
         arrived(ref.at[pl.ds(0, FAR - 1)], g)
 
     mine = lax.rem(near, 2) * 512
-    level = near // 2
+    level, across, deep = near // 2, iw // 2, ia // 4
 
     barrier = pltpu.get_barrier_semaphore()
     peers = [near_device(peer) for peer in near_peers]
@@ -166,11 +177,11 @@
         return turn[t, pl.ds(r, CH, stride=ROWS), :]
 
     def edges(pack, t0, t1, r):
-        pack = jnp.where(lane == r, pltpu.roll(t0, r, 1), pack)
-        return jnp.where(lane == ROWS + r, pltpu.roll(t1, r + 17, 1), pack)
+        pack = jnp.where(lane_wide == r, pltpu.roll(t0, r, 1), pack)
+        return jnp.where(lane_wide == ROWS + r, pltpu.roll(t1, r + 17, 1), pack)
 
     def send_halo(field, pack, which, g_row, g_pack):
-        pack_out[which] = pack.astype(BF)
+        pack_out[which] = pack
         push(field.at[1, CH : 2 * CH], row_in.at[which, 1], g_row, (up, iw))
         push(field.at[ROWS, CH : 2 * CH], row_in.at[which, 0], g_row, (down, iw))
         for slot, where in enumerate(
@@ -181,17 +192,16 @@
     def take_halo(field, which, g_row, g_pack):
         arrived(row_in.at[which], g_row)
         arrived(pack_in.at[which], g_pack)
-        top = row_in[which, 0].astype(F32) * jnp.where(ia > 0, 1.0, 0.0)
-        field[0, CH : 2 * CH] = top.astype(BF)
-        bottom = row_in[which, 1].astype(F32) * jnp.where(ia < NA - 1, 1.0, 0.0)
-        field[ROWS + 1, CH : 2 * CH] = bottom.astype(BF)
+        field[0, CH : 2 * CH] = jnp.where(ia > 0, row_in[which, 0], jnp.zeros((CH, COLS), BF))
+        field[ROWS + 1, CH : 2 * CH] = jnp.where(ia < NA - 1, row_in[which, 1], jnp.zeros((CH, COLS), BF))
         first = jnp.where(ia > 0, 0, 1)
         last = jnp.where(ia < NA - 1, ROWS + 2, ROWS + 1)
-        got = [pack_in[which, k].astype(F32) for k in range(6)]
+        got = [pack_in[which, k] for k in range(6)]
 
         def assemble(middle, above, below, has):
             joined = jnp.where(lane == 0, above, jnp.where(lane == ROWS + 1, below, middle))
-            return jnp.where((lane >= first) & (lane < jnp.where(has, last, 0)), joined, 0.0)
+            inside = (lane_wide >= first) & (lane_wide < jnp.where(has, last, 0))
+            return jnp.where(inside, joined, jnp.zeros_like(joined))
 
         edge_l[...] = assemble(
             pltpu.roll(got[0], 113, 1), pltpu.roll(got[2], 97, 1), pltpu.roll(got[4], 1, 1), iw > 0
@@ -201,16 +211,16 @@
         )
 
         def shifts(p, carry):
-            t0 = field[p, CH : 2 * CH, half(0)].astype(F32)
-            t1 = field[p, CH : 2 * CH, half(1)].astype(F32)
+            t0 = field[p, CH : 2 * CH, half(0)]
+            t1 = field[p, CH : 2 * CH, half(1)]
             a0, a1 = pltpu.roll(t0, 1, 1), pltpu.roll(t1, 1, 1)
             b0, b1 = pltpu.roll(t0, LANES - 1, 1), pltpu.roll(t1, LANES - 1, 1)
             lh = pltpu.roll(edge_l[...], lax.rem(LANES - p, LANES), 1)
             rh = pltpu.roll(edge_r[...], LANES - 1 - p, 1)
-            field[p, 0:CH, half(0)] = jnp.where(lane == 0, lh, a0).astype(BF)
-            field[p, 0:CH, half(1)] = jnp.where(lane == 0, a0, a1).astype(BF)
-            field[p, 2 * CH :, half(0)] = jnp.where(lane == LANES - 1, b1, b0).astype(BF)
-            field[p, 2 * CH :, half(1)] = jnp.where(lane == LANES - 1, rh, b1).astype(BF)
+            field[p, 0:CH, half(0)] = jnp.where(lane == 0, lh, a0)
+            field[p, 0:CH, half(1)] = jnp.where(lane == 0, a0, a1)
+            field[p, 2 * CH :, half(0)] = jnp.where(lane == LANES - 1, b1, b0)
+            field[p, 2 * CH :, half(1)] = jnp.where(lane == LANES - 1, rh, b1)
             return carry
 
         loop(ROWS + 2, shifts, unroll=9)
@@ -224,10 +234,6 @@
         later, now = carry
         y = dot(w, field[r + 2])
         return now + y[2 * CH :], (y[0:CH], later + y[CH : 2 * CH])
-
-    def step_a(a, a_in, g):
-        over_near(lambda peer: a.at[peer], a_in.at[near], g)
-        a_in[near] = a[near]
 
     def step_b(a_in, x, b, b_in, g_a, g_b):
         from_near(a_in, g_a)
@@ -240,15 +246,13 @@
 
         loop(NEAR, widen, unroll=8)
 
-        def pick(q, carry):
-            for r in range(2):
-                for c in range(4):
-                    b[r * 8 + q, :, half(c)] = x[pl.ds(r * 16 * HC + q * 4 + c, 16, stride=HC), :].astype(BF)
-            return carry
-
-        loop(8, pick, unroll=8)
-        over_far(lambda peer: b.at[peer], b_in.at[far], g_b)
-        b_in[far] = b[far]
+        for peer in [*far_peers, far]:
+            base = peer // 8 * (16 * HC) + lax.rem(peer, 8) * 4
+            slot = b_in if peer is far else b
+            for c in range(4):
+                slot[peer, :, half(c)] = x[pl.ds(base + c, 16, stride=HC), :].astype(BF)
+            if peer is not far:
+                push(b.at[peer], b_in.at[far], g_b, far_device(peer))
 
     def step_c(mixed, c, c_in, g):
         c[...] = mixed.astype(BF).reshape(FAR, 16, 512)
@@ -266,22 +270,21 @@
 
         loop(8, unpick, unroll=8)
 
-        def narrow(j, carry):
+        for peer in [*near_peers, near]:
+            slot = d_in if peer is near else d
             for t in range(2):
                 for r in range(2):
-                    d[j, t, r] = x[pl.ds(r * HC * 16 + j * 2 + t, HC, stride=16), :].astype(BF)
-            return carry
-
-        loop(NEAR, narrow, unroll=8)
-        over_near(lambda peer: d.at[peer], d_in.at[near], g_d)
-        d_in[near] = d[near]
+                    slot[peer, t, r] = x[pl.ds(r * HC * 16 + peer * 2 + t, HC, stride=16), :].astype(BF)
+            if peer is not near:
+                push(d.at[peer], d_in.at[near], g_d, near_device(peer))
 
     loads[0].wait()
     loads[1].wait()
     turn_in(frames)
     w_in[...] = w_in_t[...].astype(F32).T.astype(BF)
 
-    def value_row(r, carry):
+    def value_row(slot, peer, low):
+        r = peer * 2 + low
         for t in range(2):
             x = turned(r, t)
             xb[r, :, half(t)] = x.astype(BF)
@@ -294,13 +297,19 @@
         value, slope = gelu_parts(dot(w_in[HC:CH], nb[r]))
         dgelu[r, HC:CH] = slope
         value = value.astype(BF)
-        va[r // 2, 0, lax.rem(r, 2)] = value[:, half(0)]
-        va[r // 2, 1, lax.rem(r, 2)] = value[:, half(1)]
-        return carry
-
-    loop(ROWS, value_row, unroll=8)
-    pl.semaphore_wait(barrier, len(peers))
-    step_a(va, va_in, G_VA)
+        slot[peer, 0, low] = value[:, half(0)]
+        slot[peer, 1, low] = value[:, half(1)]
+
+    for first in range(0, NEAR, 2):
+        group = [*near_peers, near][first : first + 2]
+        for peer in group:
+            for low in range(2):
+                value_row(va_in if peer is near else va, peer, low)
+        if first == 0:
+            pl.semaphore_wait(barrier, len(peers))
+        for peer in group:
+            if peer is not near:
+                push(va.at[peer], va_in.at[near], G_VA, near_device(peer))
 
     def order():
         row = lax.broadcasted_iota(jnp.int32, (COLS, COLS), 0)
@@ -317,12 +326,12 @@
     turn_in(cot)
 
     def cot_row(r, pack):
-        t0, t1 = turned(r, 0), turned(r, 1)
-        u3[r + 1, CH : 2 * CH, half(0)] = t0.astype(BF)
-        u3[r + 1, CH : 2 * CH, half(1)] = t1.astype(BF)
+        t0, t1 = turned(r, 0).astype(BF), turned(r, 1).astype(BF)
+        u3[r + 1, CH : 2 * CH, half(0)] = t0
+        u3[r + 1, CH : 2 * CH, half(1)] = t1
         return edges(pack, t0, t1, r)
 
-    pack = loop(ROWS, cot_row, jnp.zeros((CH, LANES), F32), unroll=8)
+    pack = loop(ROWS, cot_row, jnp.zeros((CH, LANES), BF), unroll=8)
     send_halo(u3, pack, 0, G_ROW0, G_PACK0)
 
     def gate_row(r, carry):
@@ -356,34 +365,43 @@
         up_gated = dot(w_out_t, g)
         gg[r] = up_gated
         mixed = (up_gated * gates[r].astype(F32)).astype(BF)
-        ga[r // 2, 0, lax.rem(r, 2)] = mixed[0:HC, half(0)]
-        ga[r // 2, 1, lax.rem(r, 2)] = mixed[0:HC, half(1)]
+        ga[r // 2, 0, r % 2] = mixed[0:HC, half(0)]
+        ga[r // 2, 1, r % 2] = mixed[0:HC, half(1)]
         bback[r] = mixed[HC:]
         return carry
 
-    loop(ROWS, back_row, conv_start(back_w, u3), unroll=8)
-    step_a(ga, ga_in, G_GA)
+    carry = conv_start(back_w, u3)
+    for first in range(0, NEAR, 2):
+        for r in range(2 * first, 2 * first + 4):
+            carry = back_row(r, carry)
+        for peer in (first, first + 1):
+
+            @pl.when(peer != near)
+            def _():
+                push(ga.at[peer], ga_in.at[near], G_GA, near_device(peer))
+
+    ga_in[near] = ga[near]
 
     from_far(vb_in, G_VB)
     step_c(dot(mixp[...], vb_in[...].reshape(256, 512)), vc, vc_in, G_VC)
 
     def put(ref):
         def store(k, t, value):
-            ref[k, :, half(t)] = value.astype(ref.dtype)
+            ref[k, :, half(t)] = value
 
         return store
 
-    swap_granules(lambda k, t: bval[k, :, half(t)].astype(F32), put(xt), HC)
+    swap_granules(lambda k, t: bval[k, :, half(t)], put(xt), HC)
     values = xt[...].reshape(ROWS * HC, COLS)
-    mixed = dot_nt(values, block_mix[...])
+    mixed = dot_nt(values, block_mix[...]).astype(BF)
     swap_granules(lambda k, t: mixed[k * HC : (k + 1) * HC, half(t)], put(bm), HC)
 
     step_b(ga_in, gx, gb, gb_in, G_GA, G_GB)
     step_d(vc_in, vx, vd, vd_in, G_VC, G_VD)
 
-    swap_granules(lambda k, t: bback[k, :, half(t)].astype(F32), put(bt), HC)
+    swap_granules(lambda k, t: bback[k, :, half(t)], put(bt), HC)
     backs = bt[...].reshape(ROWS * HC, COLS)
-    unmixed = dot(backs, block_mix[...])
+    unmixed = dot(backs, block_mix[...]).astype(BF)
     swap_granules(lambda k, t: unmixed[k * HC : (k + 1) * HC, half(t)], put(gbv), HC)
     part_block = dot_tn(backs, values).astype(BF)
     se[2 * COLS : 3 * COLS] = part_block[:, half(0)]
@@ -410,14 +428,13 @@
         for t in range(2):
             gates_t = gates[r, :, half(t)].astype(F32)
             gated[r, 0:HC, half(t)] = (gates_t[0:HC] * (grid_mixed[t] + 1.0)).astype(BF)
-            gated[r, HC:, half(t)] = (gates_t[HC:] * (bm[r, :, half(t)] + 1.0)).astype(BF)
+            gated[r, HC:, half(t)] = (gates_t[HC:] * (bm[r, :, half(t)].astype(F32) + 1.0)).astype(BF)
         j = (xb[r].astype(F32) + dot(w_out[...], gated[r])).astype(BF)
         jp[r + 2] = j
         v3[r + 1, CH : 2 * CH] = j
-        jf = j.astype(F32)
-        return edges(pack, jf[:, half(0)], jf[:, half(1)], r)
-
-    pack = loop(ROWS, joined_row, jnp.zeros((CH, LANES), F32), unroll=8)
+        return edges(pack, j[:, half(0)], j[:, half(1)], r)
+
+    pack = loop(ROWS, joined_row, jnp.zeros((CH, LANES), BF), unroll=8)
     send_halo(v3, pack, 1, G_ROW1, G_PACK1)
 
     arrived(re0, G_E0)
@@ -432,21 +449,18 @@
     for k in range(1, 4):
         total = total + re1[k].astype(F32)
     e1[...] = total
-    over_far(lambda peer: e1.at[pl.ds(pl.multiple_of(peer * 8, 8), 8)], re2.at[far], G_E2)
-    re2[far] = e1[pl.ds(pl.multiple_of(far * 8, 8), 8)]
+    over_x(lambda peer: e1.at[pl.ds(pl.multiple_of(peer * 32, 32), 32)], re2.at[across], G_E2)
+    re2[across] = e1[pl.ds(pl.multiple_of(across * 32, 32), 32)]
 
     def conv_row(p, total):
         return total + dot_nt(u3[p], jp[pl.ds(p, 3)].reshape(3 * CH, COLS))
 
     p_conv = loop(ROWS + 2, conv_row, jnp.zeros((3 * CH, 3 * CH), F32), unroll=9)
 
-    from_far(re2, G_E2)
-    total = re2[0]
-    for k in range(1, NA):
-        total = total + re2[k]
-    e2[...] = total
-    over_far(lambda peer: e2, re3.at[far], G_E3)
-    re3[far] = e2[...]
+    arrived(re2.at[pl.ds(0, 3)], G_E2)
+    e2[...] = re2[0] + re2[1] + re2[2] + re2[3]
+    over_z(lambda peer: e2, re3.at[deep], G_E3)
+    re3[deep] = e2[...]
 
     from_near(gd_in, G_GD)
 
@@ -459,8 +473,8 @@
             d = dgelu[r, :, half(t)]
             gbef[r, 0:HC, half(t)] = (d[0:HC] * (g[0:HC] * (grid_mixed[t] + 1.0))).astype(BF)
             gbef[r, HC:CH, half(t)] = (d[HC:CH] * grid_back[t]).astype(BF)
-            gbef[r, CH : CH + HC, half(t)] = (d[CH : CH + HC] * (g[HC:] * (bm[r, :, half(t)] + 1.0))).astype(BF)
-            gbef[r, CH + HC :, half(t)] = (d[CH + HC :] * gbv[r, :, half(t)]).astype(BF)
+            gbef[r, CH : CH + HC, half(t)] = (d[CH : CH + HC] * (g[HC:] * (bm[r, :, half(t)].astype(F32) + 1.0))).astype(BF)
+            gbef[r, CH + HC :, half(t)] = (d[CH + HC :] * gbv[r, :, half(t)].astype(F32)).astype(BF)
         return p_in + dot_nt(nb[r], gbef[r]), p_out + dot_nt(gj[r], gated[r])
 
     p_in, p_out = loop(
@@ -475,10 +489,10 @@
     over_near(lambda peer: st.at[pl.ds(pl.multiple_of(peer * 48, 16), 48)], rt1.at[near], G_T1)
     rt1[near] = st[pl.ds(pl.multiple_of(near * 48, 16), 48)]
 
-    from_far(re3, G_E3)
-    e4[...] = re3[...].reshape(128, LANES).astype(BF)
-    over_y(lambda peer: e4, re4.at[level], G_E4)
-    re4[level] = e4[...]
+    arrived(re3.at[pl.ds(0, 3)], G_E3)
+    e3[...] = (re3[0] + re3[1] + re3[2] + re3[3]).astype(BF)
+    over_x(lambda peer: e3, re4.at[across], G_E4)
+    re4[across] = e3[...]
 
     def frame_row(r, carry):
         normed = dot(w_in_t[...], gbef[r])
@@ -501,8 +515,8 @@
     rt2[far] = t1[...]
 
     arrived(re4.at[pl.ds(0, 3)], G_E4)
-    push(re4, e5, G_E5, near_device(twin))
-    early_out[pl.ds(pl.multiple_of(mine, 512), 512)] = re4[...].reshape(512, LANES)
+    over_y(lambda peer: re4, re5.at[level], G_E5)
+    re5[level] = re4[...]
 
     take_halo(v3, 1, G_ROW1, G_PACK1)
     from_far(rt2, G_T2)
@@ -513,6 +527,10 @@
     over_near(lambda peer: t2, rt3.at[near], G_T3)
     rt3[near] = t2[...]
 
+    arrived(re5.at[pl.ds(0, 3)], G_E5)
+    push(re5, re6, G_E6, near_device(twin))
+    early_out[pl.ds(pl.multiple_of(mine, 512), 512)] = re5[...].reshape(512, LANES)
+
     conv_k = jnp.concatenate(
         [jnp.concatenate([conv_w[a, b] for b in range(3)], axis=1) for a in range(3)], axis=0
     )
@@ -526,8 +544,8 @@
 
     loop(ROWS, out_row, conv_start(conv_k, v3), unroll=8)
 
-    arrived(e5, G_E5)
-    early_out[pl.ds(pl.multiple_of(512 - mine, 512), 512)] = e5[...].reshape(512, LANES)
+    arrived(re6, G_E6)
+    early_out[pl.ds(pl.multiple_of(512 - mine, 512), 512)] = re6[...].reshape(512, LANES)
     from_near(rt3, G_T3)
     tail_out[...] = rt3[...]
 
@@ -540,13 +558,13 @@
     ):
         gone(ref.at[pl.ds(0, NEAR - 1)], g)
     for ref, g in (
-        (vb_in, G_VB), (vc_in, G_VC), (gb_in, G_GB), (gc_in, G_GC), (re2, G_E2), (re3, G_E3), (rt2, G_T2),
+        (vb_in, G_VB), (vc_in, G_VC), (gb_in, G_GB), (gc_in, G_GC), (rt2, G_T2),
     ):
         gone(ref.at[pl.ds(0, FAR - 1)], g)
     gone(re0, G_E0)
-    gone(re1.at[pl.ds(0, 3)], G_E1)
-    gone(re4.at[pl.ds(0, 3)], G_E4)
-    gone(e5, G_E5)
+    for ref, g in ((re1, G_E1), (re2, G_E2), (re3, G_E3), (re4, G_E4), (re5, G_E5)):
+        gone(ref.at[pl.ds(0, 3)], g)
+    gone(re6, G_E6)
 
 
 def finish(rest, gframe, early, tail, restored, grad_frames, grad_w_in_t, grad_grid, grad_block, grad_w_out, grad_conv):
@@ -610,8 +628,8 @@
     vm(ROWS, HC, COLS),
     vm(ROWS, HC, COLS),
     vm(ROWS, HC, COLS),
-    vm(ROWS, HC, COLS, dtype=F32),
-    vm(ROWS, HC, COLS, dtype=F32),
+    vm(ROWS, HC, COLS),
+    vm(ROWS, HC, COLS),
     *exchange(),
     *exchange(),
     vm(ROWS, CH, COLS),
@@ -620,20 +638,21 @@
     vm(2, 2, CH, COLS),
     vm(2, CH, LANES),
     vm(2, 6, CH, LANES),
-    vm(CH, LANES, dtype=F32),
-    vm(CH, LANES, dtype=F32),
+    vm(CH, LANES),
+    vm(CH, LANES),
     vm(COLS, COLS),
     vm(4 * COLS, LANES),
     vm(512, LANES),
     vm(512, LANES),
     vm(4, 128, LANES),
     vm(128, LANES, dtype=F32),
-    vm(NA, 8, LANES, dtype=F32),
-    vm(8, LANES, dtype=F32),
-    vm(NA, 8, LANES, dtype=F32),
-    vm(128, LANES),
-    vm(4, 128, LANES),
-    vm(4, 128, LANES),
+    vm(4, 32, LANES, dtype=F32),
+    vm(32, LANES, dtype=F32),
+    vm(4, 32, LANES, dtype=F32),
+    vm(32, LANES),
+    vm(4, 32, LANES),
+    vm(4, 4, 32, LANES),
+    vm(4, 4, 32, LANES),
     vm(6 * CH, LANES),
     vm(NW, 48, LANES),
     vm(48, LANES),

time: 63.7 us -> 62.8 us (0.986)
  Pallas kernels: 62.9 us -> 62 us
    pallas_call x1, Pallas kernels: 60.3 us -> 59.4 us  [body(): pl.pallas_call(kernel, out_shape=(shape((2, ROWS * CH, LANES), F32), shap...]
where the time goes in v5:
time: 62.8 us; the launch traced here: 62.7 us
  Pallas kernels  62 us (99%)
  between operations  0.64 us (1%)
    pallas_call x1, Pallas kernels, body(): pl.pallas_call(kernel, out_shape=(shape((2, ROWS * CH, LANES), F32), shap...  59.4 us
    pallas_call x1, Pallas kernels, body(): pl.pallas_call(finish, out_shape=(shape((CH, ROWS, COLS), BF), shape((CH,...  2.63 us

profile of v5, /device:TPU:1, one launch (start us, length us, event | category | flops | bytes accessed | tf_op | source)
XLA Modules:
  0.0 62.7 jit_solution(6299718937246705629)
XLA Ops:
  0.6 59.4 %shard_map.126 = (f32[2,1024,128]{2,1,0:T(8,128)S(1)}, f32[2,1024,128]{2,1,0:T(8,128)S(1)}, bf16[1024,128]{1,0:T(8,128)(2,1)S(1)}, bf16[8,48,128]{2,1,0:T(8,128)(2,1)S(1)}) custom-call(bf16[64,16,256]{2,1,0:T(8,128)(2,1)} %frames_hbm.1, bf16[64,128]{1,0:T(8,128)(2,1)} %bitcast.4, bf16[256,256]{1,0:T(8,128)(2,1)} %grid_mix_hbm.1, ...), custom_call_target="tpu_custom_call" | custom-call | tf_op jit(solution)/shard_map/pallas_call | solution.py:672
  60.0 2.6 %shard_map.127 = (bf16[64,16,256]{2,1,0:T(8,128)(2,1)}, bf16[64,16,256]{2,1,0:T(8,128)(2,1)}, f32[64,128]{1,0:T(8,128)}, f32[256,256]{1,0:T(8,128)}, f32[256,256...) custom-call(f32[2,1024,128]{2,1,0:T(8,128)S(1)} %get-tuple-element.18.rest, ...), custom_call_target="tpu_custom_call" | custom-call | tf_op jit(solution)/shard_map/pallas_call | solution.py:687

commit v6 on v5

--- a/solution.py
+++ b/solution.py
@@ -21,8 +21,8 @@
 FAR = 16
 
 (G_ROW0, G_PACK0, G_ROW1, G_PACK1, G_VA, G_VB, G_VC, G_VD, G_GA, G_GB, G_GC, G_GD) = range(12)
-(G_E0, G_E1, G_E2, G_E3, G_E4, G_E5, G_E6, G_T1, G_T2, G_T3) = range(12, 22)
-GROUPS = 22
+(G_E0, G_E1, G_E2, G_E3, G_E4, G_E5, G_E6, G_T1, G_T2, G_T3, G_T4, G_Q1, G_Q2) = range(12, 25)
+GROUPS = 25
 
 
 def dot(a, b):
@@ -73,13 +73,14 @@
 
 def kernel(
     frames_hbm, w_in_t_hbm, grid_mix_hbm, block_mix_hbm, w_out_hbm, conv_w_hbm, cot_hbm,
-    rest_out, gframe_out, early_out, tail_out,
+    rest_out, gframe_out, early_out, tail_out, value_out,
     frames, w_in_t, grid_mix, block_mix, w_out, conv_w, cot, w_in,
-    turn, xb, nb, unit, inv, dgelu, gates, bval, u3, v3, gj, gg, bback, xt, bt, bm, gbv,
+    turn, xb, nb, unit, inv, dgelu, gates, bval, u3, v3, gj, gg, xt, bt, bm, gbv,
     va, va_in, vx, vb, vb_in, vc, vc_in, vd, vd_in,
     ga, ga_in, gx, gb, gb_in, gc, gc_in, gd, gd_in,
     gated, gbef, jp, row_in, pack_out, pack_in, edge_l, edge_r,
-    mixp, se, re0, e0, re1, e1, re2, e2, re3, e3, re4, re5, re6, st, rt1, t1, rt2, t2, rt3,
+    mixp, se, re0, e0, re1, e1, re2, e2, re3, e3, re4, re5, re6,
+    st, rt1, t1, rt2, t2, rt3, t3, rt4, sq, rq1, q1, rq2,
     ssem, rsem, isem,
 ):
     ia = lax.axis_index("ha")
@@ -93,9 +94,9 @@
         pltpu.make_async_copy(src, dst, isem.at[k])
         for k, (src, dst) in enumerate(
             [
+                (cot_hbm, cot),
                 (frames_hbm, frames),
                 (w_in_t_hbm, w_in_t),
-                (cot_hbm, cot),
                 (conv_w_hbm, conv_w),
                 (w_out_hbm, w_out),
                 (block_mix_hbm, block_mix),
@@ -278,8 +279,31 @@
             if peer is not near:
                 push(d.at[peer], d_in.at[near], g_d, near_device(peer))
 
+    def order():
+        row = lax.broadcasted_iota(jnp.int32, (COLS, COLS), 0)
+        cell = lax.broadcasted_iota(jnp.int32, (COLS, COLS), 1)
+        found = (row & 0xC1) | ((row & 6) << 3) | ((row & 48) >> 2) | ((row & 8) >> 2)
+        return jnp.where(cell == found, 1.0, 0.0).astype(BF)
+
+    def mix_in_order():
+        swap = order()
+        return dot_nt(dot(swap, grid_mix[...]).astype(BF), swap).astype(BF)
+
     loads[0].wait()
+    turn_in(cot)
+
+    def cot_row(r, pack):
+        t0, t1 = turned(r, 0).astype(BF), turned(r, 1).astype(BF)
+        u3[r + 1, CH : 2 * CH, half(0)] = t0
+        u3[r + 1, CH : 2 * CH, half(1)] = t1
+        return edges(pack, t0, t1, r)
+
+    pack = loop(ROWS, cot_row, jnp.zeros((CH, LANES), BF), unroll=8)
+    pl.semaphore_wait(barrier, len(peers))
+    send_halo(u3, pack, 0, G_ROW0, G_PACK0)
+
     loads[1].wait()
+    loads[2].wait()
     turn_in(frames)
     w_in[...] = w_in_t[...].astype(F32).T.astype(BF)
 
@@ -305,58 +329,25 @@
         for peer in group:
             for low in range(2):
                 value_row(va_in if peer is near else va, peer, low)
-        if first == 0:
-            pl.semaphore_wait(barrier, len(peers))
         for peer in group:
             if peer is not near:
                 push(va.at[peer], va_in.at[near], G_VA, near_device(peer))
 
-    def order():
-        row = lax.broadcasted_iota(jnp.int32, (COLS, COLS), 0)
-        cell = lax.broadcasted_iota(jnp.int32, (COLS, COLS), 1)
-        found = (row & 0xC1) | ((row & 6) << 3) | ((row & 48) >> 2) | ((row & 8) >> 2)
-        return jnp.where(cell == found, 1.0, 0.0).astype(BF)
-
-    def mix_in_order():
-        swap = order()
-        return dot_nt(dot(swap, grid_mix[...]).astype(BF), swap).astype(BF)
-
-
-    loads[2].wait()
-    turn_in(cot)
-
-    def cot_row(r, pack):
-        t0, t1 = turned(r, 0).astype(BF), turned(r, 1).astype(BF)
-        u3[r + 1, CH : 2 * CH, half(0)] = t0
-        u3[r + 1, CH : 2 * CH, half(1)] = t1
-        return edges(pack, t0, t1, r)
-
-    pack = loop(ROWS, cot_row, jnp.zeros((CH, LANES), BF), unroll=8)
-    send_halo(u3, pack, 0, G_ROW0, G_PACK0)
-
-    def gate_row(r, carry):
-        before = dot(w_in[...], nb[r])
-        value, slope = gelu_parts(before[0:HC])
+    def grid_gate_row(r, carry):
+        value, slope = gelu_parts(dot(w_in[0:HC], nb[r]))
         gates[r, 0:HC] = value.astype(BF)
         dgelu[r, 0:HC] = slope
-        value, slope = gelu_parts(before[CH:])
-        dgelu[r, CH:] = slope
-        value = value.astype(BF)
-        gates[r, HC:CH] = value[0:HC]
-        bval[r] = value[HC:]
         return carry
 
-    loop(ROWS, gate_row, unroll=8)
+    loop(ROWS, grid_gate_row, unroll=8)
+
     for load in loads[3:]:
         load.wait()
-    mixp[...] = mix_in_order()
-    step_b(va_in, vx, vb, vb_in, G_VA, G_VB)
-
-    take_halo(u3, 0, G_ROW0, G_PACK0)
     back_w = jnp.concatenate(
         [jnp.concatenate([conv_w[2 - a, 2 - b] for a in range(3)], axis=1) for b in range(3)], axis=0
     ).astype(F32).T.astype(BF)
     w_out_t = w_out[...].astype(F32).T.astype(BF)
+    take_halo(u3, 0, G_ROW0, G_PACK0)
 
     def back_row(r, carry):
         total, carry = conv_step(back_w, u3, r, carry)
@@ -364,10 +355,9 @@
         gj[r] = g
         up_gated = dot(w_out_t, g)
         gg[r] = up_gated
-        mixed = (up_gated * gates[r].astype(F32)).astype(BF)
-        ga[r // 2, 0, r % 2] = mixed[0:HC, half(0)]
-        ga[r // 2, 1, r % 2] = mixed[0:HC, half(1)]
-        bback[r] = mixed[HC:]
+        mixed = (up_gated[0:HC] * gates[r, 0:HC].astype(F32)).astype(BF)
+        ga[r // 2, 0, r % 2] = mixed[:, half(0)]
+        ga[r // 2, 1, r % 2] = mixed[:, half(1)]
         return carry
 
     carry = conv_start(back_w, u3)
@@ -382,8 +372,18 @@
 
     ga_in[near] = ga[near]
 
-    from_far(vb_in, G_VB)
-    step_c(dot(mixp[...], vb_in[...].reshape(256, 512)), vc, vc_in, G_VC)
+    step_b(va_in, vx, vb, vb_in, G_VA, G_VB)
+
+    def block_gate_row(r, carry):
+        value, slope = gelu_parts(dot(w_in[CH:], nb[r]))
+        dgelu[r, CH:] = slope
+        value = value.astype(BF)
+        gates[r, HC:CH] = value[0:HC]
+        bval[r] = value[HC:]
+        return carry
+
+    loop(ROWS, block_gate_row, unroll=8)
+    mixp[...] = mix_in_order()
 
     def put(ref):
         def store(k, t, value):
@@ -397,9 +397,13 @@
     swap_granules(lambda k, t: mixed[k * HC : (k + 1) * HC, half(t)], put(bm), HC)
 
     step_b(ga_in, gx, gb, gb_in, G_GA, G_GB)
-    step_d(vc_in, vx, vd, vd_in, G_VC, G_VD)
-
-    swap_granules(lambda k, t: bback[k, :, half(t)], put(bt), HC)
+    from_far(vb_in, G_VB)
+    step_c(dot(mixp[...], vb_in[...].reshape(256, 512)), vc, vc_in, G_VC)
+
+    def block_back(k, t):
+        return (gg[k, HC:, half(t)] * gates[k, HC:, half(t)].astype(F32)).astype(BF)
+
+    swap_granules(block_back, put(bt), HC)
     backs = bt[...].reshape(ROWS * HC, COLS)
     unmixed = dot(backs, block_mix[...]).astype(BF)
     swap_granules(lambda k, t: unmixed[k * HC : (k + 1) * HC, half(t)], put(gbv), HC)
@@ -407,17 +411,30 @@
     se[2 * COLS : 3 * COLS] = part_block[:, half(0)]
     se[3 * COLS :] = part_block[:, half(1)]
 
+    def block_before_row(r, carry):
+        d = dgelu[r, CH:]
+        gbef[r, CH : CH + HC] = (d[0:HC] * (gg[r, HC:] * (bm[r].astype(F32) + 1.0))).astype(BF)
+        gbef[r, CH + HC :] = (d[HC:] * gbv[r].astype(F32)).astype(BF)
+        gbef[r, HC:CH] = jnp.zeros((HC, COLS), BF)
+        return carry
+
+    loop(ROWS, block_before_row, unroll=4)
+    for k in (0, 1, ROWS + 2, ROWS + 3):
+        jp[k] = jnp.zeros((CH, COLS), BF)
+
     from_far(gb_in, G_GB)
     back = gb_in[...].reshape(256, 512)
     step_c(dot_tn(mixp[...], back), gc, gc_in, G_GC)
+    step_d(vc_in, vx, vd, vd_in, G_VC, G_VD)
+
     part_grid = dot_nt(back, vb_in[...].reshape(256, 512)).astype(BF)
     part_grid = dot(dot_tn(order(), part_grid).astype(BF), order()).astype(BF)
     se[0:COLS] = part_grid[:, half(0)]
     se[COLS : 2 * COLS] = part_grid[:, half(1)]
     push(se.at[pl.ds(pl.multiple_of(512 - mine, 512), 512)], re0, G_E0, near_device(twin))
 
-    for k in (0, 1, ROWS + 2, ROWS + 3):
-        jp[k] = jnp.zeros((CH, COLS), BF)
+    step_d(gc_in, gx, gd, gd_in, G_GC, G_GD)
+
     from_near(vd_in, G_VD)
 
     def returned(ref, r):
@@ -442,43 +459,21 @@
     over_y(lambda peer: e0.at[pl.ds(pl.multiple_of(peer * 128, 128), 128)], re1.at[level], G_E1)
     re1[level] = e0[pl.ds(pl.multiple_of(level * 128, 128), 128)]
 
-    step_d(gc_in, gx, gd, gd_in, G_GC, G_GD)
-
-    arrived(re1.at[pl.ds(0, 3)], G_E1)
-    total = re1[0].astype(F32)
-    for k in range(1, 4):
-        total = total + re1[k].astype(F32)
-    e1[...] = total
-    over_x(lambda peer: e1.at[pl.ds(pl.multiple_of(peer * 32, 32), 32)], re2.at[across], G_E2)
-    re2[across] = e1[pl.ds(pl.multiple_of(across * 32, 32), 32)]
-
     def conv_row(p, total):
         return total + dot_nt(u3[p], jp[pl.ds(p, 3)].reshape(3 * CH, COLS))
 
     p_conv = loop(ROWS + 2, conv_row, jnp.zeros((3 * CH, 3 * CH), F32), unroll=9)
 
-    arrived(re2.at[pl.ds(0, 3)], G_E2)
-    e2[...] = re2[0] + re2[1] + re2[2] + re2[3]
-    over_z(lambda peer: e2, re3.at[deep], G_E3)
-    re3[deep] = e2[...]
-
-    from_near(gd_in, G_GD)
-
-    def before_row(r, carry):
+    def gate_before_row(r, carry):
         p_in, p_out = carry
         grid_mixed = returned(vd_in, r)
-        grid_back = returned(gd_in, r)
         for t in range(2):
-            g = gg[r, :, half(t)]
-            d = dgelu[r, :, half(t)]
-            gbef[r, 0:HC, half(t)] = (d[0:HC] * (g[0:HC] * (grid_mixed[t] + 1.0))).astype(BF)
-            gbef[r, HC:CH, half(t)] = (d[HC:CH] * grid_back[t]).astype(BF)
-            gbef[r, CH : CH + HC, half(t)] = (d[CH : CH + HC] * (g[HC:] * (bm[r, :, half(t)].astype(F32) + 1.0))).astype(BF)
-            gbef[r, CH + HC :, half(t)] = (d[CH + HC :] * gbv[r, :, half(t)].astype(F32)).astype(BF)
+            slope = dgelu[r, 0:HC, half(t)]
+            gbef[r, 0:HC, half(t)] = (slope * (gg[r, 0:HC, half(t)] * (grid_mixed[t] + 1.0))).astype(BF)
         return p_in + dot_nt(nb[r], gbef[r]), p_out + dot_nt(gj[r], gated[r])
 
     p_in, p_out = loop(
-        ROWS, before_row, (jnp.zeros((CH, 2 * CH), F32), jnp.zeros((CH, CH), F32)), unroll=4
+        ROWS, gate_before_row, (jnp.zeros((CH, 2 * CH), F32), jnp.zeros((CH, CH), F32)), unroll=4
     )
     st[0 : 3 * CH] = p_conv[:, half(0)].astype(BF)
     st[3 * CH : 4 * CH] = p_in.astype(BF)
@@ -489,10 +484,26 @@
     over_near(lambda peer: st.at[pl.ds(pl.multiple_of(peer * 48, 16), 48)], rt1.at[near], G_T1)
     rt1[near] = st[pl.ds(pl.multiple_of(near * 48, 16), 48)]
 
-    arrived(re3.at[pl.ds(0, 3)], G_E3)
-    e3[...] = (re3[0] + re3[1] + re3[2] + re3[3]).astype(BF)
-    over_x(lambda peer: e3, re4.at[across], G_E4)
-    re4[across] = e3[...]
+    from_near(gd_in, G_GD)
+
+    def value_before_row(r, total):
+        grid_back = returned(gd_in, r)
+        for t in range(2):
+            gbef[r, HC:CH, half(t)] = (dgelu[r, HC:CH, half(t)] * grid_back[t]).astype(BF)
+        return total + dot_nt(gbef[r, HC:CH], nb[r])
+
+    p_value = loop(ROWS, value_before_row, jnp.zeros((HC, CH), F32), unroll=4)
+    sq[...] = jnp.concatenate([p_value[0:16], p_value[16:]], axis=1).astype(BF)
+    over_near(lambda peer: sq, rq1.at[near], G_Q1)
+    rq1[near] = sq[...]
+
+    arrived(re1.at[pl.ds(0, 3)], G_E1)
+    total = re1[0].astype(F32)
+    for k in range(1, 4):
+        total = total + re1[k].astype(F32)
+    e1[...] = total
+    over_x(lambda peer: e1.at[pl.ds(pl.multiple_of(peer * 32, 32), 32)], re2.at[across], G_E2)
+    re2[across] = e1[pl.ds(pl.multiple_of(across * 32, 32), 32)]
 
     def frame_row(r, carry):
         normed = dot(w_in_t[...], gbef[r])
@@ -508,28 +519,39 @@
 
     from_near(rt1, G_T1)
     total = rt1[0].astype(F32)
-    for k in range(1, NW):
+    for k in range(1, NEAR):
         total = total + rt1[k].astype(F32)
     t1[...] = total.astype(BF)
-    over_far(lambda peer: t1, rt2.at[far], G_T2)
-    rt2[far] = t1[...]
-
-    arrived(re4.at[pl.ds(0, 3)], G_E4)
-    over_y(lambda peer: re4, re5.at[level], G_E5)
-    re5[level] = re4[...]
+    over_x(lambda peer: t1, rt2.at[across], G_T2)
+    rt2[across] = t1[...]
+
+    from_near(rq1, G_Q1)
+    total = rq1[0].astype(F32)
+    for k in range(1, NEAR):
+        total = total + rq1[k].astype(F32)
+    q1[...] = total.astype(BF)
+    over_far(lambda peer: q1, rq2.at[far], G_Q2)
+    rq2[far] = q1[...]
+
+    arrived(re2.at[pl.ds(0, 3)], G_E2)
+    e2[...] = re2[0] + re2[1] + re2[2] + re2[3]
+    over_z(lambda peer: e2, re3.at[deep], G_E3)
+    re3[deep] = e2[...]
 
     take_halo(v3, 1, G_ROW1, G_PACK1)
-    from_far(rt2, G_T2)
+
+    arrived(rt2.at[pl.ds(0, 3)], G_T2)
     total = rt2[0].astype(F32)
-    for k in range(1, NA):
+    for k in range(1, 4):
         total = total + rt2[k].astype(F32)
     t2[...] = total.astype(BF)
-    over_near(lambda peer: t2, rt3.at[near], G_T3)
-    rt3[near] = t2[...]
-
-    arrived(re5.at[pl.ds(0, 3)], G_E5)
-    push(re5, re6, G_E6, near_device(twin))
-    early_out[pl.ds(pl.multiple_of(mine, 512), 512)] = re5[...].reshape(512, LANES)
+    over_z(lambda peer: t2, rt3.at[deep], G_T3)
+    rt3[deep] = t2[...]
+
+    arrived(re3.at[pl.ds(0, 3)], G_E3)
+    e3[...] = (re3[0] + re3[1] + re3[2] + re3[3]).astype(BF)
+    over_x(lambda peer: e3, re4.at[across], G_E4)
+    re4[across] = e3[...]
 
     conv_k = jnp.concatenate(
         [jnp.concatenate([conv_w[a, b] for b in range(3)], axis=1) for a in range(3)], axis=0
@@ -542,32 +564,57 @@
             rest_out[t, pl.ds(r * CH, CH), :] = total[:, half(t)]
         return carry
 
-    loop(ROWS, out_row, conv_start(conv_k, v3), unroll=8)
-
+    carry = loop(ROWS // 2, out_row, conv_start(conv_k, v3), unroll=8)
+
+    arrived(re4.at[pl.ds(0, 3)], G_E4)
+    over_y(lambda peer: re4, re5.at[level], G_E5)
+    re5[level] = re4[...]
+    arrived(rt3.at[pl.ds(0, 3)], G_T3)
+    total = rt3[0].astype(F32)
+    for k in range(1, 4):
+        total = total + rt3[k].astype(F32)
+    t3[...] = total.astype(BF)
+    over_near(lambda peer: t3, rt4.at[near], G_T4)
+    rt4[near] = t3[...]
+
+    loop(ROWS // 2, lambda r, carry: out_row(r + ROWS // 2, carry), carry, unroll=8)
+
+    arrived(re5.at[pl.ds(0, 3)], G_E5)
+    push(re5, re6, G_E6, near_device(twin))
+    early_out[pl.ds(pl.multiple_of(mine, 512), 512)] = re5[...].reshape(512, LANES)
+
+    from_far(rq2, G_Q2)
+    total = rq2[0].astype(F32)
+    for k in range(1, FAR):
+        total = total + rq2[k].astype(F32)
+    value_out[...] = total
+    from_near(rt4, G_T4)
+    tail_out[...] = rt4[...]
     arrived(re6, G_E6)
     early_out[pl.ds(pl.multiple_of(512 - mine, 512), 512)] = re6[...].reshape(512, LANES)
-    from_near(rt3, G_T3)
-    tail_out[...] = rt3[...]
 
     for which, g_row, g_pack in ((0, G_ROW0, G_PACK0), (1, G_ROW1, G_PACK1)):
         gone(row_in.at[which], g_row)
         gone(pack_in.at[which], g_pack)
     for ref, g in (
         (va_in, G_VA), (vd_in, G_VD), (ga_in, G_GA), (gd_in, G_GD),
-        (rt1, G_T1), (rt3, G_T3),
+        (rt1, G_T1), (rt4, G_T4), (rq1, G_Q1),
     ):
         gone(ref.at[pl.ds(0, NEAR - 1)], g)
     for ref, g in (
-        (vb_in, G_VB), (vc_in, G_VC), (gb_in, G_GB), (gc_in, G_GC), (rt2, G_T2),
+        (vb_in, G_VB), (vc_in, G_VC), (gb_in, G_GB), (gc_in, G_GC), (rq2, G_Q2),
     ):
         gone(ref.at[pl.ds(0, FAR - 1)], g)
     gone(re0, G_E0)
-    for ref, g in ((re1, G_E1), (re2, G_E2), (re3, G_E3), (re4, G_E4), (re5, G_E5)):
+    for ref, g in ((re1, G_E1), (re2, G_E2), (re3, G_E3), (re4, G_E4), (re5, G_E5), (rt2, G_T2), (rt3, G_T3)):
         gone(ref.at[pl.ds(0, 3)], g)
     gone(re6, G_E6)
 
 
-def finish(rest, gframe, early, tail, restored, grad_frames, grad_w_in_t, grad_grid, grad_block, grad_w_out, grad_conv):
+def finish(
+    rest, gframe, early, tail, value,
+    restored, grad_frames, grad_w_in_t, grad_grid, grad_block, grad_w_out, grad_conv,
+):
     scale = float(ROWS * NA * COLS * NW) ** (-0.5)
 
     def channel(c, carry):
@@ -581,7 +628,10 @@
     for k in range(2):
         grad_grid[:, half(k)] = early[k * COLS : (k + 1) * COLS].astype(F32) * scale
         grad_block[:, half(k)] = early[(2 + k) * COLS : (3 + k) * COLS].astype(F32) * scale
-    grad_w_in_t[...] = tail[3 * CH : 4 * CH].astype(F32) * scale
+    quarter = value[...] * scale
+    zeros = jnp.zeros((HC, CH), F32)
+    quarter = jnp.concatenate([zeros, quarter[:, :CH], quarter[:, CH:], zeros, zeros], axis=0)
+    grad_w_in_t[...] = tail[3 * CH : 4 * CH].astype(F32) * scale + quarter.T
     last = tail[4 * CH :].astype(F32) * scale
     grad_w_out[...] = last[CH:, CH:]
     for b in range(3):
@@ -625,7 +675,6 @@
     vm(ROWS + 2, 3 * CH, COLS),
     vm(ROWS, CH, COLS),
     vm(ROWS, CH, COLS, dtype=F32),
-    vm(ROWS, HC, COLS),
     vm(ROWS, HC, COLS),
     vm(ROWS, HC, COLS),
     vm(ROWS, HC, COLS),
@@ -656,9 +705,15 @@
     vm(6 * CH, LANES),
     vm(NW, 48, LANES),
     vm(48, LANES),
-    vm(NA, 48, LANES),
+    vm(4, 48, LANES),
     vm(48, LANES),
-    vm(NW, 48, LANES),
+    vm(4, 48, LANES),
+    vm(48, LANES),
+    vm(NEAR, 48, LANES),
+    vm(16, LANES),
+    vm(NEAR, 16, LANES),
+    vm(16, LANES),
+    vm(FAR, 16, LANES),
     pltpu.SemaphoreType.DMA((GROUPS,)),
     pltpu.SemaphoreType.DMA((GROUPS,)),
     pltpu.SemaphoreType.DMA((7,)),
@@ -669,16 +724,17 @@
     operands = (frames, w_in.T, grid_mix, block_mix, w_out, conv_w, cotangent)
     vmem = pl.BlockSpec(memory_space=pltpu.VMEM)
     shape = jax.ShapeDtypeStruct
-    rest, gframe, early, tail = pl.pallas_call(
+    rest, gframe, early, tail, value = pl.pallas_call(
         kernel,
         out_shape=(
             shape((2, ROWS * CH, LANES), F32),
             shape((2, ROWS * CH, LANES), F32),
             shape((4 * COLS, LANES), BF),
-            shape((NW, 48, LANES), BF),
+            shape((NEAR, 48, LANES), BF),
+            shape((16, LANES), F32),
         ),
         in_specs=[pl.BlockSpec(memory_space=pltpu.HBM)] * 7,
-        out_specs=(vmem,) * 4,
+        out_specs=(vmem,) * 5,
         scratch_shapes=SCRATCH,
         compiler_params=pltpu.CompilerParams(
             collective_id=0, has_side_effects=True, vmem_limit_bytes=32 * 1024 * 1024
@@ -695,10 +751,10 @@
             shape((CH, CH), F32),
             shape((3, 3, CH, CH), F32),
         ),
-        in_specs=[vmem] * 4,
+        in_specs=[vmem] * 5,
         out_specs=(vmem,) * 7,
         compiler_params=pltpu.CompilerParams(vmem_limit_bytes=16 * 1024 * 1024),
-    )(rest, gframe, early, tail.reshape(6 * CH, LANES))
+    )(rest, gframe, early, tail.reshape(6 * CH, LANES), value)
     return restored, grad_frames, grad_w_in_t.T, grad_grid, grad_block, grad_w_out, grad_conv
 
 

time: 62.8 us -> 64.5 us (1.027)
  Pallas kernels: 62 us -> 63.7 us
    pallas_call x1, Pallas kernels: 59.4 us -> 61.1 us  [body(): pl.pallas_call(kernel, out_shape=(shape((2, ROWS * CH, LANES), F32), shap...]
where the time goes in v6:
time: 64.5 us; the launch traced here: 64.4 us
  Pallas kernels  63.7 us (99%)
    pallas_call x1, Pallas kernels, body(): pl.pallas_call(kernel, out_shape=(shape((2, ROWS * CH, LANES), F32), shap...  61.1 us
    pallas_call x1, Pallas kernels, body(): pl.pallas_call(finish, out_shape=(shape((CH, ROWS, COLS), BF), shape((CH,...  2.63 us

profile of v6, /device:TPU:1, one launch (start us, length us, event | category | flops | bytes accessed | tf_op | source)
XLA Modules:
  0.0 64.4 jit_solution(8425703981621512688)
XLA Ops:
  0.6 61.1 %shard_map.126 = (f32[2,1024,128]{2,1,0:T(8,128)S(1)}, f32[2,1024,128]{2,1,0:T(8,128)S(1)}, bf16[1024,128]{1,0:T(8,128)(2,1)S(1)}, bf16[8,48,128]{2,1,0:T(8,128)(2,1)S(1)}, f32[16,128]{1,0:T(8,128)S(1)}) custom-call(bf16[64,16,256]{2,1,0:T(8,128)(2,1)} %frames_hbm.1, bf16[64,128]{1,0:T(8,128)(2,1)} %bitcast.4, bf16[256,256]{1,0:T(8,128)(2,1)} %grid_mix_hbm.1, ...), custom_call_target="tpu_custom_call" | custom-call | tf_op jit(solution)/shard_map/pallas_call | solution.py:727
  61.7 2.6 %shard_map.127 = (bf16[64,16,256]{2,1,0:T(8,128)(2,1)}, bf16[64,16,256]{2,1,0:T(8,128)(2,1)}, f32[64,128]{1,0:T(8,128)}, f32[256,256]{1,0:T(8,128)}, f32[256,256...) custom-call(f32[2,1024,128]{2,1,0:T(8,128)S(1)} %get-tuple-element.19.rest, ...), custom_call_target="tpu_custom_call" | custom-call | tf_op jit(solution)/shard_map/pallas_call | solution.py:743

commit v7 on v6

--- a/solution.py
+++ b/solution.py
@@ -8,7 +8,7 @@
 BF = jnp.bfloat16
 F32 = jnp.float32
 EPS = 1e-06
-MESH = pl.DeviceIdType.MESH
+LOGICAL = pl.DeviceIdType.LOGICAL
 
 CH = 64
 HC = 32
@@ -21,8 +21,8 @@
 FAR = 16
 
 (G_ROW0, G_PACK0, G_ROW1, G_PACK1, G_VA, G_VB, G_VC, G_VD, G_GA, G_GB, G_GC, G_GD) = range(12)
-(G_E0, G_E1, G_E2, G_E3, G_E4, G_E5, G_E6, G_T1, G_T2, G_T3, G_T4, G_Q1, G_Q2) = range(12, 25)
-GROUPS = 25
+(G_E0, G_E1, G_E2, G_E3, G_E4, G_E5, G_E6, G_T1, G_T2, G_T3) = range(12, 22)
+GROUPS = 22
 
 
 def dot(a, b):
@@ -73,14 +73,14 @@
 
 def kernel(
     frames_hbm, w_in_t_hbm, grid_mix_hbm, block_mix_hbm, w_out_hbm, conv_w_hbm, cot_hbm,
-    rest_out, gframe_out, early_out, tail_out, value_out,
+    rest_out, gframe_out, early_out, tail_out,
     frames, w_in_t, grid_mix, block_mix, w_out, conv_w, cot, w_in,
     turn, xb, nb, unit, inv, dgelu, gates, bval, u3, v3, gj, gg, xt, bt, bm, gbv,
     va, va_in, vx, vb, vb_in, vc, vc_in, vd, vd_in,
     ga, ga_in, gx, gb, gb_in, gc, gc_in, gd, gd_in,
     gated, gbef, jp, row_in, pack_out, pack_in, edge_l, edge_r,
-    mixp, se, re0, e0, re1, e1, re2, e2, re3, e3, re4, re5, re6,
-    st, rt1, t1, rt2, t2, rt3, t3, rt4, sq, rq1, q1, rq2,
+    mixp, mixp_t, gather, spread, se, re0, e0, re1, e1, re2, e2, re3, e3, re4, re5, re6,
+    st, rt1, t1, rt2, t2, rt3,
     ssem, rsem, isem,
 ):
     ia = lax.axis_index("ha")
@@ -109,44 +109,53 @@
 
     def push(src, dst, g, where):
         pltpu.make_async_remote_copy(
-            src_ref=src, dst_ref=dst, send_sem=ssem.at[g], recv_sem=rsem.at[g], device_id=where, device_id_type=MESH
+            src_ref=src, dst_ref=dst, send_sem=ssem.at[g], recv_sem=rsem.at[g], device_id=where, device_id_type=LOGICAL
         ).start()
 
-    near = lax.rem(iw, 2) * 4 + lax.rem(ia, 4)
-    far = ia // 4 * 4 + iw // 2
-
-    def near_device(peer):
-        return ia // 4 * 4 + lax.rem(peer, 4), iw // 2 * 2 + peer // 4
-
-    def far_device(peer):
-        return peer // 4 * 4 + lax.rem(ia, 4), lax.rem(peer, 4) * 2 + lax.rem(iw, 2)
-
-    near_peers = [lax.rem(near + k, NEAR) for k in range(1, NEAR)]
-    far_peers = [lax.rem(far + k, FAR) for k in range(1, FAR)]
-    twin = near + 1 - 2 * lax.rem(near, 2)
+    deep, across = ia // 4, iw // 2
+    here, high = lax.rem(ia, 4), lax.rem(iw, 2)
+    near = high * 4 + here
+    far = deep * 4 + across
+    level = near // 2
+    core = lax.rem(ia, 2)
+    low = here - core
+    column = deep * (4 * NW) + across * 2
+    spot = here * NW + high
+    cores = (core, 1 - core)
+    lows = (low, 2 - low)
+    highs = (high, 1 - high)
+    near_peers, near_ids = [], []
+    for k in range(NEAR):
+        place = lows[k // 2 % 2] + cores[k % 2]
+        near_peers.append(highs[k // 4] * 4 + place)
+        near_ids.append(column + place * NW + highs[k // 4])
+    rings = []
+    for index in (deep, across):
+        last = lax.rem(index, 2)
+        first = index - last
+        rings.append([(first, 2 - first)[k // 2] + (last, 1 - last)[k % 2] for k in range(4)])
+    far_peers = [rings[0][k // 4] * 4 + rings[1][k % 4] for k in range(FAR)]
+    far_ids = [rings[0][k // 4] * (4 * NW) + rings[1][k % 4] * 2 + spot for k in range(FAR)]
 
     def over_near(src_of, dst, g):
-        for peer in near_peers:
-            push(src_of(peer), dst, g, near_device(peer))
+        for k in range(1, NEAR):
+            push(src_of(near_peers[k]), dst, g, near_ids[k])
 
     def over_far(src_of, dst, g):
-        for peer in far_peers:
-            push(src_of(peer), dst, g, far_device(peer))
+        for k in range(1, FAR):
+            push(src_of(far_peers[k]), dst, g, far_ids[k])
 
     def over_x(src_of, dst, g):
         for k in range(1, 4):
-            peer = lax.rem(iw // 2 + k, 4)
-            push(src_of(peer), dst, g, (ia, peer * 2 + lax.rem(iw, 2)))
+            push(src_of(rings[1][k]), dst, g, far_ids[k])
 
     def over_z(src_of, dst, g):
         for k in range(1, 4):
-            peer = lax.rem(ia // 4 + k, 4)
-            push(src_of(peer), dst, g, (peer * 4 + lax.rem(ia, 4), iw))
+            push(src_of(rings[0][k]), dst, g, far_ids[4 * k])
 
     def over_y(src_of, dst, g):
         for k in range(1, 4):
-            peer = lax.rem(near + 2 * k, NEAR)
-            push(src_of(peer // 2), dst, g, near_device(peer))
+            push(src_of(near_peers[2 * k] // 2), dst, g, near_ids[2 * k])
 
     def arrived(ref, g):
         pltpu.make_async_copy(ref, ref, rsem.at[g]).wait()
@@ -160,15 +169,17 @@
     def from_far(ref, g):
         arrived(ref.at[pl.ds(0, FAR - 1)], g)
 
-    mine = lax.rem(near, 2) * 512
-    level, across, deep = near // 2, iw // 2, ia // 4
+    mine = core * 512
+    sides = {
+        (a, b): (ia, up, down)[a] * NW + (iw, left, right)[b] for a in range(3) for b in range(3)
+    }
+    halo_ids = [sides[1, 0], sides[2, 0]]
+    halo_ids += [sides[a, b] for a, b in ((0, 2), (0, 1), (2, 2), (2, 1), (1, 2), (1, 1))]
 
     barrier = pltpu.get_barrier_semaphore()
-    peers = [near_device(peer) for peer in near_peers]
-    peers += [far_device(peer) for peer in far_peers]
-    peers += [(a, b) for a in (up, ia, down) for b in (left, right)] + [(up, iw), (down, iw)]
+    peers = near_ids[1:] + far_ids[1:] + halo_ids
     for peer in peers:
-        pl.semaphore_signal(barrier, inc=1, device_id=peer, device_id_type=MESH)
+        pl.semaphore_signal(barrier, inc=1, device_id=peer, device_id_type=LOGICAL)
 
     def turn_in(src):
         for t in range(2):
@@ -183,12 +194,10 @@
 
     def send_halo(field, pack, which, g_row, g_pack):
         pack_out[which] = pack
-        push(field.at[1, CH : 2 * CH], row_in.at[which, 1], g_row, (up, iw))
-        push(field.at[ROWS, CH : 2 * CH], row_in.at[which, 0], g_row, (down, iw))
-        for slot, where in enumerate(
-            [(ia, right), (ia, left), (down, right), (down, left), (up, right), (up, left)]
-        ):
-            push(pack_out.at[which], pack_in.at[which, slot], g_pack, where)
+        push(field.at[1, CH : 2 * CH], row_in.at[which, 1], g_row, halo_ids[0])
+        push(field.at[ROWS, CH : 2 * CH], row_in.at[which, 0], g_row, halo_ids[1])
+        for slot in range(6):
+            push(pack_out.at[which], pack_in.at[which, slot], g_pack, halo_ids[2 + slot])
 
     def take_halo(field, which, g_row, g_pack):
         arrived(row_in.at[which], g_row)
@@ -247,13 +256,14 @@
 
         loop(NEAR, widen, unroll=8)
 
-        for peer in [*far_peers, far]:
+        for k in [*range(1, FAR), 0]:
+            peer = far_peers[k]
             base = peer // 8 * (16 * HC) + lax.rem(peer, 8) * 4
-            slot = b_in if peer is far else b
+            slot = b if k else b_in
             for c in range(4):
                 slot[peer, :, half(c)] = x[pl.ds(base + c, 16, stride=HC), :].astype(BF)
-            if peer is not far:
-                push(b.at[peer], b_in.at[far], g_b, far_device(peer))
+            if k:
+                push(b.at[peer], b_in.at[far], g_b, far_ids[k])
 
     def step_c(mixed, c, c_in, g):
         c[...] = mixed.astype(BF).reshape(FAR, 16, 512)
@@ -271,23 +281,18 @@
 
         loop(8, unpick, unroll=8)
 
-        for peer in [*near_peers, near]:
-            slot = d_in if peer is near else d
+        for k in [*range(1, NEAR), 0]:
+            peer = near_peers[k]
+            slot = d if k else d_in
             for t in range(2):
                 for r in range(2):
                     slot[peer, t, r] = x[pl.ds(r * HC * 16 + peer * 2 + t, HC, stride=16), :].astype(BF)
-            if peer is not near:
-                push(d.at[peer], d_in.at[near], g_d, near_device(peer))
-
-    def order():
-        row = lax.broadcasted_iota(jnp.int32, (COLS, COLS), 0)
-        cell = lax.broadcasted_iota(jnp.int32, (COLS, COLS), 1)
+            if k:
+                push(d.at[peer], d_in.at[near], g_d, near_ids[k])
+
+    def order(cell, row):
         found = (row & 0xC1) | ((row & 6) << 3) | ((row & 48) >> 2) | ((row & 8) >> 2)
         return jnp.where(cell == found, 1.0, 0.0).astype(BF)
-
-    def mix_in_order():
-        swap = order()
-        return dot_nt(dot(swap, grid_mix[...]).astype(BF), swap).astype(BF)
 
     loads[0].wait()
     turn_in(cot)
@@ -307,8 +312,8 @@
     turn_in(frames)
     w_in[...] = w_in_t[...].astype(F32).T.astype(BF)
 
-    def value_row(slot, peer, low):
-        r = peer * 2 + low
+    def value_row(slot, peer, odd):
+        r = peer * 2 + odd
         for t in range(2):
             x = turned(r, t)
             xb[r, :, half(t)] = x.astype(BF)
@@ -321,17 +326,17 @@
         value, slope = gelu_parts(dot(w_in[HC:CH], nb[r]))
         dgelu[r, HC:CH] = slope
         value = value.astype(BF)
-        slot[peer, 0, low] = value[:, half(0)]
-        slot[peer, 1, low] = value[:, half(1)]
+        slot[peer, 0, odd] = value[:, half(0)]
+        slot[peer, 1, odd] = value[:, half(1)]
 
     for first in range(0, NEAR, 2):
-        group = [*near_peers, near][first : first + 2]
-        for peer in group:
-            for low in range(2):
-                value_row(va_in if peer is near else va, peer, low)
-        for peer in group:
-            if peer is not near:
-                push(va.at[peer], va_in.at[near], G_VA, near_device(peer))
+        group = [*range(1, NEAR), 0][first : first + 2]
+        for k in group:
+            for odd in range(2):
+                value_row(va if k else va_in, near_peers[k], odd)
+        for k in group:
+            if k:
+                push(va.at[near_peers[k]], va_in.at[near], G_VA, near_ids[k])
 
     def grid_gate_row(r, carry):
         value, slope = gelu_parts(dot(w_in[0:HC], nb[r]))
@@ -368,7 +373,7 @@
 
             @pl.when(peer != near)
             def _():
-                push(ga.at[peer], ga_in.at[near], G_GA, near_device(peer))
+                push(ga.at[peer], ga_in.at[near], G_GA, column + (peer % 4) * NW + peer // 4)
 
     ga_in[near] = ga[near]
 
@@ -383,7 +388,12 @@
         return carry
 
     loop(ROWS, block_gate_row, unroll=8)
-    mixp[...] = mix_in_order()
+    down_axis = lax.broadcasted_iota(jnp.int32, (COLS, COLS), 0)
+    along_axis = lax.broadcasted_iota(jnp.int32, (COLS, COLS), 1)
+    gather[...] = order(along_axis, down_axis)
+    spread[...] = order(down_axis, along_axis)
+    mixp[...] = dot(dot(gather[...], grid_mix[...]).astype(BF), spread[...]).astype(BF)
+    mixp_t[...] = dot(dot_nt(gather[...], grid_mix[...]).astype(BF), spread[...]).astype(BF)
 
     def put(ref):
         def store(k, t, value):
@@ -415,7 +425,6 @@
         d = dgelu[r, CH:]
         gbef[r, CH : CH + HC] = (d[0:HC] * (gg[r, HC:] * (bm[r].astype(F32) + 1.0))).astype(BF)
         gbef[r, CH + HC :] = (d[HC:] * gbv[r].astype(F32)).astype(BF)
-        gbef[r, HC:CH] = jnp.zeros((HC, COLS), BF)
         return carry
 
     loop(ROWS, block_before_row, unroll=4)
@@ -424,14 +433,14 @@
 
     from_far(gb_in, G_GB)
     back = gb_in[...].reshape(256, 512)
-    step_c(dot_tn(mixp[...], back), gc, gc_in, G_GC)
+    step_c(dot(mixp_t[...], back), gc, gc_in, G_GC)
     step_d(vc_in, vx, vd, vd_in, G_VC, G_VD)
 
     part_grid = dot_nt(back, vb_in[...].reshape(256, 512)).astype(BF)
-    part_grid = dot(dot_tn(order(), part_grid).astype(BF), order()).astype(BF)
+    part_grid = dot(dot(spread[...], part_grid).astype(BF), gather[...]).astype(BF)
     se[0:COLS] = part_grid[:, half(0)]
     se[COLS : 2 * COLS] = part_grid[:, half(1)]
-    push(se.at[pl.ds(pl.multiple_of(512 - mine, 512), 512)], re0, G_E0, near_device(twin))
+    push(se.at[pl.ds(pl.multiple_of(512 - mine, 512), 512)], re0, G_E0, near_ids[1])
 
     step_d(gc_in, gx, gd, gd_in, G_GC, G_GD)
 
@@ -464,12 +473,15 @@
 
     p_conv = loop(ROWS + 2, conv_row, jnp.zeros((3 * CH, 3 * CH), F32), unroll=9)
 
+    from_near(gd_in, G_GD)
+
     def gate_before_row(r, carry):
         p_in, p_out = carry
-        grid_mixed = returned(vd_in, r)
+        grid_mixed, grid_back = returned(vd_in, r), returned(gd_in, r)
         for t in range(2):
             slope = dgelu[r, 0:HC, half(t)]
             gbef[r, 0:HC, half(t)] = (slope * (gg[r, 0:HC, half(t)] * (grid_mixed[t] + 1.0))).astype(BF)
+            gbef[r, HC:CH, half(t)] = (dgelu[r, HC:CH, half(t)] * grid_back[t]).astype(BF)
         return p_in + dot_nt(nb[r], gbef[r]), p_out + dot_nt(gj[r], gated[r])
 
     p_in, p_out = loop(
@@ -484,19 +496,6 @@
     over_near(lambda peer: st.at[pl.ds(pl.multiple_of(peer * 48, 16), 48)], rt1.at[near], G_T1)
     rt1[near] = st[pl.ds(pl.multiple_of(near * 48, 16), 48)]
 
-    from_near(gd_in, G_GD)
-
-    def value_before_row(r, total):
-        grid_back = returned(gd_in, r)
-        for t in range(2):
-            gbef[r, HC:CH, half(t)] = (dgelu[r, HC:CH, half(t)] * grid_back[t]).astype(BF)
-        return total + dot_nt(gbef[r, HC:CH], nb[r])
-
-    p_value = loop(ROWS, value_before_row, jnp.zeros((HC, CH), F32), unroll=4)
-    sq[...] = jnp.concatenate([p_value[0:16], p_value[16:]], axis=1).astype(BF)
-    over_near(lambda peer: sq, rq1.at[near], G_Q1)
-    rq1[near] = sq[...]
-
     arrived(re1.at[pl.ds(0, 3)], G_E1)
     total = re1[0].astype(F32)
     for k in range(1, 4):
@@ -522,16 +521,8 @@
     for k in range(1, NEAR):
         total = total + rt1[k].astype(F32)
     t1[...] = total.astype(BF)
-    over_x(lambda peer: t1, rt2.at[across], G_T2)
-    rt2[across] = t1[...]
-
-    from_near(rq1, G_Q1)
-    total = rq1[0].astype(F32)
-    for k in range(1, NEAR):
-        total = total + rq1[k].astype(F32)
-    q1[...] = total.astype(BF)
-    over_far(lambda peer: q1, rq2.at[far], G_Q2)
-    rq2[far] = q1[...]
+    over_far(lambda peer: t1, rt2.at[far], G_T2)
+    rt2[far] = t1[...]
 
     arrived(re2.at[pl.ds(0, 3)], G_E2)
     e2[...] = re2[0] + re2[1] + re2[2] + re2[3]
@@ -540,13 +531,13 @@
 
     take_halo(v3, 1, G_ROW1, G_PACK1)
 
-    arrived(rt2.at[pl.ds(0, 3)], G_T2)
+    from_far(rt2, G_T2)
     total = rt2[0].astype(F32)
-    for k in range(1, 4):
+    for k in range(1, FAR):
         total = total + rt2[k].astype(F32)
     t2[...] = total.astype(BF)
-    over_z(lambda peer: t2, rt3.at[deep], G_T3)
-    rt3[deep] = t2[...]
+    over_near(lambda peer: t2, rt3.at[near], G_T3)
+    rt3[near] = t2[...]
 
     arrived(re3.at[pl.ds(0, 3)], G_E3)
     e3[...] = (re3[0] + re3[1] + re3[2] + re3[3]).astype(BF)
@@ -569,27 +560,15 @@
     arrived(re4.at[pl.ds(0, 3)], G_E4)
     over_y(lambda peer: re4, re5.at[level], G_E5)
     re5[level] = re4[...]
-    arrived(rt3.at[pl.ds(0, 3)], G_T3)
-    total = rt3[0].astype(F32)
-    for k in range(1, 4):
-        total = total + rt3[k].astype(F32)
-    t3[...] = total.astype(BF)
-    over_near(lambda peer: t3, rt4.at[near], G_T4)
-    rt4[near] = t3[...]
 
     loop(ROWS // 2, lambda r, carry: out_row(r + ROWS // 2, carry), carry, unroll=8)
 
     arrived(re5.at[pl.ds(0, 3)], G_E5)
-    push(re5, re6, G_E6, near_device(twin))
+    push(re5, re6, G_E6, near_ids[1])
     early_out[pl.ds(pl.multiple_of(mine, 512), 512)] = re5[...].reshape(512, LANES)
 
-    from_far(rq2, G_Q2)
-    total = rq2[0].astype(F32)
-    for k in range(1, FAR):
-        total = total + rq2[k].astype(F32)
-    value_out[...] = total
-    from_near(rt4, G_T4)
-    tail_out[...] = rt4[...]
+    from_near(rt3, G_T3)
+    tail_out[...] = rt3[...]
     arrived(re6, G_E6)
     early_out[pl.ds(pl.multiple_of(512 - mine, 512), 512)] = re6[...].reshape(512, LANES)
 
@@ -598,21 +577,21 @@
         gone(pack_in.at[which], g_pack)
     for ref, g in (
         (va_in, G_VA), (vd_in, G_VD), (ga_in, G_GA), (gd_in, G_GD),
-        (rt1, G_T1), (rt4, G_T4), (rq1, G_Q1),
+        (rt1, G_T1), (rt3, G_T3),
     ):
         gone(ref.at[pl.ds(0, NEAR - 1)], g)
     for ref, g in (
-        (vb_in, G_VB), (vc_in, G_VC), (gb_in, G_GB), (gc_in, G_GC), (rq2, G_Q2),
+        (vb_in, G_VB), (vc_in, G_VC), (gb_in, G_GB), (gc_in, G_GC), (rt2, G_T2),
     ):
         gone(ref.at[pl.ds(0, FAR - 1)], g)
     gone(re0, G_E0)
-    for ref, g in ((re1, G_E1), (re2, G_E2), (re3, G_E3), (re4, G_E4), (re5, G_E5), (rt2, G_T2), (rt3, G_T3)):
+    for ref, g in ((re1, G_E1), (re2, G_E2), (re3, G_E3), (re4, G_E4), (re5, G_E5)):
         gone(ref.at[pl.ds(0, 3)], g)
     gone(re6, G_E6)
 
 
 def finish(
-    rest, gframe, early, tail, value,
+    rest, gframe, early, tail,
     restored, grad_frames, grad_w_in_t, grad_grid, grad_block, grad_w_out, grad_conv,
 ):
     scale = float(ROWS * NA * COLS * NW) ** (-0.5)
@@ -628,10 +607,7 @@
     for k in range(2):
         grad_grid[:, half(k)] = early[k * COLS : (k + 1) * COLS].astype(F32) * scale
         grad_block[:, half(k)] = early[(2 + k) * COLS : (3 + k) * COLS].astype(F32) * scale
-    quarter = value[...] * scale
-    zeros = jnp.zeros((HC, CH), F32)
-    quarter = jnp.concatenate([zeros, quarter[:, :CH], quarter[:, CH:], zeros, zeros], axis=0)
-    grad_w_in_t[...] = tail[3 * CH : 4 * CH].astype(F32) * scale + quarter.T
+    grad_w_in_t[...] = tail[3 * CH : 4 * CH].astype(F32) * scale
     last = tail[4 * CH :].astype(F32) * scale
     grad_w_out[...] = last[CH:, CH:]
     for b in range(3):
@@ -690,6 +666,9 @@
     vm(CH, LANES),
     vm(CH, LANES),
     vm(COLS, COLS),
+    vm(COLS, COLS),
+    vm(COLS, COLS),
+    vm(COLS, COLS),
     vm(4 * COLS, LANES),
     vm(512, LANES),
     vm(512, LANES),
@@ -705,15 +684,9 @@
     vm(6 * CH, LANES),
     vm(NW, 48, LANES),
     vm(48, LANES),
-    vm(4, 48, LANES),
-    vm(48, LANES),
-    vm(4, 48, LANES),
+    vm(FAR, 48, LANES),
     vm(48, LANES),
     vm(NEAR, 48, LANES),
-    vm(16, LANES),
-    vm(NEAR, 16, LANES),
-    vm(16, LANES),
-    vm(FAR, 16, LANES),
     pltpu.SemaphoreType.DMA((GROUPS,)),
     pltpu.SemaphoreType.DMA((GROUPS,)),
     pltpu.SemaphoreType.DMA((7,)),
@@ -724,17 +697,16 @@
     operands = (frames, w_in.T, grid_mix, block_mix, w_out, conv_w, cotangent)
     vmem = pl.BlockSpec(memory_space=pltpu.VMEM)
     shape = jax.ShapeDtypeStruct
-    rest, gframe, early, tail, value = pl.pallas_call(
+    rest, gframe, early, tail = pl.pallas_call(
         kernel,
         out_shape=(
             shape((2, ROWS * CH, LANES), F32),
             shape((2, ROWS * CH, LANES), F32),
             shape((4 * COLS, LANES), BF),
             shape((NEAR, 48, LANES), BF),
-            shape((16, LANES), F32),
         ),
         in_specs=[pl.BlockSpec(memory_space=pltpu.HBM)] * 7,
-        out_specs=(vmem,) * 5,
+        out_specs=(vmem,) * 4,
         scratch_shapes=SCRATCH,
         compiler_params=pltpu.CompilerParams(
             collective_id=0, has_side_effects=True, vmem_limit_bytes=32 * 1024 * 1024
@@ -751,10 +723,10 @@
             shape((CH, CH), F32),
             shape((3, 3, CH, CH), F32),
         ),
-        in_specs=[vmem] * 5,
+        in_specs=[vmem] * 4,
         out_specs=(vmem,) * 7,
         compiler_params=pltpu.CompilerParams(vmem_limit_bytes=16 * 1024 * 1024),
-    )(rest, gframe, early, tail.reshape(6 * CH, LANES), value)
+    )(rest, gframe, early, tail.reshape(6 * CH, LANES))
     return restored, grad_frames, grad_w_in_t.T, grad_grid, grad_block, grad_w_out, grad_conv
 
 

time: 64.5 us -> 66 us (1.023)
  Pallas kernels: 63.7 us -> 65.2 us
    pallas_call x1, Pallas kernels: 61.1 us -> 62.6 us  [body(): pl.pallas_call(kernel, out_shape=(shape((2, ROWS * CH, LANES), F32), shap...]
where the time goes in v7:
time: 66 us; the launch traced here: 65.9 us
  Pallas kernels  65.2 us (99%)
    pallas_call x1, Pallas kernels, body(): pl.pallas_call(kernel, out_shape=(shape((2, ROWS * CH, LANES), F32), shap...  62.6 us
    pallas_call x1, Pallas kernels, body(): pl.pallas_call(finish, out_shape=(shape((CH, ROWS, COLS), BF), shape((CH,...  2.63 us

profile of v7, /device:TPU:1, one launch (start us, length us, event | category | flops | bytes accessed | tf_op | source)
XLA Modules:
  0.0 65.9 jit_solution(1565425564841418458)
XLA Ops:
  0.6 62.6 %shard_map.126 = (f32[2,1024,128]{2,1,0:T(8,128)S(1)}, f32[2,1024,128]{2,1,0:T(8,128)S(1)}, bf16[1024,128]{1,0:T(8,128)(2,1)S(1)}, bf16[8,48,128]{2,1,0:T(8,128)(2,1)S(1)}) custom-call(bf16[64,16,256]{2,1,0:T(8,128)(2,1)} %frames_hbm.1, bf16[64,128]{1,0:T(8,128)(2,1)} %bitcast.4, bf16[256,256]{1,0:T(8,128)(2,1)} %grid_mix_hbm.1, ...), custom_call_target="tpu_custom_call" | custom-call | tf_op jit(solution)/shard_map/pallas_call | solution.py:700
  63.3 2.6 %shard_map.127 = (bf16[64,16,256]{2,1,0:T(8,128)(2,1)}, bf16[64,16,256]{2,1,0:T(8,128)(2,1)}, f32[64,128]{1,0:T(8,128)}, f32[256,256]{1,0:T(8,128)}, f32[256,256...) custom-call(f32[2,1024,128]{2,1,0:T(8,128)S(1)} %get-tuple-element.18.rest, ...), custom_call_target="tpu_custom_call" | custom-call | tf_op jit(solution)/shard_map/pallas_call | solution.py:715

commit v8 on v6

--- a/solution.py
+++ b/solution.py
@@ -182,13 +182,14 @@
         return jnp.where(lane_wide == ROWS + r, pltpu.roll(t1, r + 17, 1), pack)
 
     def send_halo(field, pack, which, g_row, g_pack):
-        pack_out[which] = pack
+        pack_out[which] = jnp.concatenate([pack, jnp.zeros_like(pack)], axis=0).T[0:32]
         push(field.at[1, CH : 2 * CH], row_in.at[which, 1], g_row, (up, iw))
         push(field.at[ROWS, CH : 2 * CH], row_in.at[which, 0], g_row, (down, iw))
         for slot, where in enumerate(
-            [(ia, right), (ia, left), (down, right), (down, left), (up, right), (up, left)]
+            [(ia, right), (down, right), (up, right), (ia, left), (down, left), (up, left)]
         ):
-            push(pack_out.at[which], pack_in.at[which, slot], g_pack, where)
+            part = pack_out.at[which, pl.ds(16 if slot < 3 else 0, 16)]
+            push(part, pack_in.at[which, pl.ds(16 * slot, 16)], g_pack, where)
 
     def take_halo(field, which, g_row, g_pack):
         arrived(row_in.at[which], g_row)
@@ -197,19 +198,15 @@
         field[ROWS + 1, CH : 2 * CH] = jnp.where(ia < NA - 1, row_in[which, 1], jnp.zeros((CH, COLS), BF))
         first = jnp.where(ia > 0, 0, 1)
         last = jnp.where(ia < NA - 1, ROWS + 2, ROWS + 1)
-        got = [pack_in[which, k] for k in range(6)]
+        got = jnp.concatenate([pack_in[which], jnp.zeros((32, LANES), BF)], axis=0).T[0:CH]
 
         def assemble(middle, above, below, has):
             joined = jnp.where(lane == 0, above, jnp.where(lane == ROWS + 1, below, middle))
             inside = (lane_wide >= first) & (lane_wide < jnp.where(has, last, 0))
             return jnp.where(inside, joined, jnp.zeros_like(joined))
 
-        edge_l[...] = assemble(
-            pltpu.roll(got[0], 113, 1), pltpu.roll(got[2], 97, 1), pltpu.roll(got[4], 1, 1), iw > 0
-        )
-        edge_r[...] = assemble(
-            pltpu.roll(got[1], 1, 1), pltpu.roll(got[3], 113, 1), pltpu.roll(got[5], 17, 1), iw < NW - 1
-        )
+        edge_l[...] = assemble(pltpu.roll(got, 1, 1), pltpu.roll(got, 97, 1), pltpu.roll(got, 113, 1), iw > 0)
+        edge_r[...] = assemble(pltpu.roll(got, 81, 1), pltpu.roll(got, 49, 1), pltpu.roll(got, 65, 1), iw < NW - 1)
 
         def shifts(p, carry):
             t0 = field[p, CH : 2 * CH, half(0)]
@@ -685,8 +682,8 @@
     vm(ROWS, 2 * CH, COLS),
     vm(ROWS + 4, CH, COLS),
     vm(2, 2, CH, COLS),
-    vm(2, CH, LANES),
-    vm(2, 6, CH, LANES),
+    vm(2, 32, LANES),
+    vm(2, 96, LANES),
     vm(CH, LANES),
     vm(CH, LANES),
     vm(COLS, COLS),

time: 64.5 us -> 62.6 us (0.971)
  Pallas kernels: 63.7 us -> 61.9 us
    pallas_call x1, Pallas kernels: 61.1 us -> 59.2 us  [body(): pl.pallas_call(kernel, out_shape=(shape((2, ROWS * CH, LANES), F32), shap...]
where the time goes in v8:
time: 62.6 us; the launch traced here: 62.5 us
  Pallas kernels  61.9 us (99%)
  between operations  0.64 us (1%)
    pallas_call x1, Pallas kernels, body(): pl.pallas_call(kernel, out_shape=(shape((2, ROWS * CH, LANES), F32), shap...  59.2 us
    pallas_call x1, Pallas kernels, body(): pl.pallas_call(finish, out_shape=(shape((CH, ROWS, COLS), BF), shape((CH,...  2.63 us

profile of v8, /device:TPU:1, one launch (start us, length us, event | category | flops | bytes accessed | tf_op | source)
XLA Modules:
  0.0 62.5 jit_solution(5642521260456275499)
XLA Ops:
  0.6 59.2 %shard_map.126 = (f32[2,1024,128]{2,1,0:T(8,128)S(1)}, f32[2,1024,128]{2,1,0:T(8,128)S(1)}, bf16[1024,128]{1,0:T(8,128)(2,1)S(1)}, bf16[8,48,128]{2,1,0:T(8,128)(2,1)S(1)}, f32[16,128]{1,0:T(8,128)S(1)}) custom-call(bf16[64,16,256]{2,1,0:T(8,128)(2,1)} %frames_hbm.1, bf16[64,128]{1,0:T(8,128)(2,1)} %bitcast.4, bf16[256,256]{1,0:T(8,128)(2,1)} %grid_mix_hbm.1, ...), custom_call_target="tpu_custom_call" | custom-call | tf_op jit(solution)/shard_map/pallas_call | solution.py:724
  59.9 2.6 %shard_map.127 = (bf16[64,16,256]{2,1,0:T(8,128)(2,1)}, bf16[64,16,256]{2,1,0:T(8,128)(2,1)}, f32[64,128]{1,0:T(8,128)}, f32[256,256]{1,0:T(8,128)}, f32[256,256...) custom-call(f32[2,1024,128]{2,1,0:T(8,128)S(1)} %get-tuple-element.19.rest, ...), custom_call_target="tpu_custom_call" | custom-call | tf_op jit(solution)/shard_map/pallas_call | solution.py:740

commit v9 on v8

--- a/solution.py
+++ b/solution.py
@@ -20,9 +20,12 @@
 NEAR = 8
 FAR = 16
 
-(G_ROW0, G_PACK0, G_ROW1, G_PACK1, G_VA, G_VB, G_VC, G_VD, G_GA, G_GB, G_GC, G_GD) = range(12)
-(G_E0, G_E1, G_E2, G_E3, G_E4, G_E5, G_E6, G_T1, G_T2, G_T3, G_T4, G_Q1, G_Q2) = range(12, 25)
-GROUPS = 25
+(G_ROW0, G_PACK0, G_ROW1, G_PACK1) = range(4)
+(G_E0, G_E1, G_E2, G_E3, G_E4, G_E5, G_E6, G_T1, G_T2, G_T3, G_T4, G_Q1, G_Q2) = range(4, 17)
+VALUES, BACKS = (0, 1), (2, 3)
+G_A, G_B, G_C, G_D = 17, 21, 25, 29
+GROUPS = 33
+QC = 16
 
 
 def dot(a, b):
@@ -76,10 +79,9 @@
     rest_out, gframe_out, early_out, tail_out, value_out,
     frames, w_in_t, grid_mix, block_mix, w_out, conv_w, cot, w_in,
     turn, xb, nb, unit, inv, dgelu, gates, bval, u3, v3, gj, gg, xt, bt, bm, gbv,
-    va, va_in, vx, vb, vb_in, vc, vc_in, vd, vd_in,
-    ga, ga_in, gx, gb, gb_in, gc, gc_in, gd, gd_in,
+    a, a_in, x32, b, b_in, c, c_in, d, d_in,
     gated, gbef, jp, row_in, pack_out, pack_in, edge_l, edge_r,
-    mixp, se, re0, e0, re1, e1, re2, e2, re3, e3, re4, re5, re6,
+    mixp, mixp_t, gather, spread, se, re0, e0, re1, e1, re2, e2, re3, e3, re4, re5, re6,
     st, rt1, t1, rt2, t2, rt3, t3, rt4, sq, rq1, q1, rq2,
     ssem, rsem, isem,
 ):
@@ -233,37 +235,44 @@
         y = dot(w, field[r + 2])
         return now + y[2 * CH :], (y[0:CH], later + y[CH : 2 * CH])
 
-    def step_b(a_in, x, b, b_in, g_a, g_b):
-        from_near(a_in, g_a)
+    def step_a(n):
+        over_near(lambda peer: a.at[n, peer], a_in.at[n, near], G_A + n)
+
+    def step_b(n):
+        arrived(a_in.at[n, pl.ds(0, NEAR - 1)], G_A + n)
 
         def widen(j, carry):
             for t in range(2):
                 for r in range(2):
-                    x[pl.ds((r * 16 + j * 2 + t) * HC, HC), :] = a_in[j, t, r].astype(F32)
+                    x32[n, pl.ds((r * 16 + j * 2 + t) * QC, QC), :] = a_in[n, j, t, r].astype(F32)
             return carry
 
         loop(NEAR, widen, unroll=8)
 
         for peer in [*far_peers, far]:
-            base = peer // 8 * (16 * HC) + lax.rem(peer, 8) * 4
+            base = peer // 8 * (16 * QC) + lax.rem(peer, 8) * 2
             slot = b_in if peer is far else b
-            for c in range(4):
-                slot[peer, :, half(c)] = x[pl.ds(base + c, 16, stride=HC), :].astype(BF)
+            for k in range(2):
+                slot[n, peer, :, half(k)] = x32[n, pl.ds(base + k, 16, stride=QC), :].astype(BF)
             if peer is not far:
-                push(b.at[peer], b_in.at[far], g_b, far_device(peer))
-
-    def step_c(mixed, c, c_in, g):
-        c[...] = mixed.astype(BF).reshape(FAR, 16, 512)
-        over_far(lambda peer: c.at[peer], c_in.at[far], g)
-        c_in[far] = c[far]
-
-    def step_d(c_in, x, d, d_in, g_c, g_d):
-        from_far(c_in, g_c)
+                push(b.at[n, peer], b_in.at[n, far], G_B + n, far_device(peer))
+
+    def table(n):
+        return b_in[n].reshape(256, 256)
+
+    def step_c(n, mix):
+        arrived(b_in.at[n, pl.ds(0, FAR - 1)], G_B + n)
+        c[n] = dot(mix[...], table(n)).astype(BF).reshape(FAR, 16, 256)
+        over_far(lambda peer: c.at[n, peer], c_in.at[n, far], G_C + n)
+        c_in[n, far] = c[n, far]
+
+    def step_d(n):
+        arrived(c_in.at[n, pl.ds(0, FAR - 1)], G_C + n)
 
         def unpick(q, carry):
             for r in range(2):
-                for c in range(4):
-                    x[pl.ds((r * HC + q * 4 + c) * 16, 16), :] = c_in[r * 8 + q, :, half(c)].astype(F32)
+                for k in range(2):
+                    x32[n, pl.ds((r * QC + q * 2 + k) * 16, 16), :] = c_in[n, r * 8 + q, :, half(k)].astype(F32)
             return carry
 
         loop(8, unpick, unroll=8)
@@ -272,19 +281,16 @@
             slot = d_in if peer is near else d
             for t in range(2):
                 for r in range(2):
-                    slot[peer, t, r] = x[pl.ds(r * HC * 16 + peer * 2 + t, HC, stride=16), :].astype(BF)
+                    slot[n, peer, t, r] = x32[n, pl.ds(r * QC * 16 + peer * 2 + t, QC, stride=16), :].astype(BF)
             if peer is not near:
-                push(d.at[peer], d_in.at[near], g_d, near_device(peer))
-
-    def order():
-        row = lax.broadcasted_iota(jnp.int32, (COLS, COLS), 0)
-        cell = lax.broadcasted_iota(jnp.int32, (COLS, COLS), 1)
+                push(d.at[n, peer], d_in.at[n, near], G_D + n, near_device(peer))
+
+    def step_e(n):
+        arrived(d_in.at[n, pl.ds(0, NEAR - 1)], G_D + n)
+
+    def order(cell, row):
         found = (row & 0xC1) | ((row & 6) << 3) | ((row & 48) >> 2) | ((row & 8) >> 2)
         return jnp.where(cell == found, 1.0, 0.0).astype(BF)
-
-    def mix_in_order():
-        swap = order()
-        return dot_nt(dot(swap, grid_mix[...]).astype(BF), swap).astype(BF)
 
     loads[0].wait()
     turn_in(cot)
@@ -318,17 +324,19 @@
         value, slope = gelu_parts(dot(w_in[HC:CH], nb[r]))
         dgelu[r, HC:CH] = slope
         value = value.astype(BF)
-        slot[peer, 0, low] = value[:, half(0)]
-        slot[peer, 1, low] = value[:, half(1)]
+        for n in VALUES:
+            for t in range(2):
+                slot[n, peer, t, low] = value[n * QC : (n + 1) * QC, half(t)]
 
     for first in range(0, NEAR, 2):
         group = [*near_peers, near][first : first + 2]
         for peer in group:
             for low in range(2):
-                value_row(va_in if peer is near else va, peer, low)
+                value_row(a_in if peer is near else a, peer, low)
         for peer in group:
             if peer is not near:
-                push(va.at[peer], va_in.at[near], G_VA, near_device(peer))
+                push(a.at[0, peer], a_in.at[0, near], G_A, near_device(peer))
+    step_a(1)
 
     def grid_gate_row(r, carry):
         value, slope = gelu_parts(dot(w_in[0:HC], nb[r]))
@@ -353,8 +361,9 @@
         up_gated = dot(w_out_t, g)
         gg[r] = up_gated
         mixed = (up_gated[0:HC] * gates[r, 0:HC].astype(F32)).astype(BF)
-        ga[r // 2, 0, r % 2] = mixed[:, half(0)]
-        ga[r // 2, 1, r % 2] = mixed[:, half(1)]
+        for n in range(2):
+            for t in range(2):
+                a[2 + n, r // 2, t, r % 2] = mixed[n * QC : (n + 1) * QC, half(t)]
         return carry
 
     carry = conv_start(back_w, u3)
@@ -365,11 +374,13 @@
 
             @pl.when(peer != near)
             def _():
-                push(ga.at[peer], ga_in.at[near], G_GA, near_device(peer))
-
-    ga_in[near] = ga[near]
-
-    step_b(va_in, vx, vb, vb_in, G_VA, G_VB)
+                push(a.at[2, peer], a_in.at[2, near], G_A + 2, near_device(peer))
+
+    step_a(3)
+    for n in BACKS:
+        a_in[n, near] = a[n, near]
+    step_b(0)
+    step_b(1)
 
     def block_gate_row(r, carry):
         value, slope = gelu_parts(dot(w_in[CH:], nb[r]))
@@ -380,7 +391,13 @@
         return carry
 
     loop(ROWS, block_gate_row, unroll=8)
-    mixp[...] = mix_in_order()
+    down_axis = lax.broadcasted_iota(jnp.int32, (COLS, COLS), 0)
+    along_axis = lax.broadcasted_iota(jnp.int32, (COLS, COLS), 1)
+    gather[...] = order(along_axis, down_axis)
+    spread[...] = order(down_axis, along_axis)
+    mixp[...] = dot(dot(gather[...], grid_mix[...]).astype(BF), spread[...]).astype(BF)
+    mixp_t[...] = dot(dot_nt(gather[...], grid_mix[...]).astype(BF), spread[...]).astype(BF)
+    step_c(0, mixp)
 
     def put(ref):
         def store(k, t, value):
@@ -393,9 +410,9 @@
     mixed = dot_nt(values, block_mix[...]).astype(BF)
     swap_granules(lambda k, t: mixed[k * HC : (k + 1) * HC, half(t)], put(bm), HC)
 
-    step_b(ga_in, gx, gb, gb_in, G_GA, G_GB)
-    from_far(vb_in, G_VB)
-    step_c(dot(mixp[...], vb_in[...].reshape(256, 512)), vc, vc_in, G_VC)
+    step_c(1, mixp)
+    step_b(2)
+    step_b(3)
 
     def block_back(k, t):
         return (gg[k, HC:, half(t)] * gates[k, HC:, half(t)].astype(F32)).astype(BF)
@@ -419,59 +436,56 @@
     for k in (0, 1, ROWS + 2, ROWS + 3):
         jp[k] = jnp.zeros((CH, COLS), BF)
 
-    from_far(gb_in, G_GB)
-    back = gb_in[...].reshape(256, 512)
-    step_c(dot_tn(mixp[...], back), gc, gc_in, G_GC)
-    step_d(vc_in, vx, vd, vd_in, G_VC, G_VD)
-
-    part_grid = dot_nt(back, vb_in[...].reshape(256, 512)).astype(BF)
-    part_grid = dot(dot_tn(order(), part_grid).astype(BF), order()).astype(BF)
+    step_d(0)
+    step_d(1)
+    step_c(2, mixp_t)
+    step_c(3, mixp_t)
+
+    part_grid = (dot_nt(table(2), table(0)) + dot_nt(table(3), table(1))).astype(BF)
+    part_grid = dot(dot(spread[...], part_grid).astype(BF), gather[...]).astype(BF)
     se[0:COLS] = part_grid[:, half(0)]
     se[COLS : 2 * COLS] = part_grid[:, half(1)]
     push(se.at[pl.ds(pl.multiple_of(512 - mine, 512), 512)], re0, G_E0, near_device(twin))
 
-    step_d(gc_in, gx, gd, gd_in, G_GC, G_GD)
-
-    from_near(vd_in, G_VD)
-
-    def returned(ref, r):
-        return [ref[r // 2, t, lax.rem(r, 2)].astype(F32) for t in range(2)]
-
-    def joined_row(r, pack):
-        grid_mixed = returned(vd_in, r)
-        for t in range(2):
-            gates_t = gates[r, :, half(t)].astype(F32)
-            gated[r, 0:HC, half(t)] = (gates_t[0:HC] * (grid_mixed[t] + 1.0)).astype(BF)
-            gated[r, HC:, half(t)] = (gates_t[HC:] * (bm[r, :, half(t)].astype(F32) + 1.0)).astype(BF)
-        j = (xb[r].astype(F32) + dot(w_out[...], gated[r])).astype(BF)
-        jp[r + 2] = j
-        v3[r + 1, CH : 2 * CH] = j
-        return edges(pack, j[:, half(0)], j[:, half(1)], r)
-
-    pack = loop(ROWS, joined_row, jnp.zeros((CH, LANES), BF), unroll=8)
-    send_halo(v3, pack, 1, G_ROW1, G_PACK1)
+    step_e(0)
+    step_e(1)
 
     arrived(re0, G_E0)
     e0[...] = (se[pl.ds(pl.multiple_of(mine, 512), 512)].astype(F32) + re0[...].astype(F32)).astype(BF)
     over_y(lambda peer: e0.at[pl.ds(pl.multiple_of(peer * 128, 128), 128)], re1.at[level], G_E1)
     re1[level] = e0[pl.ds(pl.multiple_of(level * 128, 128), 128)]
 
+    def returned(chains, r):
+        return [
+            jnp.concatenate([d_in[n, r // 2, t, lax.rem(r, 2)] for n in chains], axis=0).astype(F32) for t in range(2)
+        ]
+
+    def joined_row(r, carry):
+        pack, p_in, p_out = carry
+        grid_mixed = returned(VALUES, r)
+        for t in range(2):
+            gates_t = gates[r, :, half(t)].astype(F32)
+            more = grid_mixed[t] + 1.0
+            gated[r, 0:HC, half(t)] = (gates_t[0:HC] * more).astype(BF)
+            gated[r, HC:, half(t)] = (gates_t[HC:] * (bm[r, :, half(t)].astype(F32) + 1.0)).astype(BF)
+            gbef[r, 0:HC, half(t)] = (dgelu[r, 0:HC, half(t)] * (gg[r, 0:HC, half(t)] * more)).astype(BF)
+        j = (xb[r].astype(F32) + dot(w_out[...], gated[r])).astype(BF)
+        jp[r + 2] = j
+        v3[r + 1, CH : 2 * CH] = j
+        pack = edges(pack, j[:, half(0)], j[:, half(1)], r)
+        return pack, p_in + dot_nt(nb[r], gbef[r]), p_out + dot_nt(gj[r], gated[r])
+
+    pack, p_in, p_out = loop(
+        ROWS,
+        joined_row,
+        (jnp.zeros((CH, LANES), BF), jnp.zeros((CH, 2 * CH), F32), jnp.zeros((CH, CH), F32)),
+        unroll=8,
+    )
+
     def conv_row(p, total):
         return total + dot_nt(u3[p], jp[pl.ds(p, 3)].reshape(3 * CH, COLS))
 
     p_conv = loop(ROWS + 2, conv_row, jnp.zeros((3 * CH, 3 * CH), F32), unroll=9)
-
-    def gate_before_row(r, carry):
-        p_in, p_out = carry
-        grid_mixed = returned(vd_in, r)
-        for t in range(2):
-            slope = dgelu[r, 0:HC, half(t)]
-            gbef[r, 0:HC, half(t)] = (slope * (gg[r, 0:HC, half(t)] * (grid_mixed[t] + 1.0))).astype(BF)
-        return p_in + dot_nt(nb[r], gbef[r]), p_out + dot_nt(gj[r], gated[r])
-
-    p_in, p_out = loop(
-        ROWS, gate_before_row, (jnp.zeros((CH, 2 * CH), F32), jnp.zeros((CH, CH), F32)), unroll=4
-    )
     st[0 : 3 * CH] = p_conv[:, half(0)].astype(BF)
     st[3 * CH : 4 * CH] = p_in.astype(BF)
     third = p_conv[:, 2 * CH :]
@@ -480,19 +494,10 @@
     ).astype(BF)
     over_near(lambda peer: st.at[pl.ds(pl.multiple_of(peer * 48, 16), 48)], rt1.at[near], G_T1)
     rt1[near] = st[pl.ds(pl.multiple_of(near * 48, 16), 48)]
-
-    from_near(gd_in, G_GD)
-
-    def value_before_row(r, total):
-        grid_back = returned(gd_in, r)
-        for t in range(2):
-            gbef[r, HC:CH, half(t)] = (dgelu[r, HC:CH, half(t)] * grid_back[t]).astype(BF)
-        return total + dot_nt(gbef[r, HC:CH], nb[r])
-
-    p_value = loop(ROWS, value_before_row, jnp.zeros((HC, CH), F32), unroll=4)
-    sq[...] = jnp.concatenate([p_value[0:16], p_value[16:]], axis=1).astype(BF)
-    over_near(lambda peer: sq, rq1.at[near], G_Q1)
-    rq1[near] = sq[...]
+    send_halo(v3, pack, 1, G_ROW1, G_PACK1)
+
+    step_d(2)
+    step_d(3)
 
     arrived(re1.at[pl.ds(0, 3)], G_E1)
     total = re1[0].astype(F32)
@@ -501,6 +506,56 @@
     e1[...] = total
     over_x(lambda peer: e1.at[pl.ds(pl.multiple_of(peer * 32, 32), 32)], re2.at[across], G_E2)
     re2[across] = e1[pl.ds(pl.multiple_of(across * 32, 32), 32)]
+
+    take_halo(v3, 1, G_ROW1, G_PACK1)
+
+    from_near(rt1, G_T1)
+    total = rt1[0].astype(F32)
+    for k in range(1, NEAR):
+        total = total + rt1[k].astype(F32)
+    t1[...] = total.astype(BF)
+    over_x(lambda peer: t1, rt2.at[across], G_T2)
+    rt2[across] = t1[...]
+
+    conv_k = jnp.concatenate(
+        [jnp.concatenate([conv_w[a, b] for b in range(3)], axis=1) for a in range(3)], axis=0
+    )
+
+    def out_row(r, carry):
+        total, carry = conv_step(conv_k, v3, r, carry)
+        total = total + v3[r + 1, CH : 2 * CH].astype(F32)
+        for t in range(2):
+            rest_out[t, pl.ds(r * CH, CH), :] = total[:, half(t)]
+        return carry
+
+    carry = loop(ROWS // 2, out_row, conv_start(conv_k, v3), unroll=8)
+
+    arrived(re2.at[pl.ds(0, 3)], G_E2)
+    e2[...] = re2[0] + re2[1] + re2[2] + re2[3]
+    over_z(lambda peer: e2, re3.at[deep], G_E3)
+    re3[deep] = e2[...]
+
+    step_e(2)
+    step_e(3)
+
+    def value_before_row(r, total):
+        grid_back = returned(BACKS, r)
+        for t in range(2):
+            gbef[r, HC:CH, half(t)] = (dgelu[r, HC:CH, half(t)] * grid_back[t]).astype(BF)
+        return total + dot_nt(gbef[r, HC:CH], nb[r])
+
+    p_value = loop(ROWS, value_before_row, jnp.zeros((HC, CH), F32), unroll=4)
+    sq[...] = jnp.concatenate([p_value[0:16], p_value[16:]], axis=1).astype(BF)
+    over_near(lambda peer: sq, rq1.at[near], G_Q1)
+    rq1[near] = sq[...]
+
+    arrived(rt2.at[pl.ds(0, 3)], G_T2)
+    total = rt2[0].astype(F32)
+    for k in range(1, 4):
+        total = total + rt2[k].astype(F32)
+    t2[...] = total.astype(BF)
+    over_z(lambda peer: t2, rt3.at[deep], G_T3)
+    rt3[deep] = t2[...]
 
     def frame_row(r, carry):
         normed = dot(w_in_t[...], gbef[r])
@@ -514,14 +569,6 @@
 
     loop(ROWS, frame_row, unroll=8)
 
-    from_near(rt1, G_T1)
-    total = rt1[0].astype(F32)
-    for k in range(1, NEAR):
-        total = total + rt1[k].astype(F32)
-    t1[...] = total.astype(BF)
-    over_x(lambda peer: t1, rt2.at[across], G_T2)
-    rt2[across] = t1[...]
-
     from_near(rq1, G_Q1)
     total = rq1[0].astype(F32)
     for k in range(1, NEAR):
@@ -530,42 +577,11 @@
     over_far(lambda peer: q1, rq2.at[far], G_Q2)
     rq2[far] = q1[...]
 
-    arrived(re2.at[pl.ds(0, 3)], G_E2)
-    e2[...] = re2[0] + re2[1] + re2[2] + re2[3]
-    over_z(lambda peer: e2, re3.at[deep], G_E3)
-    re3[deep] = e2[...]
-
-    take_halo(v3, 1, G_ROW1, G_PACK1)
-
-    arrived(rt2.at[pl.ds(0, 3)], G_T2)
-    total = rt2[0].astype(F32)
-    for k in range(1, 4):
-        total = total + rt2[k].astype(F32)
-    t2[...] = total.astype(BF)
-    over_z(lambda peer: t2, rt3.at[deep], G_T3)
-    rt3[deep] = t2[...]
-
     arrived(re3.at[pl.ds(0, 3)], G_E3)
     e3[...] = (re3[0] + re3[1] + re3[2] + re3[3]).astype(BF)
     over_x(lambda peer: e3, re4.at[across], G_E4)
     re4[across] = e3[...]
 
-    conv_k = jnp.concatenate(
-        [jnp.concatenate([conv_w[a, b] for b in range(3)], axis=1) for a in range(3)], axis=0
-    )
-
-    def out_row(r, carry):
-        total, carry = conv_step(conv_k, v3, r, carry)
-        total = total + v3[r + 1, CH : 2 * CH].astype(F32)
-        for t in range(2):
-            rest_out[t, pl.ds(r * CH, CH), :] = total[:, half(t)]
-        return carry
-
-    carry = loop(ROWS // 2, out_row, conv_start(conv_k, v3), unroll=8)
-
-    arrived(re4.at[pl.ds(0, 3)], G_E4)
-    over_y(lambda peer: re4, re5.at[level], G_E5)
-    re5[level] = re4[...]
     arrived(rt3.at[pl.ds(0, 3)], G_T3)
     total = rt3[0].astype(F32)
     for k in range(1, 4):
@@ -573,6 +589,11 @@
     t3[...] = total.astype(BF)
     over_near(lambda peer: t3, rt4.at[near], G_T4)
     rt4[near] = t3[...]
+
+
+    arrived(re4.at[pl.ds(0, 3)], G_E4)
+    over_y(lambda peer: re4, re5.at[level], G_E5)
+    re5[level] = re4[...]
 
     loop(ROWS // 2, lambda r, carry: out_row(r + ROWS // 2, carry), carry, unroll=8)
 
@@ -593,15 +614,12 @@
     for which, g_row, g_pack in ((0, G_ROW0, G_PACK0), (1, G_ROW1, G_PACK1)):
         gone(row_in.at[which], g_row)
         gone(pack_in.at[which], g_pack)
-    for ref, g in (
-        (va_in, G_VA), (vd_in, G_VD), (ga_in, G_GA), (gd_in, G_GD),
-        (rt1, G_T1), (rt4, G_T4), (rq1, G_Q1),
-    ):
+    for n in VALUES + BACKS:
+        for ref, count, g in ((a_in, NEAR, G_A), (b_in, FAR, G_B), (c_in, FAR, G_C), (d_in, NEAR, G_D)):
+            gone(ref.at[n, pl.ds(0, count - 1)], g + n)
+    for ref, g in ((rt1, G_T1), (rt4, G_T4), (rq1, G_Q1)):
         gone(ref.at[pl.ds(0, NEAR - 1)], g)
-    for ref, g in (
-        (vb_in, G_VB), (vc_in, G_VC), (gb_in, G_GB), (gc_in, G_GC), (rq2, G_Q2),
-    ):
-        gone(ref.at[pl.ds(0, FAR - 1)], g)
+    gone(rq2.at[pl.ds(0, FAR - 1)], G_Q2)
     gone(re0, G_E0)
     for ref, g in ((re1, G_E1), (re2, G_E2), (re3, G_E3), (re4, G_E4), (re5, G_E5), (rt2, G_T2), (rt3, G_T3)):
         gone(ref.at[pl.ds(0, 3)], g)
@@ -646,9 +664,9 @@
 
 
 def exchange():
-    message_w = vm(NW, 2, 2, HC, LANES)
-    message_a = vm(NA, 16, 512)
-    return [message_w, message_w, vm(2 * 16 * HC, LANES, dtype=F32)] + [message_a] * 4 + [message_w] * 2
+    message_w = vm(4, NEAR, 2, 2, QC, LANES)
+    message_a = vm(4, FAR, 16, 256)
+    return [message_w, message_w, vm(4, 2 * 16 * QC, LANES, dtype=F32)] + [message_a] * 4 + [message_w] * 2
 
 
 SCRATCH = [
@@ -677,7 +695,6 @@
     vm(ROWS, HC, COLS),
     vm(ROWS, HC, COLS),
     *exchange(),
-    *exchange(),
     vm(ROWS, CH, COLS),
     vm(ROWS, 2 * CH, COLS),
     vm(ROWS + 4, CH, COLS),
@@ -686,6 +703,9 @@
     vm(2, 96, LANES),
     vm(CH, LANES),
     vm(CH, LANES),
+    vm(COLS, COLS),
+    vm(COLS, COLS),
+    vm(COLS, COLS),
     vm(COLS, COLS),
     vm(4 * COLS, LANES),
     vm(512, LANES),

time: 62.6 us -> 60.3 us (0.963)
  Pallas kernels: 61.9 us -> 59.5 us
    pallas_call x1, Pallas kernels: 59.2 us -> 56.9 us  [body(): pl.pallas_call(kernel, out_shape=(shape((2, ROWS * CH, LANES), F32), shap...]
where the time goes in v9:
time: 60.3 us; the launch traced here: 60.2 us
  Pallas kernels  59.5 us (99%)
  between operations  0.64 us (1%)
    pallas_call x1, Pallas kernels, body(): pl.pallas_call(kernel, out_shape=(shape((2, ROWS * CH, LANES), F32), shap...  56.9 us
    pallas_call x1, Pallas kernels, body(): pl.pallas_call(finish, out_shape=(shape((CH, ROWS, COLS), BF), shape((CH,...  2.63 us

profile of v9, /device:TPU:1, one launch (start us, length us, event | category | flops | bytes accessed | tf_op | source)
XLA Modules:
  0.0 60.2 jit_solution(2013027881295132655)
XLA Ops:
  0.6 56.9 %shard_map.126 = (f32[2,1024,128]{2,1,0:T(8,128)S(1)}, f32[2,1024,128]{2,1,0:T(8,128)S(1)}, bf16[1024,128]{1,0:T(8,128)(2,1)S(1)}, bf16[8,48,128]{2,1,0:T(8,128)(2,1)S(1)}, f32[16,128]{1,0:T(8,128)S(1)}) custom-call(bf16[64,16,256]{2,1,0:T(8,128)(2,1)} %frames_hbm.1, bf16[64,128]{1,0:T(8,128)(2,1)} %bitcast.4, bf16[256,256]{1,0:T(8,128)(2,1)} %grid_mix_hbm.1, ...), custom_call_target="tpu_custom_call" | custom-call | tf_op jit(solution)/shard_map/pallas_call | solution.py:744
  57.5 2.6 %shard_map.127 = (bf16[64,16,256]{2,1,0:T(8,128)(2,1)}, bf16[64,16,256]{2,1,0:T(8,128)(2,1)}, f32[64,128]{1,0:T(8,128)}, f32[256,256]{1,0:T(8,128)}, f32[256,256...) custom-call(f32[2,1024,128]{2,1,0:T(8,128)S(1)} %get-tuple-element.19.rest, ...), custom_call_target="tpu_custom_call" | custom-call | tf_op jit(solution)/shard_map/pallas_call | solution.py:760

commit v10 on v9

--- a/solution.py
+++ b/solution.py
@@ -127,13 +127,16 @@
     far_peers = [lax.rem(far + k, FAR) for k in range(1, FAR)]
     twin = near + 1 - 2 * lax.rem(near, 2)
 
+    near_places = [near_device(peer) for peer in near_peers]
+    far_places = [far_device(peer) for peer in far_peers]
+
     def over_near(src_of, dst, g):
-        for peer in near_peers:
-            push(src_of(peer), dst, g, near_device(peer))
+        for peer, place in zip(near_peers, near_places):
+            push(src_of(peer), dst, g, place)
 
     def over_far(src_of, dst, g):
-        for peer in far_peers:
-            push(src_of(peer), dst, g, far_device(peer))
+        for peer, place in zip(far_peers, far_places):
+            push(src_of(peer), dst, g, place)
 
     def over_x(src_of, dst, g):
         for k in range(1, 4):
@@ -249,13 +252,13 @@
 
         loop(NEAR, widen, unroll=8)
 
-        for peer in [*far_peers, far]:
+        for peer, place in zip([*far_peers, far], [*far_places, None]):
             base = peer // 8 * (16 * QC) + lax.rem(peer, 8) * 2
             slot = b_in if peer is far else b
             for k in range(2):
                 slot[n, peer, :, half(k)] = x32[n, pl.ds(base + k, 16, stride=QC), :].astype(BF)
             if peer is not far:
-                push(b.at[n, peer], b_in.at[n, far], G_B + n, far_device(peer))
+                push(b.at[n, peer], b_in.at[n, far], G_B + n, place)
 
     def table(n):
         return b_in[n].reshape(256, 256)
@@ -277,13 +280,13 @@
 
         loop(8, unpick, unroll=8)
 
-        for peer in [*near_peers, near]:
+        for peer, place in zip([*near_peers, near], [*near_places, None]):
             slot = d_in if peer is near else d
             for t in range(2):
                 for r in range(2):
                     slot[n, peer, t, r] = x32[n, pl.ds(r * QC * 16 + peer * 2 + t, QC, stride=16), :].astype(BF)
             if peer is not near:
-                push(d.at[n, peer], d_in.at[n, near], G_D + n, near_device(peer))
+                push(d.at[n, peer], d_in.at[n, near], G_D + n, place)
 
     def step_e(n):
         arrived(d_in.at[n, pl.ds(0, NEAR - 1)], G_D + n)
@@ -461,7 +464,7 @@
         ]
 
     def joined_row(r, carry):
-        pack, p_in, p_out = carry
+        pack, p_in, p_out, p_conv = carry
         grid_mixed = returned(VALUES, r)
         for t in range(2):
             gates_t = gates[r, :, half(t)].astype(F32)
@@ -473,19 +476,23 @@
         jp[r + 2] = j
         v3[r + 1, CH : 2 * CH] = j
         pack = edges(pack, j[:, half(0)], j[:, half(1)], r)
-        return pack, p_in + dot_nt(nb[r], gbef[r]), p_out + dot_nt(gj[r], gated[r])
-
-    pack, p_in, p_out = loop(
+        return pack, p_in + dot_nt(nb[r], gbef[r]), p_out + dot_nt(gj[r], gated[r]), p_conv + conv_plane(r)
+
+    def conv_plane(p):
+        return dot_nt(u3[p], jp[pl.ds(p, 3)].reshape(3 * CH, COLS))
+
+    pack, p_in, p_out, p_conv = loop(
         ROWS,
         joined_row,
-        (jnp.zeros((CH, LANES), BF), jnp.zeros((CH, 2 * CH), F32), jnp.zeros((CH, CH), F32)),
+        (
+            jnp.zeros((CH, LANES), BF),
+            jnp.zeros((CH, 2 * CH), F32),
+            jnp.zeros((CH, CH), F32),
+            jnp.zeros((3 * CH, 3 * CH), F32),
+        ),
         unroll=8,
     )
-
-    def conv_row(p, total):
-        return total + dot_nt(u3[p], jp[pl.ds(p, 3)].reshape(3 * CH, COLS))
-
-    p_conv = loop(ROWS + 2, conv_row, jnp.zeros((3 * CH, 3 * CH), F32), unroll=9)
+    p_conv = p_conv + conv_plane(ROWS) + conv_plane(ROWS + 1)
     st[0 : 3 * CH] = p_conv[:, half(0)].astype(BF)
     st[3 * CH : 4 * CH] = p_in.astype(BF)
     third = p_conv[:, 2 * CH :]
@@ -496,9 +503,6 @@
     rt1[near] = st[pl.ds(pl.multiple_of(near * 48, 16), 48)]
     send_halo(v3, pack, 1, G_ROW1, G_PACK1)
 
-    step_d(2)
-    step_d(3)
-
     arrived(re1.at[pl.ds(0, 3)], G_E1)
     total = re1[0].astype(F32)
     for k in range(1, 4):
@@ -507,7 +511,15 @@
     over_x(lambda peer: e1.at[pl.ds(pl.multiple_of(peer * 32, 32), 32)], re2.at[across], G_E2)
     re2[across] = e1[pl.ds(pl.multiple_of(across * 32, 32), 32)]
 
+    step_d(2)
+    step_d(3)
+
     take_halo(v3, 1, G_ROW1, G_PACK1)
+
+    arrived(re2.at[pl.ds(0, 3)], G_E2)
+    e2[...] = re2[0] + re2[1] + re2[2] + re2[3]
+    over_z(lambda peer: e2, re3.at[deep], G_E3)
+    re3[deep] = e2[...]
 
     from_near(rt1, G_T1)
     total = rt1[0].astype(F32)
@@ -530,10 +542,10 @@
 
     carry = loop(ROWS // 2, out_row, conv_start(conv_k, v3), unroll=8)
 
-    arrived(re2.at[pl.ds(0, 3)], G_E2)
-    e2[...] = re2[0] + re2[1] + re2[2] + re2[3]
-    over_z(lambda peer: e2, re3.at[deep], G_E3)
-    re3[deep] = e2[...]
+    arrived(re3.at[pl.ds(0, 3)], G_E3)
+    e3[...] = (re3[0] + re3[1] + re3[2] + re3[3]).astype(BF)
+    over_x(lambda peer: e3, re4.at[across], G_E4)
+    re4[across] = e3[...]
 
     step_e(2)
     step_e(3)
@@ -548,6 +560,10 @@
     sq[...] = jnp.concatenate([p_value[0:16], p_value[16:]], axis=1).astype(BF)
     over_near(lambda peer: sq, rq1.at[near], G_Q1)
     rq1[near] = sq[...]
+
+    arrived(re4.at[pl.ds(0, 3)], G_E4)
+    over_y(lambda peer: re4, re5.at[level], G_E5)
+    re5[level] = re4[...]
 
     arrived(rt2.at[pl.ds(0, 3)], G_T2)
     total = rt2[0].astype(F32)
@@ -577,11 +593,6 @@
     over_far(lambda peer: q1, rq2.at[far], G_Q2)
     rq2[far] = q1[...]
 
-    arrived(re3.at[pl.ds(0, 3)], G_E3)
-    e3[...] = (re3[0] + re3[1] + re3[2] + re3[3]).astype(BF)
-    over_x(lambda peer: e3, re4.at[across], G_E4)
-    re4[across] = e3[...]
-
     arrived(rt3.at[pl.ds(0, 3)], G_T3)
     total = rt3[0].astype(F32)
     for k in range(1, 4):
@@ -591,15 +602,11 @@
     rt4[near] = t3[...]
 
 
-    arrived(re4.at[pl.ds(0, 3)], G_E4)
-    over_y(lambda peer: re4, re5.at[level], G_E5)
-    re5[level] = re4[...]
-
-    loop(ROWS // 2, lambda r, carry: out_row(r + ROWS // 2, carry), carry, unroll=8)
-
     arrived(re5.at[pl.ds(0, 3)], G_E5)
     push(re5, re6, G_E6, near_device(twin))
     early_out[pl.ds(pl.multiple_of(mine, 512), 512)] = re5[...].reshape(512, LANES)
+
+    loop(ROWS // 2, lambda r, carry: out_row(r + ROWS // 2, carry), carry, unroll=8)
 
     from_far(rq2, G_Q2)
     total = rq2[0].astype(F32)
@@ -626,29 +633,45 @@
     gone(re6, G_E6)
 
 
-def finish(
-    rest, gframe, early, tail, value,
-    restored, grad_frames, grad_w_in_t, grad_grid, grad_block, grad_w_out, grad_conv,
-):
+def finish(rest, gframe, early, tail, value, *refs):
+    outs, sem = (refs[:7], refs[7:14]), refs[14]
+    restored, grad_frames, grad_w_in_t, grad_grid, grad_block, grad_w_out, grad_conv = outs[1]
+    copies = []
+
+    def leave(k, part=None):
+        src, dst = outs[1][k], outs[0][k]
+        if part is not None:
+            src, dst = src.at[part], dst.at[part]
+        copies.append(pltpu.make_async_copy(src, dst, sem.at[len(copies)]))
+        copies[-1].start()
+
+    def turn_out(src, dst, k):
+        for first in range(0, CH, CH // 2):
+
+            def channel(c, carry):
+                for t in range(2):
+                    dst[first + c, :, half(t)] = src[t, pl.ds(first + c, ROWS, stride=CH), :].astype(BF)
+                return carry
+
+            loop(CH // 2, channel, unroll=16)
+            leave(k, pl.ds(first, CH // 2))
+
     scale = float(ROWS * NA * COLS * NW) ** (-0.5)
-
-    def channel(c, carry):
-        for src, dst in ((rest, restored), (gframe, grad_frames)):
-            for t in range(2):
-                dst[c, :, half(t)] = src[t, pl.ds(c, ROWS, stride=CH), :].astype(BF)
-        return carry
-
-    loop(CH, channel, unroll=8)
-
     for k in range(2):
         grad_grid[:, half(k)] = early[k * COLS : (k + 1) * COLS].astype(F32) * scale
         grad_block[:, half(k)] = early[(2 + k) * COLS : (3 + k) * COLS].astype(F32) * scale
+    leave(3)
+    leave(4)
+    turn_out(gframe, grad_frames, 1)
+    turn_out(rest, restored, 0)
     quarter = value[...] * scale
     zeros = jnp.zeros((HC, CH), F32)
     quarter = jnp.concatenate([zeros, quarter[:, :CH], quarter[:, CH:], zeros, zeros], axis=0)
     grad_w_in_t[...] = tail[3 * CH : 4 * CH].astype(F32) * scale + quarter.T
+    leave(2)
     last = tail[4 * CH :].astype(F32) * scale
     grad_w_out[...] = last[CH:, CH:]
+    leave(5)
     for b in range(3):
         rows = slice((2 - b) * CH, (3 - b) * CH)
         pair = tail[rows].astype(F32) * scale
@@ -657,6 +680,9 @@
     grad_conv[2, 2] = last[:CH, :CH]
     grad_conv[2, 1] = last[CH:, :CH]
     grad_conv[2, 0] = last[:CH, CH:]
+    leave(6)
+    for copy in copies:
+        copy.wait()
 
 
 def vm(*shape, dtype=BF):
@@ -769,7 +795,17 @@
             shape((3, 3, CH, CH), F32),
         ),
         in_specs=[vmem] * 5,
-        out_specs=(vmem,) * 7,
+        out_specs=(pl.BlockSpec(memory_space=pl.ANY),) * 7,
+        scratch_shapes=[
+            vm(CH, ROWS, COLS),
+            vm(CH, ROWS, COLS),
+            vm(CH, 2 * CH, dtype=F32),
+            vm(COLS, COLS, dtype=F32),
+            vm(COLS, COLS, dtype=F32),
+            vm(CH, CH, dtype=F32),
+            vm(3, 3, CH, CH, dtype=F32),
+            pltpu.SemaphoreType.DMA((9,)),
+        ],
         compiler_params=pltpu.CompilerParams(vmem_limit_bytes=16 * 1024 * 1024),
     )(rest, gframe, early, tail.reshape(6 * CH, LANES), value)
     return restored, grad_frames, grad_w_in_t.T, grad_grid, grad_block, grad_w_out, grad_conv

time: 60.3 us -> 61.2 us (1.015)
  Pallas kernels: 59.5 us -> 60.5 us
    pallas_call x1, Pallas kernels: 56.9 us -> 58.2 us  [body(): pl.pallas_call(kernel, out_shape=(shape((2, ROWS * CH, LANES), F32), shap...]
where the time goes in v10:
time: 61.2 us; the launch traced here: 61.1 us
  Pallas kernels  60.5 us (99%)
  between operations  0.64 us (1%)
    pallas_call x1, Pallas kernels, body(): pl.pallas_call(kernel, out_shape=(shape((2, ROWS * CH, LANES), F32), shap...  58.2 us
    pallas_call x1, Pallas kernels, body(): pl.pallas_call(finish, out_shape=(shape((CH, ROWS, COLS), BF), shape((CH,...  2.26 us

profile of v10, /device:TPU:1, one launch (start us, length us, event | category | flops | bytes accessed | tf_op | source)
XLA Modules:
  0.0 61.1 jit_solution(5259839614310176101)
XLA Ops:
  0.6 58.2 %shard_map.126 = (f32[2,1024,128]{2,1,0:T(8,128)S(1)}, f32[2,1024,128]{2,1,0:T(8,128)S(1)}, bf16[1024,128]{1,0:T(8,128)(2,1)S(1)}, bf16[8,48,128]{2,1,0:T(8,128)(2,1)S(1)}, f32[16,128]{1,0:T(8,128)S(1)}) custom-call(bf16[64,16,256]{2,1,0:T(8,128)(2,1)} %frames_hbm.1, bf16[64,128]{1,0:T(8,128)(2,1)} %bitcast.4, bf16[256,256]{1,0:T(8,128)(2,1)} %grid_mix_hbm.1, ...), custom_call_target="tpu_custom_call" | custom-call | tf_op jit(solution)/shard_map/pallas_call | solution.py:770
  58.9 2.3 %shard_map.127 = (bf16[64,16,256]{2,1,0:T(8,128)(2,1)}, bf16[64,16,256]{2,1,0:T(8,128)(2,1)}, f32[64,128]{1,0:T(8,128)}, f32[256,256]{1,0:T(8,128)}, f32[256,256...) custom-call(f32[2,1024,128]{2,1,0:T(8,128)S(1)} %get-tuple-element.19.rest, ...), custom_call_target="tpu_custom_call" | custom-call | tf_op jit(solution)/shard_map/pallas_call | solution.py:786

commit v11 on v10

--- a/solution.py
+++ b/solution.py
@@ -96,9 +96,9 @@
         pltpu.make_async_copy(src, dst, isem.at[k])
         for k, (src, dst) in enumerate(
             [
-                (cot_hbm, cot),
                 (frames_hbm, frames),
                 (w_in_t_hbm, w_in_t),
+                (cot_hbm, cot),
                 (conv_w_hbm, conv_w),
                 (w_out_hbm, w_out),
                 (block_mix_hbm, block_mix),
@@ -296,20 +296,7 @@
         return jnp.where(cell == found, 1.0, 0.0).astype(BF)
 
     loads[0].wait()
-    turn_in(cot)
-
-    def cot_row(r, pack):
-        t0, t1 = turned(r, 0).astype(BF), turned(r, 1).astype(BF)
-        u3[r + 1, CH : 2 * CH, half(0)] = t0
-        u3[r + 1, CH : 2 * CH, half(1)] = t1
-        return edges(pack, t0, t1, r)
-
-    pack = loop(ROWS, cot_row, jnp.zeros((CH, LANES), BF), unroll=8)
-    pl.semaphore_wait(barrier, len(peers))
-    send_halo(u3, pack, 0, G_ROW0, G_PACK0)
-
     loads[1].wait()
-    loads[2].wait()
     turn_in(frames)
     w_in[...] = w_in_t[...].astype(F32).T.astype(BF)
 
@@ -336,10 +323,24 @@
         for peer in group:
             for low in range(2):
                 value_row(a_in if peer is near else a, peer, low)
+        if first == 0:
+            pl.semaphore_wait(barrier, len(peers))
         for peer in group:
             if peer is not near:
                 push(a.at[0, peer], a_in.at[0, near], G_A, near_device(peer))
     step_a(1)
+
+    loads[2].wait()
+    turn_in(cot)
+
+    def cot_row(r, pack):
+        t0, t1 = turned(r, 0).astype(BF), turned(r, 1).astype(BF)
+        u3[r + 1, CH : 2 * CH, half(0)] = t0
+        u3[r + 1, CH : 2 * CH, half(1)] = t1
+        return edges(pack, t0, t1, r)
+
+    pack = loop(ROWS, cot_row, jnp.zeros((CH, LANES), BF), unroll=8)
+    send_halo(u3, pack, 0, G_ROW0, G_PACK0)
 
     def grid_gate_row(r, carry):
         value, slope = gelu_parts(dot(w_in[0:HC], nb[r]))
@@ -349,8 +350,24 @@
 
     loop(ROWS, grid_gate_row, unroll=8)
 
+    def block_gate_row(r, carry):
+        value, slope = gelu_parts(dot(w_in[CH:], nb[r]))
+        dgelu[r, CH:] = slope
+        value = value.astype(BF)
+        gates[r, HC:CH] = value[0:HC]
+        bval[r] = value[HC:]
+        return carry
+
+    loop(ROWS, block_gate_row, unroll=8)
     for load in loads[3:]:
         load.wait()
+    down_axis = lax.broadcasted_iota(jnp.int32, (COLS, COLS), 0)
+    along_axis = lax.broadcasted_iota(jnp.int32, (COLS, COLS), 1)
+    gather[...] = order(along_axis, down_axis)
+    spread[...] = order(down_axis, along_axis)
+    mixp[...] = dot(dot(gather[...], grid_mix[...]).astype(BF), spread[...]).astype(BF)
+    mixp_t[...] = dot(dot_nt(gather[...], grid_mix[...]).astype(BF), spread[...]).astype(BF)
+
     back_w = jnp.concatenate(
         [jnp.concatenate([conv_w[2 - a, 2 - b] for a in range(3)], axis=1) for b in range(3)], axis=0
     ).astype(F32).T.astype(BF)
@@ -369,8 +386,11 @@
                 a[2 + n, r // 2, t, r % 2] = mixed[n * QC : (n + 1) * QC, half(t)]
         return carry
 
+    step_b(0)
     carry = conv_start(back_w, u3)
     for first in range(0, NEAR, 2):
+        if first == NEAR // 2:
+            step_b(1)
         for r in range(2 * first, 2 * first + 4):
             carry = back_row(r, carry)
         for peer in (first, first + 1):
@@ -382,25 +402,7 @@
     step_a(3)
     for n in BACKS:
         a_in[n, near] = a[n, near]
-    step_b(0)
-    step_b(1)
-
-    def block_gate_row(r, carry):
-        value, slope = gelu_parts(dot(w_in[CH:], nb[r]))
-        dgelu[r, CH:] = slope
-        value = value.astype(BF)
-        gates[r, HC:CH] = value[0:HC]
-        bval[r] = value[HC:]
-        return carry
-
-    loop(ROWS, block_gate_row, unroll=8)
-    down_axis = lax.broadcasted_iota(jnp.int32, (COLS, COLS), 0)
-    along_axis = lax.broadcasted_iota(jnp.int32, (COLS, COLS), 1)
-    gather[...] = order(along_axis, down_axis)
-    spread[...] = order(down_axis, along_axis)
-    mixp[...] = dot(dot(gather[...], grid_mix[...]).astype(BF), spread[...]).astype(BF)
-    mixp_t[...] = dot(dot_nt(gather[...], grid_mix[...]).astype(BF), spread[...]).astype(BF)
-    step_c(0, mixp)
+
 
     def put(ref):
         def store(k, t, value):
@@ -413,8 +415,9 @@
     mixed = dot_nt(values, block_mix[...]).astype(BF)
     swap_granules(lambda k, t: mixed[k * HC : (k + 1) * HC, half(t)], put(bm), HC)
 
+    step_c(0, mixp)
+    step_b(2)
     step_c(1, mixp)
-    step_b(2)
     step_b(3)
 
     def block_back(k, t):
@@ -464,7 +467,7 @@
         ]
 
     def joined_row(r, carry):
-        pack, p_in, p_out, p_conv = carry
+        pack, p_in, p_out = carry
         grid_mixed = returned(VALUES, r)
         for t in range(2):
             gates_t = gates[r, :, half(t)].astype(F32)
@@ -476,23 +479,19 @@
         jp[r + 2] = j
         v3[r + 1, CH : 2 * CH] = j
         pack = edges(pack, j[:, half(0)], j[:, half(1)], r)
-        return pack, p_in + dot_nt(nb[r], gbef[r]), p_out + dot_nt(gj[r], gated[r]), p_conv + conv_plane(r)
-
-    def conv_plane(p):
-        return dot_nt(u3[p], jp[pl.ds(p, 3)].reshape(3 * CH, COLS))
-
-    pack, p_in, p_out, p_conv = loop(
+        return pack, p_in + dot_nt(nb[r], gbef[r]), p_out + dot_nt(gj[r], gated[r])
+
+    pack, p_in, p_out = loop(
         ROWS,
         joined_row,
-        (
-            jnp.zeros((CH, LANES), BF),
-            jnp.zeros((CH, 2 * CH), F32),
-            jnp.zeros((CH, CH), F32),
-            jnp.zeros((3 * CH, 3 * CH), F32),
-        ),
+        (jnp.zeros((CH, LANES), BF), jnp.zeros((CH, 2 * CH), F32), jnp.zeros((CH, CH), F32)),
         unroll=8,
     )
-    p_conv = p_conv + conv_plane(ROWS) + conv_plane(ROWS + 1)
+
+    def conv_row(p, total):
+        return total + dot_nt(u3[p], jp[pl.ds(p, 3)].reshape(3 * CH, COLS))
+
+    p_conv = loop(ROWS + 2, conv_row, jnp.zeros((3 * CH, 3 * CH), F32), unroll=9)
     st[0 : 3 * CH] = p_conv[:, half(0)].astype(BF)
     st[3 * CH : 4 * CH] = p_in.astype(BF)
     third = p_conv[:, 2 * CH :]
@@ -516,10 +515,11 @@
 
     take_halo(v3, 1, G_ROW1, G_PACK1)
 
-    arrived(re2.at[pl.ds(0, 3)], G_E2)
-    e2[...] = re2[0] + re2[1] + re2[2] + re2[3]
-    over_z(lambda peer: e2, re3.at[deep], G_E3)
-    re3[deep] = e2[...]
+    for n in VALUES + BACKS:
+        for ref, count, g in ((a_in, NEAR, G_A), (b_in, FAR, G_B), (c_in, FAR, G_C)):
+            gone(ref.at[n, pl.ds(0, count - 1)], g + n)
+    for n in VALUES:
+        gone(d_in.at[n, pl.ds(0, NEAR - 1)], G_D + n)
 
     from_near(rt1, G_T1)
     total = rt1[0].astype(F32)
@@ -529,6 +529,11 @@
     over_x(lambda peer: t1, rt2.at[across], G_T2)
     rt2[across] = t1[...]
 
+    arrived(re2.at[pl.ds(0, 3)], G_E2)
+    e2[...] = re2[0] + re2[1] + re2[2] + re2[3]
+    over_z(lambda peer: e2, re3.at[deep], G_E3)
+    re3[deep] = e2[...]
+
     conv_k = jnp.concatenate(
         [jnp.concatenate([conv_w[a, b] for b in range(3)], axis=1) for a in range(3)], axis=0
     )
@@ -542,11 +547,6 @@
 
     carry = loop(ROWS // 2, out_row, conv_start(conv_k, v3), unroll=8)
 
-    arrived(re3.at[pl.ds(0, 3)], G_E3)
-    e3[...] = (re3[0] + re3[1] + re3[2] + re3[3]).astype(BF)
-    over_x(lambda peer: e3, re4.at[across], G_E4)
-    re4[across] = e3[...]
-
     step_e(2)
     step_e(3)
 
@@ -561,9 +561,10 @@
     over_near(lambda peer: sq, rq1.at[near], G_Q1)
     rq1[near] = sq[...]
 
-    arrived(re4.at[pl.ds(0, 3)], G_E4)
-    over_y(lambda peer: re4, re5.at[level], G_E5)
-    re5[level] = re4[...]
+    arrived(re3.at[pl.ds(0, 3)], G_E3)
+    e3[...] = (re3[0] + re3[1] + re3[2] + re3[3]).astype(BF)
+    over_x(lambda peer: e3, re4.at[across], G_E4)
+    re4[across] = e3[...]
 
     arrived(rt2.at[pl.ds(0, 3)], G_T2)
     total = rt2[0].astype(F32)
@@ -593,6 +594,10 @@
     over_far(lambda peer: q1, rq2.at[far], G_Q2)
     rq2[far] = q1[...]
 
+    arrived(re4.at[pl.ds(0, 3)], G_E4)
+    over_y(lambda peer: re4, re5.at[level], G_E5)
+    re5[level] = re4[...]
+
     arrived(rt3.at[pl.ds(0, 3)], G_T3)
     total = rt3[0].astype(F32)
     for k in range(1, 4):
@@ -602,11 +607,11 @@
     rt4[near] = t3[...]
 
 
+    loop(ROWS // 2, lambda r, carry: out_row(r + ROWS // 2, carry), carry, unroll=8)
+
     arrived(re5.at[pl.ds(0, 3)], G_E5)
     push(re5, re6, G_E6, near_device(twin))
     early_out[pl.ds(pl.multiple_of(mine, 512), 512)] = re5[...].reshape(512, LANES)
-
-    loop(ROWS // 2, lambda r, carry: out_row(r + ROWS // 2, carry), carry, unroll=8)
 
     from_far(rq2, G_Q2)
     total = rq2[0].astype(F32)
@@ -621,9 +626,8 @@
     for which, g_row, g_pack in ((0, G_ROW0, G_PACK0), (1, G_ROW1, G_PACK1)):
         gone(row_in.at[which], g_row)
         gone(pack_in.at[which], g_pack)
-    for n in VALUES + BACKS:
-        for ref, count, g in ((a_in, NEAR, G_A), (b_in, FAR, G_B), (c_in, FAR, G_C), (d_in, NEAR, G_D)):
-            gone(ref.at[n, pl.ds(0, count - 1)], g + n)
+    for n in BACKS:
+        gone(d_in.at[n, pl.ds(0, NEAR - 1)], G_D + n)
     for ref, g in ((rt1, G_T1), (rt4, G_T4), (rq1, G_Q1)):
         gone(ref.at[pl.ds(0, NEAR - 1)], g)
     gone(rq2.at[pl.ds(0, FAR - 1)], G_Q2)

time: 61.2 us -> 58.3 us (0.953)
  Pallas kernels: 60.5 us -> 57.5 us
    pallas_call x1, Pallas kernels: 58.2 us -> 55.3 us  [body(): pl.pallas_call(kernel, out_shape=(shape((2, ROWS * CH, LANES), F32), shap...]
where the time goes in v11:
time: 58.3 us; the launch traced here: 58.2 us
  Pallas kernels  57.5 us (99%)
  between operations  0.64 us (1%)
    pallas_call x1, Pallas kernels, body(): pl.pallas_call(kernel, out_shape=(shape((2, ROWS * CH, LANES), F32), shap...  55.3 us
    pallas_call x1, Pallas kernels, body(): pl.pallas_call(finish, out_shape=(shape((CH, ROWS, COLS), BF), shape((CH,...  2.26 us

profile of v11, /device:TPU:1, one launch (start us, length us, event | category | flops | bytes accessed | tf_op | source)
XLA Modules:
  0.0 58.2 jit_solution(17136903737072116867)
XLA Ops:
  0.6 55.3 %shard_map.126 = (f32[2,1024,128]{2,1,0:T(8,128)S(1)}, f32[2,1024,128]{2,1,0:T(8,128)S(1)}, bf16[1024,128]{1,0:T(8,128)(2,1)S(1)}, bf16[8,48,128]{2,1,0:T(8,128)(2,1)S(1)}, f32[16,128]{1,0:T(8,128)S(1)}) custom-call(bf16[64,16,256]{2,1,0:T(8,128)(2,1)} %frames_hbm.1, bf16[64,128]{1,0:T(8,128)(2,1)} %bitcast.4, bf16[256,256]{1,0:T(8,128)(2,1)} %grid_mix_hbm.1, ...), custom_call_target="tpu_custom_call" | custom-call | tf_op jit(solution)/shard_map/pallas_call | solution.py:774
  55.9 2.3 %shard_map.127 = (bf16[64,16,256]{2,1,0:T(8,128)(2,1)}, bf16[64,16,256]{2,1,0:T(8,128)(2,1)}, f32[64,128]{1,0:T(8,128)}, f32[256,256]{1,0:T(8,128)}, f32[256,256...) custom-call(f32[2,1024,128]{2,1,0:T(8,128)S(1)} %get-tuple-element.19.rest, ...), custom_call_target="tpu_custom_call" | custom-call | tf_op jit(solution)/shard_map/pallas_call | solution.py:790

commit v12 on v11

--- a/solution.py
+++ b/solution.py
@@ -466,8 +466,7 @@
             jnp.concatenate([d_in[n, r // 2, t, lax.rem(r, 2)] for n in chains], axis=0).astype(F32) for t in range(2)
         ]
 
-    def joined_row(r, carry):
-        pack, p_in, p_out = carry
+    def joined_row(r, pack):
         grid_mixed = returned(VALUES, r)
         for t in range(2):
             gates_t = gates[r, :, half(t)].astype(F32)
@@ -478,20 +477,19 @@
         j = (xb[r].astype(F32) + dot(w_out[...], gated[r])).astype(BF)
         jp[r + 2] = j
         v3[r + 1, CH : 2 * CH] = j
-        pack = edges(pack, j[:, half(0)], j[:, half(1)], r)
-        return pack, p_in + dot_nt(nb[r], gbef[r]), p_out + dot_nt(gj[r], gated[r])
-
-    pack, p_in, p_out = loop(
-        ROWS,
-        joined_row,
-        (jnp.zeros((CH, LANES), BF), jnp.zeros((CH, 2 * CH), F32), jnp.zeros((CH, CH), F32)),
-        unroll=8,
+        return edges(pack, j[:, half(0)], j[:, half(1)], r)
+
+    pack = loop(ROWS, joined_row, jnp.zeros((CH, LANES), BF), unroll=8)
+
+    def pixels(ref, rows=slice(None)):
+        return jnp.concatenate([ref[r, rows] for r in range(ROWS)], axis=1)
+
+    p_conv = dot_nt(
+        jnp.concatenate([u3[p] for p in range(ROWS + 2)], axis=1),
+        jnp.concatenate([jp[p : p + 3].reshape(3 * CH, COLS) for p in range(ROWS + 2)], axis=1),
     )
-
-    def conv_row(p, total):
-        return total + dot_nt(u3[p], jp[pl.ds(p, 3)].reshape(3 * CH, COLS))
-
-    p_conv = loop(ROWS + 2, conv_row, jnp.zeros((3 * CH, 3 * CH), F32), unroll=9)
+    p_in = dot_nt(pixels(nb), pixels(gbef))
+    p_out = dot_nt(pixels(gj), pixels(gated))
     st[0 : 3 * CH] = p_conv[:, half(0)].astype(BF)
     st[3 * CH : 4 * CH] = p_in.astype(BF)
     third = p_conv[:, 2 * CH :]
@@ -550,13 +548,14 @@
     step_e(2)
     step_e(3)
 
-    def value_before_row(r, total):
+    def value_before_row(r, carry):
         grid_back = returned(BACKS, r)
         for t in range(2):
             gbef[r, HC:CH, half(t)] = (dgelu[r, HC:CH, half(t)] * grid_back[t]).astype(BF)
-        return total + dot_nt(gbef[r, HC:CH], nb[r])
-
-    p_value = loop(ROWS, value_before_row, jnp.zeros((HC, CH), F32), unroll=4)
+        return carry
+
+    loop(ROWS, value_before_row, unroll=4)
+    p_value = dot_nt(pixels(gbef, slice(HC, CH)), pixels(nb))
     sq[...] = jnp.concatenate([p_value[0:16], p_value[16:]], axis=1).astype(BF)
     over_near(lambda peer: sq, rq1.at[near], G_Q1)
     rq1[near] = sq[...]

time: 58.3 us -> 58.3 us (level)
  no operation moved by 1% of the time
where the time goes in v12:
time: 58.3 us; the launch traced here: 58.2 us
  Pallas kernels  57.5 us (99%)
  between operations  0.64 us (1%)
    pallas_call x1, Pallas kernels, body(): pl.pallas_call(kernel, out_shape=(shape((2, ROWS * CH, LANES), F32), shap...  55.3 us
    pallas_call x1, Pallas kernels, body(): pl.pallas_call(finish, out_shape=(shape((CH, ROWS, COLS), BF), shape((CH,...  2.26 us

profile of v12, /device:TPU:1, one launch (start us, length us, event | category | flops | bytes accessed | tf_op | source)
XLA Modules:
  0.0 58.2 jit_solution(17672491725994854660)
XLA Ops:
  0.6 55.3 %shard_map.126 = (f32[2,1024,128]{2,1,0:T(8,128)S(1)}, f32[2,1024,128]{2,1,0:T(8,128)S(1)}, bf16[1024,128]{1,0:T(8,128)(2,1)S(1)}, bf16[8,48,128]{2,1,0:T(8,128)(2,1)S(1)}, f32[16,128]{1,0:T(8,128)S(1)}) custom-call(bf16[64,16,256]{2,1,0:T(8,128)(2,1)} %frames_hbm.1, bf16[64,128]{1,0:T(8,128)(2,1)} %bitcast.4, bf16[256,256]{1,0:T(8,128)(2,1)} %grid_mix_hbm.1, ...), custom_call_target="tpu_custom_call" | custom-call | tf_op jit(solution)/shard_map/pallas_call | solution.py:773
  55.9 2.3 %shard_map.127 = (bf16[64,16,256]{2,1,0:T(8,128)(2,1)}, bf16[64,16,256]{2,1,0:T(8,128)(2,1)}, f32[64,128]{1,0:T(8,128)}, f32[256,256]{1,0:T(8,128)}, f32[256,256...) custom-call(f32[2,1024,128]{2,1,0:T(8,128)S(1)} %get-tuple-element.19.rest, ...), custom_call_target="tpu_custom_call" | custom-call | tf_op jit(solution)/shard_map/pallas_call | solution.py:789

commit v13 on v12

--- a/solution.py
+++ b/solution.py
@@ -21,10 +21,10 @@
 FAR = 16
 
 (G_ROW0, G_PACK0, G_ROW1, G_PACK1) = range(4)
-(G_E0, G_E1, G_E2, G_E3, G_E4, G_E5, G_E6, G_T1, G_T2, G_T3, G_T4, G_Q1, G_Q2) = range(4, 17)
+(G_E0, G_E1, G_E2, G_E3, G_E4, G_E5, G_E6, G_T1, G_T2, G_T3, G_Q1, G_Q2) = range(4, 16)
 VALUES, BACKS = (0, 1), (2, 3)
-G_A, G_B, G_C, G_D = 17, 21, 25, 29
-GROUPS = 33
+G_A, G_B, G_C, G_D = 16, 20, 24, 28
+GROUPS = 32
 QC = 16
 
 
@@ -82,7 +82,7 @@
     a, a_in, x32, b, b_in, c, c_in, d, d_in,
     gated, gbef, jp, row_in, pack_out, pack_in, edge_l, edge_r,
     mixp, mixp_t, gather, spread, se, re0, e0, re1, e1, re2, e2, re3, e3, re4, re5, re6,
-    st, rt1, t1, rt2, t2, rt3, t3, rt4, sq, rq1, q1, rq2,
+    st, rt1, t1, rt2, t2, rt3, sq, rq1, q1, rq2,
     ssem, rsem, isem,
 ):
     ia = lax.axis_index("ha")
@@ -480,6 +480,7 @@
         return edges(pack, j[:, half(0)], j[:, half(1)], r)
 
     pack = loop(ROWS, joined_row, jnp.zeros((CH, LANES), BF), unroll=8)
+    send_halo(v3, pack, 1, G_ROW1, G_PACK1)
 
     def pixels(ref, rows=slice(None)):
         return jnp.concatenate([ref[r, rows] for r in range(ROWS)], axis=1)
@@ -496,9 +497,19 @@
     st[4 * CH :] = jnp.concatenate(
         [third[: 2 * CH], jnp.concatenate([third[2 * CH :], p_out], axis=0)], axis=1
     ).astype(BF)
-    over_near(lambda peer: st.at[pl.ds(pl.multiple_of(peer * 48, 16), 48)], rt1.at[near], G_T1)
-    rt1[near] = st[pl.ds(pl.multiple_of(near * 48, 16), 48)]
-    send_halo(v3, pack, 1, G_ROW1, G_PACK1)
+    summing = far < 12
+    for peer, place in zip(far_peers, far_places):
+
+        @pl.when(peer < 12)
+        def _():
+            push(st.at[pl.ds(pl.multiple_of(peer * 32, 32), 32)], rt1.at[far], G_T1, place)
+
+    @pl.when(summing)
+    def _():
+        rt1[far] = st[pl.ds(pl.multiple_of(far * 32, 32), 32)]
+
+    step_d(2)
+    step_d(3)
 
     arrived(re1.at[pl.ds(0, 3)], G_E1)
     total = re1[0].astype(F32)
@@ -508,29 +519,7 @@
     over_x(lambda peer: e1.at[pl.ds(pl.multiple_of(peer * 32, 32), 32)], re2.at[across], G_E2)
     re2[across] = e1[pl.ds(pl.multiple_of(across * 32, 32), 32)]
 
-    step_d(2)
-    step_d(3)
-
     take_halo(v3, 1, G_ROW1, G_PACK1)
-
-    for n in VALUES + BACKS:
-        for ref, count, g in ((a_in, NEAR, G_A), (b_in, FAR, G_B), (c_in, FAR, G_C)):
-            gone(ref.at[n, pl.ds(0, count - 1)], g + n)
-    for n in VALUES:
-        gone(d_in.at[n, pl.ds(0, NEAR - 1)], G_D + n)
-
-    from_near(rt1, G_T1)
-    total = rt1[0].astype(F32)
-    for k in range(1, NEAR):
-        total = total + rt1[k].astype(F32)
-    t1[...] = total.astype(BF)
-    over_x(lambda peer: t1, rt2.at[across], G_T2)
-    rt2[across] = t1[...]
-
-    arrived(re2.at[pl.ds(0, 3)], G_E2)
-    e2[...] = re2[0] + re2[1] + re2[2] + re2[3]
-    over_z(lambda peer: e2, re3.at[deep], G_E3)
-    re3[deep] = e2[...]
 
     conv_k = jnp.concatenate(
         [jnp.concatenate([conv_w[a, b] for b in range(3)], axis=1) for a in range(3)], axis=0
@@ -545,6 +534,27 @@
 
     carry = loop(ROWS // 2, out_row, conv_start(conv_k, v3), unroll=8)
 
+    for n in VALUES + BACKS:
+        for ref, count, g in ((a_in, NEAR, G_A), (b_in, FAR, G_B), (c_in, FAR, G_C)):
+            gone(ref.at[n, pl.ds(0, count - 1)], g + n)
+    for n in VALUES:
+        gone(d_in.at[n, pl.ds(0, NEAR - 1)], G_D + n)
+
+    @pl.when(summing)
+    def _():
+        from_far(rt1, G_T1)
+        total = rt1[0].astype(F32)
+        for k in range(1, FAR):
+            total = total + rt1[k].astype(F32)
+        t1[...] = total.astype(BF)
+        over_near(lambda peer: t1, rt2.at[near], G_T2)
+        rt2[near] = t1[...]
+
+    arrived(re2.at[pl.ds(0, 3)], G_E2)
+    e2[...] = re2[0] + re2[1] + re2[2] + re2[3]
+    over_z(lambda peer: e2, re3.at[deep], G_E3)
+    re3[deep] = e2[...]
+
     step_e(2)
     step_e(3)
 
@@ -560,18 +570,20 @@
     over_near(lambda peer: sq, rq1.at[near], G_Q1)
     rq1[near] = sq[...]
 
+    @pl.when(summing)
+    def _():
+        from_near(rt2, G_T2)
+        total = rt2[0].astype(F32)
+        for k in range(1, NEAR):
+            total = total + rt2[k].astype(F32)
+        t2[...] = total.astype(BF)
+        over_far(lambda peer: t2, rt3.at[far], G_T3)
+        rt3[far] = t2[...]
+
     arrived(re3.at[pl.ds(0, 3)], G_E3)
     e3[...] = (re3[0] + re3[1] + re3[2] + re3[3]).astype(BF)
     over_x(lambda peer: e3, re4.at[across], G_E4)
     re4[across] = e3[...]
-
-    arrived(rt2.at[pl.ds(0, 3)], G_T2)
-    total = rt2[0].astype(F32)
-    for k in range(1, 4):
-        total = total + rt2[k].astype(F32)
-    t2[...] = total.astype(BF)
-    over_z(lambda peer: t2, rt3.at[deep], G_T3)
-    rt3[deep] = t2[...]
 
     def frame_row(r, carry):
         normed = dot(w_in_t[...], gbef[r])
@@ -597,15 +609,6 @@
     over_y(lambda peer: re4, re5.at[level], G_E5)
     re5[level] = re4[...]
 
-    arrived(rt3.at[pl.ds(0, 3)], G_T3)
-    total = rt3[0].astype(F32)
-    for k in range(1, 4):
-        total = total + rt3[k].astype(F32)
-    t3[...] = total.astype(BF)
-    over_near(lambda peer: t3, rt4.at[near], G_T4)
-    rt4[near] = t3[...]
-
-
     loop(ROWS // 2, lambda r, carry: out_row(r + ROWS // 2, carry), carry, unroll=8)
 
     arrived(re5.at[pl.ds(0, 3)], G_E5)
@@ -617,8 +620,20 @@
     for k in range(1, FAR):
         total = total + rq2[k].astype(F32)
     value_out[...] = total
-    from_near(rt4, G_T4)
-    tail_out[...] = rt4[...]
+
+    @pl.when(summing)
+    def _():
+        arrived(rt3.at[pl.ds(0, 11)], G_T3)
+        gone(rt1.at[pl.ds(0, 11)], G_T1)
+        gone(rt2.at[pl.ds(0, NEAR - 1)], G_T2)
+        gone(rt1.at[pl.ds(0, FAR - 1)], G_T3)
+
+    @pl.when(far >= 12)
+    def _():
+        arrived(rt3, G_T3)
+        gone(rt1.at[pl.ds(0, 12)], G_T1)
+
+    tail_out[...] = rt3[...]
     arrived(re6, G_E6)
     early_out[pl.ds(pl.multiple_of(512 - mine, 512), 512)] = re6[...].reshape(512, LANES)
 
@@ -627,11 +642,10 @@
         gone(pack_in.at[which], g_pack)
     for n in BACKS:
         gone(d_in.at[n, pl.ds(0, NEAR - 1)], G_D + n)
-    for ref, g in ((rt1, G_T1), (rt4, G_T4), (rq1, G_Q1)):
-        gone(ref.at[pl.ds(0, NEAR - 1)], g)
+    gone(rq1.at[pl.ds(0, NEAR - 1)], G_Q1)
     gone(rq2.at[pl.ds(0, FAR - 1)], G_Q2)
     gone(re0, G_E0)
-    for ref, g in ((re1, G_E1), (re2, G_E2), (re3, G_E3), (re4, G_E4), (re5, G_E5), (rt2, G_T2), (rt3, G_T3)):
+    for ref, g in ((re1, G_E1), (re2, G_E2), (re3, G_E3), (re4, G_E4), (re5, G_E5)):
         gone(ref.at[pl.ds(0, 3)], g)
     gone(re6, G_E6)
 
@@ -749,13 +763,11 @@
     vm(4, 4, 32, LANES),
     vm(4, 4, 32, LANES),
     vm(6 * CH, LANES),
-    vm(NW, 48, LANES),
-    vm(48, LANES),
-    vm(4, 48, LANES),
-    vm(48, LANES),
-    vm(4, 48, LANES),
-    vm(48, LANES),
-    vm(NEAR, 48, LANES),
+    vm(FAR, 32, LANES),
+    vm(32, LANES),
+    vm(NEAR, 32, LANES),
+    vm(32, LANES),
+    vm(12, 32, LANES),
     vm(16, LANES),
     vm(NEAR, 16, LANES),
     vm(16, LANES),
@@ -776,7 +788,7 @@
             shape((2, ROWS * CH, LANES), F32),
             shape((2, ROWS * CH, LANES), F32),
             shape((4 * COLS, LANES), BF),
-            shape((NEAR, 48, LANES), BF),
+            shape((12, 32, LANES), BF),
             shape((16, LANES), F32),
         ),
         in_specs=[pl.BlockSpec(memory_space=pltpu.HBM)] * 7,

time: 58.3 us -> 58.7 us (level)
  no operation moved by 1% of the time
where the time goes in v13:
time: 58.7 us; the launch traced here: 58.6 us
  Pallas kernels  57.9 us (99%)
  between operations  0.64 us (1%)
    pallas_call x1, Pallas kernels, body(): pl.pallas_call(kernel, out_shape=(shape((2, ROWS * CH, LANES), F32), shap...  55.7 us
    pallas_call x1, Pallas kernels, body(): pl.pallas_call(finish, out_shape=(shape((CH, ROWS, COLS), BF), shape((CH,...  2.26 us

profile of v13, /device:TPU:1, one launch (start us, length us, event | category | flops | bytes accessed | tf_op | source)
XLA Modules:
  0.0 58.6 jit_solution(3015586968611363017)
XLA Ops:
  0.6 55.7 %shard_map.126 = (f32[2,1024,128]{2,1,0:T(8,128)S(1)}, f32[2,1024,128]{2,1,0:T(8,128)S(1)}, bf16[1024,128]{1,0:T(8,128)(2,1)S(1)}, bf16[12,32,128]{2,1,0:T(8,128)(2,1)S(1)}, f32[16,128]{1,0:T(8,128)S(1)}) custom-call(bf16[64,16,256]{2,1,0:T(8,128)(2,1)} %frames_hbm.1, bf16[64,128]{1,0:T(8,128)(2,1)} %bitcast.4, bf16[256,256]{1,0:T(8,128)(2,1)} %grid_mix_hbm.1, ...), custom_call_target="tpu_custom_call" | custom-call | tf_op jit(solution)/shard_map/pallas_call | solution.py:785
  56.3 2.3 %shard_map.127 = (bf16[64,16,256]{2,1,0:T(8,128)(2,1)}, bf16[64,16,256]{2,1,0:T(8,128)(2,1)}, f32[64,128]{1,0:T(8,128)}, f32[256,256]{1,0:T(8,128)}, f32[256,256...) custom-call(f32[2,1024,128]{2,1,0:T(8,128)S(1)} %get-tuple-element.19.rest, ...), custom_call_target="tpu_custom_call" | custom-call | tf_op jit(solution)/shard_map/pallas_call | solution.py:801

commit v14 on v13

--- a/solution.py
+++ b/solution.py
@@ -453,13 +453,13 @@
     se[COLS : 2 * COLS] = part_grid[:, half(1)]
     push(se.at[pl.ds(pl.multiple_of(512 - mine, 512), 512)], re0, G_E0, near_device(twin))
 
-    step_e(0)
-    step_e(1)
-
     arrived(re0, G_E0)
     e0[...] = (se[pl.ds(pl.multiple_of(mine, 512), 512)].astype(F32) + re0[...].astype(F32)).astype(BF)
     over_y(lambda peer: e0.at[pl.ds(pl.multiple_of(peer * 128, 128), 128)], re1.at[level], G_E1)
     re1[level] = e0[pl.ds(pl.multiple_of(level * 128, 128), 128)]
+
+    step_e(0)
+    step_e(1)
 
     def returned(chains, r):
         return [
@@ -482,6 +482,9 @@
     pack = loop(ROWS, joined_row, jnp.zeros((CH, LANES), BF), unroll=8)
     send_halo(v3, pack, 1, G_ROW1, G_PACK1)
 
+    step_d(2)
+    step_d(3)
+
     def pixels(ref, rows=slice(None)):
         return jnp.concatenate([ref[r, rows] for r in range(ROWS)], axis=1)
 
@@ -489,6 +492,14 @@
         jnp.concatenate([u3[p] for p in range(ROWS + 2)], axis=1),
         jnp.concatenate([jp[p : p + 3].reshape(3 * CH, COLS) for p in range(ROWS + 2)], axis=1),
     )
+    arrived(re1.at[pl.ds(0, 3)], G_E1)
+    total = re1[0].astype(F32)
+    for k in range(1, 4):
+        total = total + re1[k].astype(F32)
+    e1[...] = total
+    over_x(lambda peer: e1.at[pl.ds(pl.multiple_of(peer * 32, 32), 32)], re2.at[across], G_E2)
+    re2[across] = e1[pl.ds(pl.multiple_of(across * 32, 32), 32)]
+
     p_in = dot_nt(pixels(nb), pixels(gbef))
     p_out = dot_nt(pixels(gj), pixels(gated))
     st[0 : 3 * CH] = p_conv[:, half(0)].astype(BF)
@@ -508,18 +519,12 @@
     def _():
         rt1[far] = st[pl.ds(pl.multiple_of(far * 32, 32), 32)]
 
-    step_d(2)
-    step_d(3)
-
-    arrived(re1.at[pl.ds(0, 3)], G_E1)
-    total = re1[0].astype(F32)
-    for k in range(1, 4):
-        total = total + re1[k].astype(F32)
-    e1[...] = total
-    over_x(lambda peer: e1.at[pl.ds(pl.multiple_of(peer * 32, 32), 32)], re2.at[across], G_E2)
-    re2[across] = e1[pl.ds(pl.multiple_of(across * 32, 32), 32)]
-
     take_halo(v3, 1, G_ROW1, G_PACK1)
+
+    arrived(re2.at[pl.ds(0, 3)], G_E2)
+    e2[...] = re2[0] + re2[1] + re2[2] + re2[3]
+    over_z(lambda peer: e2, re3.at[deep], G_E3)
+    re3[deep] = e2[...]
 
     conv_k = jnp.concatenate(
         [jnp.concatenate([conv_w[a, b] for b in range(3)], axis=1) for a in range(3)], axis=0
@@ -533,6 +538,21 @@
         return carry
 
     carry = loop(ROWS // 2, out_row, conv_start(conv_k, v3), unroll=8)
+
+    step_e(2)
+    step_e(3)
+
+    def value_before_row(r, carry):
+        grid_back = returned(BACKS, r)
+        for t in range(2):
+            gbef[r, HC:CH, half(t)] = (dgelu[r, HC:CH, half(t)] * grid_back[t]).astype(BF)
+        return carry
+
+    loop(ROWS, value_before_row, unroll=4)
+    p_value = dot_nt(pixels(gbef, slice(HC, CH)), pixels(nb))
+    sq[...] = jnp.concatenate([p_value[0:16], p_value[16:]], axis=1).astype(BF)
+    over_near(lambda peer: sq, rq1.at[near], G_Q1)
+    rq1[near] = sq[...]
 
     for n in VALUES + BACKS:
         for ref, count, g in ((a_in, NEAR, G_A), (b_in, FAR, G_B), (c_in, FAR, G_C)):
@@ -550,25 +570,34 @@
         over_near(lambda peer: t1, rt2.at[near], G_T2)
         rt2[near] = t1[...]
 
-    arrived(re2.at[pl.ds(0, 3)], G_E2)
-    e2[...] = re2[0] + re2[1] + re2[2] + re2[3]
-    over_z(lambda peer: e2, re3.at[deep], G_E3)
-    re3[deep] = e2[...]
-
-    step_e(2)
-    step_e(3)
-
-    def value_before_row(r, carry):
-        grid_back = returned(BACKS, r)
+    arrived(re3.at[pl.ds(0, 3)], G_E3)
+    e3[...] = (re3[0] + re3[1] + re3[2] + re3[3]).astype(BF)
+    over_x(lambda peer: e3, re4.at[across], G_E4)
+    re4[across] = e3[...]
+
+    def frame_row(r, carry):
+        normed = dot(w_in_t[...], gbef[r])
+        u = unit[r]
+        mean_grad = jnp.mean(normed, axis=0, keepdims=True)
+        mean_proj = jnp.mean(normed * u, axis=0, keepdims=True)
+        source = gj[r].astype(F32) + inv[r, 0:1] * (normed - mean_grad - u * mean_proj)
         for t in range(2):
-            gbef[r, HC:CH, half(t)] = (dgelu[r, HC:CH, half(t)] * grid_back[t]).astype(BF)
+            gframe_out[t, pl.ds(r * CH, CH), :] = source[:, half(t)]
         return carry
 
-    loop(ROWS, value_before_row, unroll=4)
-    p_value = dot_nt(pixels(gbef, slice(HC, CH)), pixels(nb))
-    sq[...] = jnp.concatenate([p_value[0:16], p_value[16:]], axis=1).astype(BF)
-    over_near(lambda peer: sq, rq1.at[near], G_Q1)
-    rq1[near] = sq[...]
+    loop(ROWS, frame_row, unroll=8)
+
+    from_near(rq1, G_Q1)
+    total = rq1[0].astype(F32)
+    for k in range(1, NEAR):
+        total = total + rq1[k].astype(F32)
+    q1[...] = total.astype(BF)
+    over_far(lambda peer: q1, rq2.at[far], G_Q2)
+    rq2[far] = q1[...]
+
+    arrived(re4.at[pl.ds(0, 3)], G_E4)
+    over_y(lambda peer: re4, re5.at[level], G_E5)
+    re5[level] = re4[...]
 
     @pl.when(summing)
     def _():
@@ -580,46 +609,17 @@
         over_far(lambda peer: t2, rt3.at[far], G_T3)
         rt3[far] = t2[...]
 
-    arrived(re3.at[pl.ds(0, 3)], G_E3)
-    e3[...] = (re3[0] + re3[1] + re3[2] + re3[3]).astype(BF)
-    over_x(lambda peer: e3, re4.at[across], G_E4)
-    re4[across] = e3[...]
-
-    def frame_row(r, carry):
-        normed = dot(w_in_t[...], gbef[r])
-        u = unit[r]
-        mean_grad = jnp.mean(normed, axis=0, keepdims=True)
-        mean_proj = jnp.mean(normed * u, axis=0, keepdims=True)
-        source = gj[r].astype(F32) + inv[r, 0:1] * (normed - mean_grad - u * mean_proj)
-        for t in range(2):
-            gframe_out[t, pl.ds(r * CH, CH), :] = source[:, half(t)]
-        return carry
-
-    loop(ROWS, frame_row, unroll=8)
-
-    from_near(rq1, G_Q1)
-    total = rq1[0].astype(F32)
-    for k in range(1, NEAR):
-        total = total + rq1[k].astype(F32)
-    q1[...] = total.astype(BF)
-    over_far(lambda peer: q1, rq2.at[far], G_Q2)
-    rq2[far] = q1[...]
-
-    arrived(re4.at[pl.ds(0, 3)], G_E4)
-    over_y(lambda peer: re4, re5.at[level], G_E5)
-    re5[level] = re4[...]
-
     loop(ROWS // 2, lambda r, carry: out_row(r + ROWS // 2, carry), carry, unroll=8)
-
-    arrived(re5.at[pl.ds(0, 3)], G_E5)
-    push(re5, re6, G_E6, near_device(twin))
-    early_out[pl.ds(pl.multiple_of(mine, 512), 512)] = re5[...].reshape(512, LANES)
 
     from_far(rq2, G_Q2)
     total = rq2[0].astype(F32)
     for k in range(1, FAR):
         total = total + rq2[k].astype(F32)
     value_out[...] = total
+
+    arrived(re5.at[pl.ds(0, 3)], G_E5)
+    push(re5, re6, G_E6, near_device(twin))
+    early_out[pl.ds(pl.multiple_of(mine, 512), 512)] = re5[...].reshape(512, LANES)
 
     @pl.when(summing)
     def _():

time: 58.7 us -> 57.8 us (0.985)
  Pallas kernels: 57.9 us -> 57 us
    pallas_call x1, Pallas kernels: 55.7 us -> 54.7 us  [body(): pl.pallas_call(kernel, out_shape=(shape((2, ROWS * CH, LANES), F32), shap...]
where the time goes in v14:
time: 57.8 us; the launch traced here: 57.6 us
  Pallas kernels  57 us (99%)
  between operations  0.64 us (1%)
    pallas_call x1, Pallas kernels, body(): pl.pallas_call(kernel, out_shape=(shape((2, ROWS * CH, LANES), F32), shap...  54.7 us
    pallas_call x1, Pallas kernels, body(): pl.pallas_call(finish, out_shape=(shape((CH, ROWS, COLS), BF), shape((CH,...  2.26 us

profile of v14, /device:TPU:1, one launch (start us, length us, event | category | flops | bytes accessed | tf_op | source)
XLA Modules:
  0.0 57.6 jit_solution(14718904185550409811)
XLA Ops:
  0.6 54.7 %shard_map.126 = (f32[2,1024,128]{2,1,0:T(8,128)S(1)}, f32[2,1024,128]{2,1,0:T(8,128)S(1)}, bf16[1024,128]{1,0:T(8,128)(2,1)S(1)}, bf16[12,32,128]{2,1,0:T(8,128)(2,1)S(1)}, f32[16,128]{1,0:T(8,128)S(1)}) custom-call(bf16[64,16,256]{2,1,0:T(8,128)(2,1)} %frames_hbm.1, bf16[64,128]{1,0:T(8,128)(2,1)} %bitcast.4, bf16[256,256]{1,0:T(8,128)(2,1)} %grid_mix_hbm.1, ...), custom_call_target="tpu_custom_call" | custom-call | tf_op jit(solution)/shard_map/pallas_call | solution.py:785
  55.4 2.3 %shard_map.127 = (bf16[64,16,256]{2,1,0:T(8,128)(2,1)}, bf16[64,16,256]{2,1,0:T(8,128)(2,1)}, f32[64,128]{1,0:T(8,128)}, f32[256,256]{1,0:T(8,128)}, f32[256,256...) custom-call(f32[2,1024,128]{2,1,0:T(8,128)S(1)} %get-tuple-element.19.rest, ...), custom_call_target="tpu_custom_call" | custom-call | tf_op jit(solution)/shard_map/pallas_call | solution.py:801

commit v15 on v14

--- a/solution.py
+++ b/solution.py
@@ -228,15 +228,8 @@
 
         loop(ROWS + 2, shifts, unroll=9)
 
-    def conv_start(w, field):
-        y = dot(w, field[0])
-        z = dot(w, field[1])
-        return z[0:CH], y[0:CH] + z[CH : 2 * CH]
-
-    def conv_step(w, field, r, carry):
-        later, now = carry
-        y = dot(w, field[r + 2])
-        return now + y[2 * CH :], (y[0:CH], later + y[CH : 2 * CH])
+    def conv_step(w, field, r):
+        return dot(w, field[pl.ds(r, 3)].reshape(9 * CH, COLS))
 
     def step_a(n):
         over_near(lambda peer: a.at[n, peer], a_in.at[n, near], G_A + n)
@@ -369,13 +362,13 @@
     mixp_t[...] = dot(dot_nt(gather[...], grid_mix[...]).astype(BF), spread[...]).astype(BF)
 
     back_w = jnp.concatenate(
-        [jnp.concatenate([conv_w[2 - a, 2 - b] for a in range(3)], axis=1) for b in range(3)], axis=0
+        [conv_w[2 - a, 2 - b] for a in range(3) for b in range(3)], axis=0
     ).astype(F32).T.astype(BF)
     w_out_t = w_out[...].astype(F32).T.astype(BF)
     take_halo(u3, 0, G_ROW0, G_PACK0)
 
-    def back_row(r, carry):
-        total, carry = conv_step(back_w, u3, r, carry)
+    def back_row(r):
+        total = conv_step(back_w, u3, r)
         g = (total + u3[r + 1, CH : 2 * CH].astype(F32)).astype(BF)
         gj[r] = g
         up_gated = dot(w_out_t, g)
@@ -384,15 +377,13 @@
         for n in range(2):
             for t in range(2):
                 a[2 + n, r // 2, t, r % 2] = mixed[n * QC : (n + 1) * QC, half(t)]
-        return carry
 
     step_b(0)
-    carry = conv_start(back_w, u3)
     for first in range(0, NEAR, 2):
         if first == NEAR // 2:
             step_b(1)
         for r in range(2 * first, 2 * first + 4):
-            carry = back_row(r, carry)
+            back_row(r)
         for peer in (first, first + 1):
 
             @pl.when(peer != near)
@@ -527,17 +518,16 @@
     re3[deep] = e2[...]
 
     conv_k = jnp.concatenate(
-        [jnp.concatenate([conv_w[a, b] for b in range(3)], axis=1) for a in range(3)], axis=0
-    )
+        [conv_w[a, b].astype(F32).T for a in range(3) for b in range(3)], axis=0
+    ).T.astype(BF)
 
     def out_row(r, carry):
-        total, carry = conv_step(conv_k, v3, r, carry)
-        total = total + v3[r + 1, CH : 2 * CH].astype(F32)
+        total = conv_step(conv_k, v3, r) + v3[r + 1, CH : 2 * CH].astype(F32)
         for t in range(2):
             rest_out[t, pl.ds(r * CH, CH), :] = total[:, half(t)]
         return carry
 
-    carry = loop(ROWS // 2, out_row, conv_start(conv_k, v3), unroll=8)
+    loop(ROWS // 2, out_row, unroll=8)
 
     step_e(2)
     step_e(3)
@@ -609,7 +599,7 @@
         over_far(lambda peer: t2, rt3.at[far], G_T3)
         rt3[far] = t2[...]
 
-    loop(ROWS // 2, lambda r, carry: out_row(r + ROWS // 2, carry), carry, unroll=8)
+    loop(ROWS // 2, lambda r, carry: out_row(r + ROWS // 2, carry), unroll=8)
 
     from_far(rq2, G_Q2)
     total = rq2[0].astype(F32)

time: 57.8 us -> 59.5 us (1.029)
  Pallas kernels: 57 us -> 58.8 us
    pallas_call x1, Pallas kernels: 54.7 us -> 56.5 us  [body(): pl.pallas_call(kernel, out_shape=(shape((2, ROWS * CH, LANES), F32), shap...]
where the time goes in v15:
time: 59.5 us; the launch traced here: 59.4 us
  Pallas kernels  58.8 us (99%)
  between operations  0.64 us (1%)
    pallas_call x1, Pallas kernels, body(): pl.pallas_call(kernel, out_shape=(shape((2, ROWS * CH, LANES), F32), shap...  56.5 us
    pallas_call x1, Pallas kernels, body(): pl.pallas_call(finish, out_shape=(shape((CH, ROWS, COLS), BF), shape((CH,...  2.26 us

profile of v15, /device:TPU:1, one launch (start us, length us, event | category | flops | bytes accessed | tf_op | source)
XLA Modules:
  0.0 59.4 jit_solution(16593373404073192306)
XLA Ops:
  0.6 56.5 %shard_map.126 = (f32[2,1024,128]{2,1,0:T(8,128)S(1)}, f32[2,1024,128]{2,1,0:T(8,128)S(1)}, bf16[1024,128]{1,0:T(8,128)(2,1)S(1)}, bf16[12,32,128]{2,1,0:T(8,128)(2,1)S(1)}, f32[16,128]{1,0:T(8,128)S(1)}) custom-call(bf16[64,16,256]{2,1,0:T(8,128)(2,1)} %frames_hbm.1, bf16[64,128]{1,0:T(8,128)(2,1)} %bitcast.4, bf16[256,256]{1,0:T(8,128)(2,1)} %grid_mix_hbm.1, ...), custom_call_target="tpu_custom_call" | custom-call | tf_op jit(solution)/shard_map/pallas_call | solution.py:775
  57.2 2.3 %shard_map.127 = (bf16[64,16,256]{2,1,0:T(8,128)(2,1)}, bf16[64,16,256]{2,1,0:T(8,128)(2,1)}, f32[64,128]{1,0:T(8,128)}, f32[256,256]{1,0:T(8,128)}, f32[256,256...) custom-call(f32[2,1024,128]{2,1,0:T(8,128)S(1)} %get-tuple-element.19.rest, ...), custom_call_target="tpu_custom_call" | custom-call | tf_op jit(solution)/shard_map/pallas_call | solution.py:791

commit v16 on v14

--- a/solution.py
+++ b/solution.py
@@ -318,8 +318,8 @@
             for t in range(2):
                 slot[n, peer, t, low] = value[n * QC : (n + 1) * QC, half(t)]
 
-    for first in range(0, NEAR, 2):
-        group = [*near_peers, near][first : first + 2]
+    for first in range(0, NEAR, 4):
+        group = [*near_peers, near][first : first + 4]
         for peer in group:
             for low in range(2):
                 value_row(a_in if peer is near else a, peer, low)
@@ -339,7 +339,7 @@
         u3[r + 1, CH : 2 * CH, half(1)] = t1
         return edges(pack, t0, t1, r)
 
-    pack = loop(ROWS, cot_row, jnp.zeros((CH, LANES), BF), unroll=8)
+    pack = loop(ROWS, cot_row, jnp.zeros((CH, LANES), BF), unroll=16)
     send_halo(u3, pack, 0, G_ROW0, G_PACK0)
 
     def grid_gate_row(r, carry):
@@ -348,7 +348,7 @@
         dgelu[r, 0:HC] = slope
         return carry
 
-    loop(ROWS, grid_gate_row, unroll=8)
+    loop(ROWS, grid_gate_row, unroll=16)
 
     def block_gate_row(r, carry):
         value, slope = gelu_parts(dot(w_in[CH:], nb[r]))
@@ -358,7 +358,7 @@
         bval[r] = value[HC:]
         return carry
 
-    loop(ROWS, block_gate_row, unroll=8)
+    loop(ROWS, block_gate_row, unroll=16)
     for load in loads[3:]:
         load.wait()
     down_axis = lax.broadcasted_iota(jnp.int32, (COLS, COLS), 0)
@@ -366,7 +366,7 @@
     gather[...] = order(along_axis, down_axis)
     spread[...] = order(down_axis, along_axis)
     mixp[...] = dot(dot(gather[...], grid_mix[...]).astype(BF), spread[...]).astype(BF)
-    mixp_t[...] = dot(dot_nt(gather[...], grid_mix[...]).astype(BF), spread[...]).astype(BF)
+    mixp_t[...] = mixp[...].T
 
     back_w = jnp.concatenate(
         [jnp.concatenate([conv_w[2 - a, 2 - b] for a in range(3)], axis=1) for b in range(3)], axis=0
@@ -388,12 +388,12 @@
 
     step_b(0)
     carry = conv_start(back_w, u3)
-    for first in range(0, NEAR, 2):
-        if first == NEAR // 2:
+    for first in range(0, NEAR, 4):
+        if first:
             step_b(1)
-        for r in range(2 * first, 2 * first + 4):
+        for r in range(2 * first, 2 * first + 8):
             carry = back_row(r, carry)
-        for peer in (first, first + 1):
+        for peer in range(first, first + 4):
 
             @pl.when(peer != near)
             def _():
@@ -438,7 +438,7 @@
         gbef[r, HC:CH] = jnp.zeros((HC, COLS), BF)
         return carry
 
-    loop(ROWS, block_before_row, unroll=4)
+    loop(ROWS, block_before_row, unroll=8)
     for k in (0, 1, ROWS + 2, ROWS + 3):
         jp[k] = jnp.zeros((CH, COLS), BF)
 
@@ -479,7 +479,7 @@
         v3[r + 1, CH : 2 * CH] = j
         return edges(pack, j[:, half(0)], j[:, half(1)], r)
 
-    pack = loop(ROWS, joined_row, jnp.zeros((CH, LANES), BF), unroll=8)
+    pack = loop(ROWS, joined_row, jnp.zeros((CH, LANES), BF), unroll=16)
     send_halo(v3, pack, 1, G_ROW1, G_PACK1)
 
     step_d(2)
@@ -548,7 +548,7 @@
             gbef[r, HC:CH, half(t)] = (dgelu[r, HC:CH, half(t)] * grid_back[t]).astype(BF)
         return carry
 
-    loop(ROWS, value_before_row, unroll=4)
+    loop(ROWS, value_before_row, unroll=8)
     p_value = dot_nt(pixels(gbef, slice(HC, CH)), pixels(nb))
     sq[...] = jnp.concatenate([p_value[0:16], p_value[16:]], axis=1).astype(BF)
     over_near(lambda peer: sq, rq1.at[near], G_Q1)
@@ -585,7 +585,7 @@
             gframe_out[t, pl.ds(r * CH, CH), :] = source[:, half(t)]
         return carry
 
-    loop(ROWS, frame_row, unroll=8)
+    loop(ROWS, frame_row, unroll=16)
 
     from_near(rq1, G_Q1)
     total = rq1[0].astype(F32)

time: 57.8 us -> 57.1 us (0.988)
  Pallas kernels: 57 us -> 56.3 us
    pallas_call x1, Pallas kernels: 54.7 us -> 54.1 us  [body(): pl.pallas_call(kernel, out_shape=(shape((2, ROWS * CH, LANES), F32), shap...]
where the time goes in v16:
time: 57.1 us; the launch traced here: 57 us
  Pallas kernels  56.3 us (99%)
  between operations  0.64 us (1%)
    pallas_call x1, Pallas kernels, body(): pl.pallas_call(kernel, out_shape=(shape((2, ROWS * CH, LANES), F32), shap...  54.1 us
    pallas_call x1, Pallas kernels, body(): pl.pallas_call(finish, out_shape=(shape((CH, ROWS, COLS), BF), shape((CH,...  2.26 us

profile of v16, /device:TPU:1, one launch (start us, length us, event | category | flops | bytes accessed | tf_op | source)
XLA Modules:
  0.0 57.0 jit_solution(4622574508022210503)
XLA Ops:
  0.6 54.1 %shard_map.126 = (f32[2,1024,128]{2,1,0:T(8,128)S(1)}, f32[2,1024,128]{2,1,0:T(8,128)S(1)}, bf16[1024,128]{1,0:T(8,128)(2,1)S(1)}, bf16[12,32,128]{2,1,0:T(8,128)(2,1)S(1)}, f32[16,128]{1,0:T(8,128)S(1)}) custom-call(bf16[64,16,256]{2,1,0:T(8,128)(2,1)} %frames_hbm.1, bf16[64,128]{1,0:T(8,128)(2,1)} %bitcast.4, bf16[256,256]{1,0:T(8,128)(2,1)} %grid_mix_hbm.1, ...), custom_call_target="tpu_custom_call" | custom-call | tf_op jit(solution)/shard_map/pallas_call | solution.py:785
  54.7 2.3 %shard_map.127 = (bf16[64,16,256]{2,1,0:T(8,128)(2,1)}, bf16[64,16,256]{2,1,0:T(8,128)(2,1)}, f32[64,128]{1,0:T(8,128)}, f32[256,256]{1,0:T(8,128)}, f32[256,256...) custom-call(f32[2,1024,128]{2,1,0:T(8,128)S(1)} %get-tuple-element.19.rest, ...), custom_call_target="tpu_custom_call" | custom-call | tf_op jit(solution)/shard_map/pallas_call | solution.py:801

commit v17 on v16

--- a/solution.py
+++ b/solution.py
@@ -22,9 +22,9 @@
 
 (G_ROW0, G_PACK0, G_ROW1, G_PACK1) = range(4)
 (G_E0, G_E1, G_E2, G_E3, G_E4, G_E5, G_E6, G_T1, G_T2, G_T3, G_Q1, G_Q2) = range(4, 16)
-VALUES, BACKS = (0, 1), (2, 3)
-G_A, G_B, G_C, G_D = 16, 20, 24, 28
-GROUPS = 32
+VALUES, BACKS = (0, 1), 2
+G_A, G_B, G_C, G_D = 16, 19, 22, 25
+GROUPS = 28
 QC = 16
 
 
@@ -80,6 +80,7 @@
     frames, w_in_t, grid_mix, block_mix, w_out, conv_w, cot, w_in,
     turn, xb, nb, unit, inv, dgelu, gates, bval, u3, v3, gj, gg, xt, bt, bm, gbv,
     a, a_in, x32, b, b_in, c, c_in, d, d_in,
+    ga, ga_in, gx32, gb, gb_in, gc, gc_in, gd, gd_in,
     gated, gbef, jp, row_in, pack_out, pack_in, edge_l, edge_r,
     mixp, mixp_t, gather, spread, se, re0, e0, re1, e1, re2, e2, re3, e3, re4, re5, re6,
     st, rt1, t1, rt2, t2, rt3, sq, rq1, q1, rq2,
@@ -238,44 +239,54 @@
         y = dot(w, field[r + 2])
         return now + y[2 * CH :], (y[0:CH], later + y[CH : 2 * CH])
 
+    chains = [[ref.at[n] for ref in (a, a_in, x32, b, b_in, c, c_in, d, d_in)] + [QC, n] for n in VALUES]
+    chains.append([ga, ga_in, gx32, gb, gb_in, gc, gc_in, gd, gd_in, HC, BACKS])
+
+    def channels(count):
+        return [k // 2 * QC + k % 2 for k in range(count // 8)]
+
     def step_a(n):
-        over_near(lambda peer: a.at[n, peer], a_in.at[n, near], G_A + n)
+        src, dst = chains[n][:2]
+        over_near(lambda peer: src.at[peer], dst.at[near], G_A + n)
 
     def step_b(n):
-        arrived(a_in.at[n, pl.ds(0, NEAR - 1)], G_A + n)
+        _, a_in, x, b, b_in, *_, count, _ = chains[n]
+        arrived(a_in.at[pl.ds(0, NEAR - 1)], G_A + n)
 
         def widen(j, carry):
             for t in range(2):
                 for r in range(2):
-                    x32[n, pl.ds((r * 16 + j * 2 + t) * QC, QC), :] = a_in[n, j, t, r].astype(F32)
+                    x[pl.ds((r * 16 + j * 2 + t) * count, count), :] = a_in[j, t, r].astype(F32)
             return carry
 
         loop(NEAR, widen, unroll=8)
 
         for peer, place in zip([*far_peers, far], [*far_places, None]):
-            base = peer // 8 * (16 * QC) + lax.rem(peer, 8) * 2
+            base = peer // 8 * (16 * count) + lax.rem(peer, 8) * 2
             slot = b_in if peer is far else b
-            for k in range(2):
-                slot[n, peer, :, half(k)] = x32[n, pl.ds(base + k, 16, stride=QC), :].astype(BF)
+            for k, channel in enumerate(channels(count)):
+                slot[peer, :, half(k)] = x[pl.ds(base + channel, 16, stride=count), :].astype(BF)
             if peer is not far:
-                push(b.at[n, peer], b_in.at[n, far], G_B + n, place)
+                push(b.at[peer], b_in.at[far], G_B + n, place)
 
     def table(n):
-        return b_in[n].reshape(256, 256)
+        return chains[n][4][...].reshape(256, -1)
 
     def step_c(n, mix):
-        arrived(b_in.at[n, pl.ds(0, FAR - 1)], G_B + n)
-        c[n] = dot(mix[...], table(n)).astype(BF).reshape(FAR, 16, 256)
-        over_far(lambda peer: c.at[n, peer], c_in.at[n, far], G_C + n)
-        c_in[n, far] = c[n, far]
+        b_in, c, c_in = chains[n][4:7]
+        arrived(b_in.at[pl.ds(0, FAR - 1)], G_B + n)
+        c[...] = dot(mix[...], table(n)).astype(BF).reshape(c.shape)
+        over_far(lambda peer: c.at[peer], c_in.at[far], G_C + n)
+        c_in[far] = c[far]
 
     def step_d(n):
-        arrived(c_in.at[n, pl.ds(0, FAR - 1)], G_C + n)
+        _, _, x, _, _, _, c_in, d, d_in, count, _ = chains[n]
+        arrived(c_in.at[pl.ds(0, FAR - 1)], G_C + n)
 
         def unpick(q, carry):
             for r in range(2):
-                for k in range(2):
-                    x32[n, pl.ds((r * QC + q * 2 + k) * 16, 16), :] = c_in[n, r * 8 + q, :, half(k)].astype(F32)
+                for k, channel in enumerate(channels(count)):
+                    x[pl.ds((r * count + q * 2 + channel) * 16, 16), :] = c_in[r * 8 + q, :, half(k)].astype(F32)
             return carry
 
         loop(8, unpick, unroll=8)
@@ -284,12 +295,12 @@
             slot = d_in if peer is near else d
             for t in range(2):
                 for r in range(2):
-                    slot[n, peer, t, r] = x32[n, pl.ds(r * QC * 16 + peer * 2 + t, QC, stride=16), :].astype(BF)
+                    slot[peer, t, r] = x[pl.ds(r * count * 16 + peer * 2 + t, count, stride=16), :].astype(BF)
             if peer is not near:
-                push(d.at[n, peer], d_in.at[n, near], G_D + n, place)
+                push(d.at[peer], d_in.at[near], G_D + n, place)
 
     def step_e(n):
-        arrived(d_in.at[n, pl.ds(0, NEAR - 1)], G_D + n)
+        arrived(chains[n][8].at[pl.ds(0, NEAR - 1)], G_D + n)
 
     def order(cell, row):
         found = (row & 0xC1) | ((row & 6) << 3) | ((row & 48) >> 2) | ((row & 8) >> 2)
@@ -302,6 +313,7 @@
 
     def value_row(slot, peer, low):
         r = peer * 2 + low
+        normed = []
         for t in range(2):
             x = turned(r, t)
             xb[r, :, half(t)] = x.astype(BF)
@@ -310,8 +322,10 @@
             u = off * rstd
             unit[r, :, half(t)] = u
             inv[r, :, half(t)] = jnp.broadcast_to(rstd, (8, LANES))
-            nb[r, :, half(t)] = u.astype(BF)
-        value, slope = gelu_parts(dot(w_in[HC:CH], nb[r]))
+            normed.append(u.astype(BF))
+        normed = jnp.concatenate(normed, axis=1)
+        nb[r] = normed
+        value, slope = gelu_parts(dot(w_in[HC:CH], normed))
         dgelu[r, HC:CH] = slope
         value = value.astype(BF)
         for n in VALUES:
@@ -342,23 +356,21 @@
     pack = loop(ROWS, cot_row, jnp.zeros((CH, LANES), BF), unroll=16)
     send_halo(u3, pack, 0, G_ROW0, G_PACK0)
 
-    def grid_gate_row(r, carry):
-        value, slope = gelu_parts(dot(w_in[0:HC], nb[r]))
+    w_rest = jnp.concatenate([w_in[0:HC], w_in[CH:]], axis=0)
+
+    def gate_row(r, carry):
+        before = dot(w_rest, nb[r])
+        value, slope = gelu_parts(before[0:HC])
         gates[r, 0:HC] = value.astype(BF)
         dgelu[r, 0:HC] = slope
-        return carry
-
-    loop(ROWS, grid_gate_row, unroll=16)
-
-    def block_gate_row(r, carry):
-        value, slope = gelu_parts(dot(w_in[CH:], nb[r]))
+        value, slope = gelu_parts(before[HC:])
         dgelu[r, CH:] = slope
         value = value.astype(BF)
         gates[r, HC:CH] = value[0:HC]
         bval[r] = value[HC:]
         return carry
 
-    loop(ROWS, block_gate_row, unroll=16)
+    loop(ROWS, gate_row, unroll=8)
     for load in loads[3:]:
         load.wait()
     down_axis = lax.broadcasted_iota(jnp.int32, (COLS, COLS), 0)
@@ -381,9 +393,8 @@
         up_gated = dot(w_out_t, g)
         gg[r] = up_gated
         mixed = (up_gated[0:HC] * gates[r, 0:HC].astype(F32)).astype(BF)
-        for n in range(2):
-            for t in range(2):
-                a[2 + n, r // 2, t, r % 2] = mixed[n * QC : (n + 1) * QC, half(t)]
+        for t in range(2):
+            ga[r // 2, t, r % 2] = mixed[:, half(t)]
         return carry
 
     step_b(0)
@@ -397,11 +408,9 @@
 
             @pl.when(peer != near)
             def _():
-                push(a.at[2, peer], a_in.at[2, near], G_A + 2, near_device(peer))
-
-    step_a(3)
-    for n in BACKS:
-        a_in[n, near] = a[n, near]
+                push(ga.at[peer], ga_in.at[near], G_A + BACKS, near_device(peer))
+
+    ga_in[near] = ga[near]
 
 
     def put(ref):
@@ -416,9 +425,8 @@
     swap_granules(lambda k, t: mixed[k * HC : (k + 1) * HC, half(t)], put(bm), HC)
 
     step_c(0, mixp)
-    step_b(2)
     step_c(1, mixp)
-    step_b(3)
+    step_b(BACKS)
 
     def block_back(k, t):
         return (gg[k, HC:, half(t)] * gates[k, HC:, half(t)].astype(F32)).astype(BF)
@@ -444,10 +452,9 @@
 
     step_d(0)
     step_d(1)
-    step_c(2, mixp_t)
-    step_c(3, mixp_t)
-
-    part_grid = (dot_nt(table(2), table(0)) + dot_nt(table(3), table(1))).astype(BF)
+    step_c(BACKS, mixp_t)
+
+    part_grid = dot_nt(table(BACKS), jnp.concatenate([table(0), table(1)], axis=1)).astype(BF)
     part_grid = dot(dot(spread[...], part_grid).astype(BF), gather[...]).astype(BF)
     se[0:COLS] = part_grid[:, half(0)]
     se[COLS : 2 * COLS] = part_grid[:, half(1)]
@@ -461,13 +468,13 @@
     step_e(0)
     step_e(1)
 
-    def returned(chains, r):
+    def returned_values(r):
         return [
-            jnp.concatenate([d_in[n, r // 2, t, lax.rem(r, 2)] for n in chains], axis=0).astype(F32) for t in range(2)
+            jnp.concatenate([d_in[n, r // 2, t, lax.rem(r, 2)] for n in VALUES], axis=0).astype(F32) for t in range(2)
         ]
 
     def joined_row(r, pack):
-        grid_mixed = returned(VALUES, r)
+        grid_mixed = returned_values(r)
         for t in range(2):
             gates_t = gates[r, :, half(t)].astype(F32)
             more = grid_mixed[t] + 1.0
@@ -482,8 +489,7 @@
     pack = loop(ROWS, joined_row, jnp.zeros((CH, LANES), BF), unroll=16)
     send_halo(v3, pack, 1, G_ROW1, G_PACK1)
 
-    step_d(2)
-    step_d(3)
+    step_d(BACKS)
 
     def pixels(ref, rows=slice(None)):
         return jnp.concatenate([ref[r, rows] for r in range(ROWS)], axis=1)
@@ -539,13 +545,12 @@
 
     carry = loop(ROWS // 2, out_row, conv_start(conv_k, v3), unroll=8)
 
-    step_e(2)
-    step_e(3)
+    step_e(BACKS)
 
     def value_before_row(r, carry):
-        grid_back = returned(BACKS, r)
         for t in range(2):
-            gbef[r, HC:CH, half(t)] = (dgelu[r, HC:CH, half(t)] * grid_back[t]).astype(BF)
+            grid_back = gd_in[r // 2, t, lax.rem(r, 2)].astype(F32)
+            gbef[r, HC:CH, half(t)] = (dgelu[r, HC:CH, half(t)] * grid_back).astype(BF)
         return carry
 
     loop(ROWS, value_before_row, unroll=8)
@@ -554,9 +559,11 @@
     over_near(lambda peer: sq, rq1.at[near], G_Q1)
     rq1[near] = sq[...]
 
-    for n in VALUES + BACKS:
-        for ref, count, g in ((a_in, NEAR, G_A), (b_in, FAR, G_B), (c_in, FAR, G_C)):
-            gone(ref.at[n, pl.ds(0, count - 1)], g + n)
+    for n in (*VALUES, BACKS):
+        _, a_in, _, _, b_in, _, c_in, *_ = chains[n]
+        gone(a_in.at[pl.ds(0, NEAR - 1)], G_A + n)
+        gone(b_in.at[pl.ds(0, FAR - 1)], G_B + n)
+        gone(c_in.at[pl.ds(0, FAR - 1)], G_C + n)
     for n in VALUES:
         gone(d_in.at[n, pl.ds(0, NEAR - 1)], G_D + n)
 
@@ -640,8 +647,7 @@
     for which, g_row, g_pack in ((0, G_ROW0, G_PACK0), (1, G_ROW1, G_PACK1)):
         gone(row_in.at[which], g_row)
         gone(pack_in.at[which], g_pack)
-    for n in BACKS:
-        gone(d_in.at[n, pl.ds(0, NEAR - 1)], G_D + n)
+    gone(gd_in.at[pl.ds(0, NEAR - 1)], G_D + BACKS)
     gone(rq1.at[pl.ds(0, NEAR - 1)], G_Q1)
     gone(rq2.at[pl.ds(0, FAR - 1)], G_Q2)
     gone(re0, G_E0)
@@ -706,10 +712,11 @@
     return pltpu.VMEM(shape, dtype)
 
 
-def exchange():
-    message_w = vm(4, NEAR, 2, 2, QC, LANES)
-    message_a = vm(4, FAR, 16, 256)
-    return [message_w, message_w, vm(4, 2 * 16 * QC, LANES, dtype=F32)] + [message_a] * 4 + [message_w] * 2
+def exchange(count, *several):
+    message_w = vm(*several, NEAR, 2, 2, count, LANES)
+    message_a = vm(*several, FAR, 16, 16 * count)
+    wide = vm(*several, 2 * 16 * count, LANES, dtype=F32)
+    return [message_w, message_w, wide] + [message_a] * 4 + [message_w] * 2
 
 
 SCRATCH = [
@@ -737,7 +744,8 @@
     vm(ROWS, HC, COLS),
     vm(ROWS, HC, COLS),
     vm(ROWS, HC, COLS),
-    *exchange(),
+    *exchange(QC, 2),
+    *exchange(HC),
     vm(ROWS, CH, COLS),
     vm(ROWS, 2 * CH, COLS),
     vm(ROWS + 4, CH, COLS),

time: 57.1 us -> 57.7 us (1.011)
  Pallas kernels: 56.3 us -> 56.9 us
where the time goes in v17:
time: 57.7 us; the launch traced here: 57.5 us
  Pallas kernels  56.9 us (99%)
  between operations  0.64 us (1%)
    pallas_call x1, Pallas kernels, body(): pl.pallas_call(kernel, out_shape=(shape((2, ROWS * CH, LANES), F32), shap...  54.6 us
    pallas_call x1, Pallas kernels, body(): pl.pallas_call(finish, out_shape=(shape((CH, ROWS, COLS), BF), shape((CH,...  2.26 us

profile of v17, /device:TPU:1, one launch (start us, length us, event | category | flops | bytes accessed | tf_op | source)
XLA Modules:
  0.0 57.5 jit_solution(5202360615573257105)
XLA Ops:
  0.6 54.6 %shard_map.126 = (f32[2,1024,128]{2,1,0:T(8,128)S(1)}, f32[2,1024,128]{2,1,0:T(8,128)S(1)}, bf16[1024,128]{1,0:T(8,128)(2,1)S(1)}, bf16[12,32,128]{2,1,0:T(8,128)(2,1)S(1)}, f32[16,128]{1,0:T(8,128)S(1)}) custom-call(bf16[64,16,256]{2,1,0:T(8,128)(2,1)} %frames_hbm.1, bf16[64,128]{1,0:T(8,128)(2,1)} %bitcast.4, bf16[256,256]{1,0:T(8,128)(2,1)} %grid_mix_hbm.1, ...), custom_call_target="tpu_custom_call" | custom-call | tf_op jit(solution)/shard_map/pallas_call | solution.py:793
  55.3 2.3 %shard_map.127 = (bf16[64,16,256]{2,1,0:T(8,128)(2,1)}, bf16[64,16,256]{2,1,0:T(8,128)(2,1)}, f32[64,128]{1,0:T(8,128)}, f32[256,256]{1,0:T(8,128)}, f32[256,256...) custom-call(f32[2,1024,128]{2,1,0:T(8,128)S(1)} %get-tuple-element.19.rest, ...), custom_call_target="tpu_custom_call" | custom-call | tf_op jit(solution)/shard_map/pallas_call | solution.py:809

commit v18 on v16

--- a/solution.py
+++ b/solution.py
@@ -302,6 +302,7 @@
 
     def value_row(slot, peer, low):
         r = peer * 2 + low
+        normed = []
         for t in range(2):
             x = turned(r, t)
             xb[r, :, half(t)] = x.astype(BF)
@@ -310,8 +311,10 @@
             u = off * rstd
             unit[r, :, half(t)] = u
             inv[r, :, half(t)] = jnp.broadcast_to(rstd, (8, LANES))
-            nb[r, :, half(t)] = u.astype(BF)
-        value, slope = gelu_parts(dot(w_in[HC:CH], nb[r]))
+            normed.append(u.astype(BF))
+        normed = jnp.concatenate(normed, axis=1)
+        nb[r] = normed
+        value, slope = gelu_parts(dot(w_in[HC:CH], normed))
         dgelu[r, HC:CH] = slope
         value = value.astype(BF)
         for n in VALUES:
@@ -342,23 +345,21 @@
     pack = loop(ROWS, cot_row, jnp.zeros((CH, LANES), BF), unroll=16)
     send_halo(u3, pack, 0, G_ROW0, G_PACK0)
 
-    def grid_gate_row(r, carry):
-        value, slope = gelu_parts(dot(w_in[0:HC], nb[r]))
+    w_rest = jnp.concatenate([w_in[0:HC], w_in[CH:]], axis=0)
+
+    def gate_row(r, carry):
+        before = dot(w_rest, nb[r])
+        value, slope = gelu_parts(before[0:HC])
         gates[r, 0:HC] = value.astype(BF)
         dgelu[r, 0:HC] = slope
-        return carry
-
-    loop(ROWS, grid_gate_row, unroll=16)
-
-    def block_gate_row(r, carry):
-        value, slope = gelu_parts(dot(w_in[CH:], nb[r]))
+        value, slope = gelu_parts(before[HC:])
         dgelu[r, CH:] = slope
         value = value.astype(BF)
         gates[r, HC:CH] = value[0:HC]
         bval[r] = value[HC:]
         return carry
 
-    loop(ROWS, block_gate_row, unroll=16)
+    loop(ROWS, gate_row, unroll=8)
     for load in loads[3:]:
         load.wait()
     down_axis = lax.broadcasted_iota(jnp.int32, (COLS, COLS), 0)
@@ -416,9 +417,6 @@
     swap_granules(lambda k, t: mixed[k * HC : (k + 1) * HC, half(t)], put(bm), HC)
 
     step_c(0, mixp)
-    step_b(2)
-    step_c(1, mixp)
-    step_b(3)
 
     def block_back(k, t):
         return (gg[k, HC:, half(t)] * gates[k, HC:, half(t)].astype(F32)).astype(BF)
@@ -427,9 +425,15 @@
     backs = bt[...].reshape(ROWS * HC, COLS)
     unmixed = dot(backs, block_mix[...]).astype(BF)
     swap_granules(lambda k, t: unmixed[k * HC : (k + 1) * HC, half(t)], put(gbv), HC)
+
+    step_c(1, mixp)
+    step_b(2)
+
     part_block = dot_tn(backs, values).astype(BF)
     se[2 * COLS : 3 * COLS] = part_block[:, half(0)]
     se[3 * COLS :] = part_block[:, half(1)]
+
+    step_b(3)
 
     def block_before_row(r, carry):
         d = dgelu[r, CH:]

time: 57.1 us -> 57 us (level)
  no operation moved by 1% of the time
where the time goes in v18:
time: 57 us; the launch traced here: 56.9 us
  Pallas kernels  56.2 us (99%)
  between operations  0.64 us (1%)
    pallas_call x1, Pallas kernels, body(): pl.pallas_call(kernel, out_shape=(shape((2, ROWS * CH, LANES), F32), shap...  54 us
    pallas_call x1, Pallas kernels, body(): pl.pallas_call(finish, out_shape=(shape((CH, ROWS, COLS), BF), shape((CH,...  2.26 us

profile of v18, /device:TPU:1, one launch (start us, length us, event | category | flops | bytes accessed | tf_op | source)
XLA Modules:
  0.0 56.9 jit_solution(14116716988874341158)
XLA Ops:
  0.6 54.0 %shard_map.126 = (f32[2,1024,128]{2,1,0:T(8,128)S(1)}, f32[2,1024,128]{2,1,0:T(8,128)S(1)}, bf16[1024,128]{1,0:T(8,128)(2,1)S(1)}, bf16[12,32,128]{2,1,0:T(8,128)(2,1)S(1)}, f32[16,128]{1,0:T(8,128)S(1)}) custom-call(bf16[64,16,256]{2,1,0:T(8,128)(2,1)} %frames_hbm.1, bf16[64,128]{1,0:T(8,128)(2,1)} %bitcast.4, bf16[256,256]{1,0:T(8,128)(2,1)} %grid_mix_hbm.1, ...), custom_call_target="tpu_custom_call" | custom-call | tf_op jit(solution)/shard_map/pallas_call | solution.py:789
  54.6 2.3 %shard_map.127 = (bf16[64,16,256]{2,1,0:T(8,128)(2,1)}, bf16[64,16,256]{2,1,0:T(8,128)(2,1)}, f32[64,128]{1,0:T(8,128)}, f32[256,256]{1,0:T(8,128)}, f32[256,256...) custom-call(f32[2,1024,128]{2,1,0:T(8,128)S(1)} %get-tuple-element.19.rest, ...), custom_call_target="tpu_custom_call" | custom-call | tf_op jit(solution)/shard_map/pallas_call | solution.py:805

commit v19 on v18

--- a/solution.py
+++ b/solution.py
@@ -21,7 +21,7 @@
 FAR = 16
 
 (G_ROW0, G_PACK0, G_ROW1, G_PACK1) = range(4)
-(G_E0, G_E1, G_E2, G_E3, G_E4, G_E5, G_E6, G_T1, G_T2, G_T3, G_Q1, G_Q2) = range(4, 16)
+(G_E0, G_E1, G_E2, G_E3, G_E5, G_E6, G_T1, G_T2, G_T3, G_Q1, G_Q2) = range(4, 15)
 VALUES, BACKS = (0, 1), (2, 3)
 G_A, G_B, G_C, G_D = 16, 20, 24, 28
 GROUPS = 32
@@ -81,7 +81,7 @@
     turn, xb, nb, unit, inv, dgelu, gates, bval, u3, v3, gj, gg, xt, bt, bm, gbv,
     a, a_in, x32, b, b_in, c, c_in, d, d_in,
     gated, gbef, jp, row_in, pack_out, pack_in, edge_l, edge_r,
-    mixp, mixp_t, gather, spread, se, re0, e0, re1, e1, re2, e2, re3, e3, re4, re5, re6,
+    mixp, mixp_t, gather, spread, se, re0, e0, re1, e1, re2, e2, re3, e3, re5, re6,
     st, rt1, t1, rt2, t2, rt3, sq, rq1, q1, rq2,
     ssem, rsem, isem,
 ):
@@ -138,16 +138,6 @@
         for peer, place in zip(far_peers, far_places):
             push(src_of(peer), dst, g, place)
 
-    def over_x(src_of, dst, g):
-        for k in range(1, 4):
-            peer = lax.rem(iw // 2 + k, 4)
-            push(src_of(peer), dst, g, (ia, peer * 2 + lax.rem(iw, 2)))
-
-    def over_z(src_of, dst, g):
-        for k in range(1, 4):
-            peer = lax.rem(ia // 4 + k, 4)
-            push(src_of(peer), dst, g, (peer * 4 + lax.rem(ia, 4), iw))
-
     def over_y(src_of, dst, g):
         for k in range(1, 4):
             peer = lax.rem(near + 2 * k, NEAR)
@@ -166,7 +156,7 @@
         arrived(ref.at[pl.ds(0, FAR - 1)], g)
 
     mine = lax.rem(near, 2) * 512
-    level, across, deep = near // 2, iw // 2, ia // 4
+    level = near // 2
 
     barrier = pltpu.get_barrier_semaphore()
     peers = [near_device(peer) for peer in near_peers]
@@ -501,8 +491,8 @@
     for k in range(1, 4):
         total = total + re1[k].astype(F32)
     e1[...] = total
-    over_x(lambda peer: e1.at[pl.ds(pl.multiple_of(peer * 32, 32), 32)], re2.at[across], G_E2)
-    re2[across] = e1[pl.ds(pl.multiple_of(across * 32, 32), 32)]
+    over_far(lambda peer: e1.at[pl.ds(pl.multiple_of(peer * 8, 8), 8)], re2.at[far], G_E2)
+    re2[far] = e1[pl.ds(pl.multiple_of(far * 8, 8), 8)]
 
     p_in = dot_nt(pixels(nb), pixels(gbef))
     p_out = dot_nt(pixels(gj), pixels(gated))
@@ -525,11 +515,6 @@
 
     take_halo(v3, 1, G_ROW1, G_PACK1)
 
-    arrived(re2.at[pl.ds(0, 3)], G_E2)
-    e2[...] = re2[0] + re2[1] + re2[2] + re2[3]
-    over_z(lambda peer: e2, re3.at[deep], G_E3)
-    re3[deep] = e2[...]
-
     conv_k = jnp.concatenate(
         [jnp.concatenate([conv_w[a, b] for b in range(3)], axis=1) for a in range(3)], axis=0
     )
@@ -542,6 +527,14 @@
         return carry
 
     carry = loop(ROWS // 2, out_row, conv_start(conv_k, v3), unroll=8)
+
+    from_far(re2, G_E2)
+    total = re2[0]
+    for k in range(1, FAR):
+        total = total + re2[k]
+    e2[...] = total
+    over_far(lambda peer: e2, re3.at[far], G_E3)
+    re3[far] = e2[...]
 
     step_e(2)
     step_e(3)
@@ -574,10 +567,10 @@
         over_near(lambda peer: t1, rt2.at[near], G_T2)
         rt2[near] = t1[...]
 
-    arrived(re3.at[pl.ds(0, 3)], G_E3)
-    e3[...] = (re3[0] + re3[1] + re3[2] + re3[3]).astype(BF)
-    over_x(lambda peer: e3, re4.at[across], G_E4)
-    re4[across] = e3[...]
+    from_far(re3, G_E3)
+    e3[...] = re3[...].reshape(128, LANES).astype(BF)
+    over_y(lambda peer: e3, re5.at[level], G_E5)
+    re5[level] = e3[...]
 
     def frame_row(r, carry):
         normed = dot(w_in_t[...], gbef[r])
@@ -599,10 +592,6 @@
     over_far(lambda peer: q1, rq2.at[far], G_Q2)
     rq2[far] = q1[...]
 
-    arrived(re4.at[pl.ds(0, 3)], G_E4)
-    over_y(lambda peer: re4, re5.at[level], G_E5)
-    re5[level] = re4[...]
-
     @pl.when(summing)
     def _():
         from_near(rt2, G_T2)
@@ -649,8 +638,10 @@
     gone(rq1.at[pl.ds(0, NEAR - 1)], G_Q1)
     gone(rq2.at[pl.ds(0, FAR - 1)], G_Q2)
     gone(re0, G_E0)
-    for ref, g in ((re1, G_E1), (re2, G_E2), (re3, G_E3), (re4, G_E4), (re5, G_E5)):
+    for ref, g in ((re1, G_E1), (re5, G_E5)):
         gone(ref.at[pl.ds(0, 3)], g)
+    for ref, g in ((re2, G_E2), (re3, G_E3)):
+        gone(ref.at[pl.ds(0, FAR - 1)], g)
     gone(re6, G_E6)
 
 
@@ -759,13 +750,12 @@
     vm(512, LANES),
     vm(4, 128, LANES),
     vm(128, LANES, dtype=F32),
-    vm(4, 32, LANES, dtype=F32),
-    vm(32, LANES, dtype=F32),
-    vm(4, 32, LANES, dtype=F32),
-    vm(32, LANES),
-    vm(4, 32, LANES),
-    vm(4, 4, 32, LANES),
-    vm(4, 4, 32, LANES),
+    vm(FAR, 8, LANES, dtype=F32),
+    vm(8, LANES, dtype=F32),
+    vm(FAR, 8, LANES, dtype=F32),
+    vm(128, LANES),
+    vm(4, 128, LANES),
+    vm(4, 128, LANES),
     vm(6 * CH, LANES),
     vm(FAR, 32, LANES),
     vm(32, LANES),

time: 57 us -> 56.8 us (level)
  no operation moved by 1% of the time
where the time goes in v19:
time: 56.8 us; the launch traced here: 56.7 us
  Pallas kernels  56 us (99%)
  between operations  0.64 us (1%)
    pallas_call x1, Pallas kernels, body(): pl.pallas_call(kernel, out_shape=(shape((2, ROWS * CH, LANES), F32), shap...  53.8 us
    pallas_call x1, Pallas kernels, body(): pl.pallas_call(finish, out_shape=(shape((CH, ROWS, COLS), BF), shape((CH,...  2.26 us

profile of v19, /device:TPU:1, one launch (start us, length us, event | category | flops | bytes accessed | tf_op | source)
XLA Modules:
  0.0 56.7 jit_solution(16784354924569128140)
XLA Ops:
  0.6 53.8 %shard_map.126 = (f32[2,1024,128]{2,1,0:T(8,128)S(1)}, f32[2,1024,128]{2,1,0:T(8,128)S(1)}, bf16[1024,128]{1,0:T(8,128)(2,1)S(1)}, bf16[12,32,128]{2,1,0:T(8,128)(2,1)S(1)}, f32[16,128]{1,0:T(8,128)S(1)}) custom-call(bf16[64,16,256]{2,1,0:T(8,128)(2,1)} %frames_hbm.1, bf16[64,128]{1,0:T(8,128)(2,1)} %bitcast.4, bf16[256,256]{1,0:T(8,128)(2,1)} %grid_mix_hbm.1, ...), custom_call_target="tpu_custom_call" | custom-call | tf_op jit(solution)/shard_map/pallas_call | solution.py:779
  54.4 2.3 %shard_map.127 = (bf16[64,16,256]{2,1,0:T(8,128)(2,1)}, bf16[64,16,256]{2,1,0:T(8,128)(2,1)}, f32[64,128]{1,0:T(8,128)}, f32[256,256]{1,0:T(8,128)}, f32[256,256...) custom-call(f32[2,1024,128]{2,1,0:T(8,128)S(1)} %get-tuple-element.19.rest, ...), custom_call_target="tpu_custom_call" | custom-call | tf_op jit(solution)/shard_map/pallas_call | solution.py:795

commit v20 on v19

--- a/solution.py
+++ b/solution.py
@@ -523,7 +523,7 @@
         total, carry = conv_step(conv_k, v3, r, carry)
         total = total + v3[r + 1, CH : 2 * CH].astype(F32)
         for t in range(2):
-            rest_out[t, pl.ds(r * CH, CH), :] = total[:, half(t)]
+            rest_out[t, pl.ds(r, CH, stride=ROWS), :] = total[:, half(t)]
         return carry
 
     carry = loop(ROWS // 2, out_row, conv_start(conv_k, v3), unroll=8)
@@ -579,7 +579,7 @@
         mean_proj = jnp.mean(normed * u, axis=0, keepdims=True)
         source = gj[r].astype(F32) + inv[r, 0:1] * (normed - mean_grad - u * mean_proj)
         for t in range(2):
-            gframe_out[t, pl.ds(r * CH, CH), :] = source[:, half(t)]
+            gframe_out[t, pl.ds(r, CH, stride=ROWS), :] = source[:, half(t)]
         return carry
 
     loop(ROWS, frame_row, unroll=16)
@@ -660,12 +660,9 @@
     def turn_out(src, dst, k):
         for first in range(0, CH, CH // 2):
 
-            def channel(c, carry):
-                for t in range(2):
-                    dst[first + c, :, half(t)] = src[t, pl.ds(first + c, ROWS, stride=CH), :].astype(BF)
-                return carry
-
-            loop(CH // 2, channel, unroll=16)
+            part = pl.ds(first * ROWS, CH // 2 * ROWS)
+            for t in range(2):
+                dst[first : first + CH // 2, :, half(t)] = src[t, part, :].astype(BF).reshape(CH // 2, ROWS, LANES)
             leave(k, pl.ds(first, CH // 2))
 
     scale = float(ROWS * NA * COLS * NW) ** (-0.5)

time: 56.8 us -> 56.4 us (level)
    pallas_call x1, Pallas kernels: 2.26 us -> 1.42 us  [body(): pl.pallas_call(finish, out_shape=(shape((CH, ROWS, COLS), BF), shape((CH,...]
where the time goes in v20:
time: 56.4 us; the launch traced here: 56.3 us
  Pallas kernels  55.6 us (99%)
  between operations  0.64 us (1%)
    pallas_call x1, Pallas kernels, body(): pl.pallas_call(kernel, out_shape=(shape((2, ROWS * CH, LANES), F32), shap...  54.2 us
    pallas_call x1, Pallas kernels, body(): pl.pallas_call(finish, out_shape=(shape((CH, ROWS, COLS), BF), shape((CH,...  1.42 us

profile of v20, /device:TPU:1, one launch (start us, length us, event | category | flops | bytes accessed | tf_op | source)
XLA Modules:
  0.0 56.3 jit_solution(1268834946425011676)
XLA Ops:
  0.6 54.2 %shard_map.126 = (f32[2,1024,128]{2,1,0:T(8,128)S(1)}, f32[2,1024,128]{2,1,0:T(8,128)S(1)}, bf16[1024,128]{1,0:T(8,128)(2,1)S(1)}, bf16[12,32,128]{2,1,0:T(8,128)(2,1)S(1)}, f32[16,128]{1,0:T(8,128)S(1)}) custom-call(bf16[64,16,256]{2,1,0:T(8,128)(2,1)} %frames_hbm.1, bf16[64,128]{1,0:T(8,128)(2,1)} %bitcast.4, bf16[256,256]{1,0:T(8,128)(2,1)} %grid_mix_hbm.1, ...), custom_call_target="tpu_custom_call" | custom-call | tf_op jit(solution)/shard_map/pallas_call | solution.py:776
  54.8 1.4 %shard_map.127 = (bf16[64,16,256]{2,1,0:T(8,128)(2,1)}, bf16[64,16,256]{2,1,0:T(8,128)(2,1)}, f32[64,128]{1,0:T(8,128)}, f32[256,256]{1,0:T(8,128)}, f32[256,256...) custom-call(f32[2,1024,128]{2,1,0:T(8,128)S(1)} %get-tuple-element.19.rest, ...), custom_call_target="tpu_custom_call" | custom-call | tf_op jit(solution)/shard_map/pallas_call | solution.py:792

commit v21 on v20

--- a/solution.py
+++ b/solution.py
@@ -432,7 +432,7 @@
         gbef[r, HC:CH] = jnp.zeros((HC, COLS), BF)
         return carry
 
-    loop(ROWS, block_before_row, unroll=8)
+    loop(ROWS, block_before_row, unroll=16)
     for k in (0, 1, ROWS + 2, ROWS + 3):
         jp[k] = jnp.zeros((CH, COLS), BF)
 
@@ -545,7 +545,7 @@
             gbef[r, HC:CH, half(t)] = (dgelu[r, HC:CH, half(t)] * grid_back[t]).astype(BF)
         return carry
 
-    loop(ROWS, value_before_row, unroll=8)
+    loop(ROWS, value_before_row, unroll=16)
     p_value = dot_nt(pixels(gbef, slice(HC, CH)), pixels(nb))
     sq[...] = jnp.concatenate([p_value[0:16], p_value[16:]], axis=1).astype(BF)
     over_near(lambda peer: sq, rq1.at[near], G_Q1)
@@ -584,13 +584,7 @@
 
     loop(ROWS, frame_row, unroll=16)
 
-    from_near(rq1, G_Q1)
-    total = rq1[0].astype(F32)
-    for k in range(1, NEAR):
-        total = total + rq1[k].astype(F32)
-    q1[...] = total.astype(BF)
-    over_far(lambda peer: q1, rq2.at[far], G_Q2)
-    rq2[far] = q1[...]
+    carry = loop(ROWS // 4, lambda r, carry: out_row(r + ROWS // 2, carry), carry, unroll=4)
 
     @pl.when(summing)
     def _():
@@ -602,7 +596,15 @@
         over_far(lambda peer: t2, rt3.at[far], G_T3)
         rt3[far] = t2[...]
 
-    loop(ROWS // 2, lambda r, carry: out_row(r + ROWS // 2, carry), carry, unroll=8)
+    from_near(rq1, G_Q1)
+    total = rq1[0].astype(F32)
+    for k in range(1, NEAR):
+        total = total + rq1[k].astype(F32)
+    q1[...] = total.astype(BF)
+    over_far(lambda peer: q1, rq2.at[far], G_Q2)
+    rq2[far] = q1[...]
+
+    loop(ROWS // 4, lambda r, carry: out_row(r + 3 * ROWS // 4, carry), carry, unroll=4)
 
     from_far(rq2, G_Q2)
     total = rq2[0].astype(F32)

time: 56.4 us -> 57.3 us (1.016)
  Pallas kernels: 55.6 us -> 56.5 us
    pallas_call x1, Pallas kernels: 54.2 us -> 55.1 us  [body(): pl.pallas_call(kernel, out_shape=(shape((2, ROWS * CH, LANES), F32), shap...]
where the time goes in v21:
time: 57.3 us; the launch traced here: 57.1 us
  Pallas kernels  56.5 us (99%)
  between operations  0.64 us (1%)
    pallas_call x1, Pallas kernels, body(): pl.pallas_call(kernel, out_shape=(shape((2, ROWS * CH, LANES), F32), shap...  55.1 us
    pallas_call x1, Pallas kernels, body(): pl.pallas_call(finish, out_shape=(shape((CH, ROWS, COLS), BF), shape((CH,...  1.42 us

profile of v21, /device:TPU:1, one launch (start us, length us, event | category | flops | bytes accessed | tf_op | source)
XLA Modules:
  0.0 57.1 jit_solution(6293061627038892049)
XLA Ops:
  0.6 55.1 %shard_map.126 = (f32[2,1024,128]{2,1,0:T(8,128)S(1)}, f32[2,1024,128]{2,1,0:T(8,128)S(1)}, bf16[1024,128]{1,0:T(8,128)(2,1)S(1)}, bf16[12,32,128]{2,1,0:T(8,128)(2,1)S(1)}, f32[16,128]{1,0:T(8,128)S(1)}) custom-call(bf16[64,16,256]{2,1,0:T(8,128)(2,1)} %frames_hbm.1, bf16[64,128]{1,0:T(8,128)(2,1)} %bitcast.4, bf16[256,256]{1,0:T(8,128)(2,1)} %grid_mix_hbm.1, ...), custom_call_target="tpu_custom_call" | custom-call | tf_op jit(solution)/shard_map/pallas_call | solution.py:778
  55.7 1.4 %shard_map.127 = (bf16[64,16,256]{2,1,0:T(8,128)(2,1)}, bf16[64,16,256]{2,1,0:T(8,128)(2,1)}, f32[64,128]{1,0:T(8,128)}, f32[256,256]{1,0:T(8,128)}, f32[256,256...) custom-call(f32[2,1024,128]{2,1,0:T(8,128)S(1)} %get-tuple-element.19.rest, ...), custom_call_target="tpu_custom_call" | custom-call | tf_op jit(solution)/shard_map/pallas_call | solution.py:794
